TPU v7x, 512 devices: a whole 4x8x8 slice. The times are simulated.
512 devices in a mesh: dp: 16 (over z, core), tm: 32 (over y, x).
Axes of the slice: x: 4, y: 8, z: 8, core: 2. Of those that a mesh axis runs over, the one named last changes fastest.
Arguments:
- frames_in: bfloat16 [16, 96, 32, 8, 320], P('dp', 'tm'), may hold values from -6 to 6
- cotangent: bfloat16 [16, 96, 32, 8, 320], P('dp', 'tm'), may hold values from -6 to 6
- counts: int32 [16, 32], P('dp'), may hold values from 1 to 3, 64 in all within a row
- norm_gain: float32 [320], replicated, may hold values from 0.5 to 1.5
- norm_shift: float32 [320], replicated, may hold values from -3 to 3
- spatial_weight: bfloat16 [2880, 320], replicated, may hold values from -0.109375 to 0.109375
- temporal_weight: bfloat16 [960, 320], replicated, may hold values from -0.1875 to 0.1875
Outputs:
- input_grad: bfloat16 [16, 96, 32, 8, 320], P('dp', 'tm')
- temporal_grad: float32 [960, 320], replicated
Inputs may be any that keep to these rules, and one draw needn't show every extreme that they name: `counts`: each row sums to 64; in every row some index of tm holds exactly 3 frames.
All inputs are finite; a program needn't handle non-finite values.
Results may differ from a plain program's by a relative error of at most 0.006.
Values may be sent and summed in bfloat16 or wider, within the bound.
No kernel may reach another device: no remote copies, remote signals or barrier semaphores. Data moves between devices by JAX's collectives and lax.ppermute only.
A program may use at most 64 MiB of HBM per device.

v0:
```python
import math

import jax
import jax.numpy as jnp
from jax import lax
from jax.sharding import PartitionSpec as P

GROUPS = 32


def norm_act(values, gain, shift, groups):
    nframes, height, width, channels = values.shape
    per_group = channels // groups
    entries = height * width * per_group

    def group_mean(totals):
        summed = totals.reshape(nframes, groups, per_group).sum(axis=2) / entries
        return jnp.repeat(summed, per_group, axis=1).reshape(nframes, 1, 1, channels)

    centre = group_mean(values.sum(axis=(1, 2)))
    centred = values - centre
    spread = group_mean((centred * centred).sum(axis=(1, 2)))
    normed = centred * lax.rsqrt(spread + 1e-05) * gain + shift
    return jax.nn.silu(normed)


def patches(field):
    height, width = (field.shape[1], field.shape[2])
    padded = jnp.pad(field, ((0, 0), (1, 1), (1, 1), (0, 0)))
    pieces = [
        padded[:, row_off : row_off + height, col_off : col_off + width, :]
        for row_off in range(3)
        for col_off in range(3)
    ]
    return jnp.concatenate(pieces, axis=3)


def spatial_conv(field, weight):
    stacked = patches(field)
    leading = stacked.shape[:3]
    product = jnp.dot(
        stacked.reshape(-1, stacked.shape[3]), weight, preferred_element_type=jnp.float32
    )
    return product.reshape(leading + (weight.shape[1],))


def spatial_conv_t(field, weight):
    channels = weight.shape[1]
    flipped = (
        weight.reshape(9, -1, channels)[::-1].transpose(0, 2, 1).reshape(-1, weight.shape[0] // 9)
    )
    return spatial_conv(field, flipped)


def silu_grad(values):
    sigma = jax.nn.sigmoid(values)
    return sigma * (1.0 + values * (1.0 - sigma))


def temporal_core(y_ext, g_ext, weight):
    nframes = y_ext.shape[0] - 2
    channels = weight.shape[1]
    units = jax.nn.silu(y_ext.astype(jnp.float32)).astype(jnp.bfloat16)
    g_middle = g_ext[1:-1]
    g_mid = g_middle.reshape(-1, channels)
    grads = []
    back_sum = jnp.zeros((g_mid.shape[0], channels), jnp.float32)
    for tap_k in range(3):
        taken = units[tap_k : tap_k + nframes].reshape(-1, channels)
        grads.append(
            lax.dot_general(
                taken, g_mid, (((0,), (0,)), ((), ())), preferred_element_type=jnp.float32
            )
        )
        tap_weight = weight[tap_k * channels : (tap_k + 1) * channels]
        source = g_ext[2 - tap_k : 2 - tap_k + nframes].reshape(-1, channels)
        back_sum = back_sum + lax.dot_general(
            source, tap_weight, (((1,), (1,)), ((), ())), preferred_element_type=jnp.float32
        )
    middle = y_ext[1:-1]
    back_t = (silu_grad(middle.astype(jnp.float32)) * back_sum.reshape(middle.shape)).astype(
        jnp.bfloat16
    )
    return (back_t, jnp.concatenate(grads, axis=0))


def frame_slots(counts_row, nframes, cap):
    ndevices = counts_row.shape[0]
    ends = jnp.cumsum(counts_row)
    starts = ends - counts_row
    frame_ids = jnp.arange(nframes, dtype=jnp.int32)
    owner = jnp.sum((ends[None, :] <= frame_ids[:, None]).astype(jnp.int32), axis=1)
    device_ids = jnp.arange(ndevices, dtype=jnp.int32)
    first = jnp.sum(jnp.where(device_ids[None, :] == owner[:, None], starts[None, :], 0), axis=1)
    return owner * cap + frame_ids - first


def slot_frames(counts_row, cap):
    ndevices = counts_row.shape[0]
    ends = jnp.cumsum(counts_row)
    starts = ends - counts_row
    slot_ids = jnp.arange(ndevices * cap, dtype=jnp.int32)
    device = slot_ids // cap
    inner = slot_ids % cap
    device_ids = jnp.arange(ndevices, dtype=jnp.int32)
    onehot = device[:, None] == device_ids[None, :]
    held = jnp.sum(jnp.where(onehot, counts_row[None, :], 0), axis=1)
    first = jnp.sum(jnp.where(onehot, starts[None, :], 0), axis=1)
    live = inner < held
    return (jnp.where(live, first + inner, 0), live)


def shards(frames_in, cotangent, counts, norm_gain, norm_shift, spatial_weight, temporal_weight):
    inputs = frames_in[0]
    cotan = cotangent[0]
    counts_row = counts[0]
    cap = inputs.shape[0]
    tm_size = lax.axis_size("tm")
    own_count = jnp.sum(
        jnp.where(jnp.arange(tm_size, dtype=jnp.int32) == lax.axis_index("tm"), counts_row, 0)
    )
    live_slots = (jnp.arange(cap, dtype=jnp.int32) < own_count)[:, None, None, None]

    def activate(values):
        return norm_act(values, norm_gain, norm_shift, GROUPS)

    inputs_f = inputs.astype(jnp.float32)
    act_f, act_back = jax.vjp(activate, inputs_f)
    acts = act_f.astype(jnp.bfloat16)
    mixed = spatial_conv(acts, spatial_weight)
    y_out = (inputs_f + mixed).astype(jnp.bfloat16)
    y_rows, g_rows = (
        lax.all_to_all(y_out, "tm", split_axis=1, concat_axis=0, tiled=True),
        lax.all_to_all(cotan, "tm", split_axis=1, concat_axis=0, tiled=True),
    )
    pick = frame_slots(counts_row, 2 * tm_size, cap)
    pad_spec = ((1, 1), (0, 0), (0, 0), (0, 0))
    y_ext = jnp.pad(jnp.take(y_rows, pick, axis=0), pad_spec)
    g_ext = jnp.pad(jnp.take(g_rows, pick, axis=0), pad_spec)
    back_rows, grad_part = temporal_core(y_ext, g_ext, temporal_weight)
    back_idx, live = slot_frames(counts_row, cap)
    back_slots = jnp.where(
        live[:, None, None, None],
        jnp.take(back_rows, back_idx, axis=0),
        jnp.zeros((), jnp.bfloat16),
    )
    back_t = lax.all_to_all(back_slots, "tm", split_axis=0, concat_axis=1, tiled=True)
    d_out = (cotan.astype(jnp.float32) + back_t.astype(jnp.float32)).astype(jnp.bfloat16)
    d_act = spatial_conv_t(d_out, spatial_weight)
    d_in = d_out.astype(jnp.float32) + act_back(d_act)[0]
    d_in = jnp.where(live_slots, d_in, 0.0).astype(jnp.bfloat16)
    height, width = (inputs.shape[1], inputs.shape[2])
    scale = 1.0 / math.sqrt(lax.axis_size("dp") * 2 * tm_size * height * width)
    summed = lax.psum(grad_part, ("dp", "tm"))
    return (d_in[None], summed * scale)


def solution(mesh):
    return jax.shard_map(
        shards,
        mesh=mesh,
        in_specs=(
            P("dp", "tm", None, None, None),
            P("dp", "tm", None, None, None),
            P("dp", None),
            P(),
            P(),
            P(),
            P(),
        ),
        out_specs=(P("dp", "tm", None, None, None), P()),
        check_vma=False,
    )
```

profile of v0, /device:TPU:1, one launch (start us, length us, event | category | flops | bytes accessed | tf_op | source)
XLA Modules:
  0.0 392.2 jit_solution(6571887825265822804)
XLA Ops:
  7.2 2.0 copy.45
  9.2 10.7 %all-to-all-start.1 = ((bf16[3,32,8,320]{3,2,0,1:T(8,128)(2,1)}), bf16[3,32,8,320]{3,2,0,1:T(8,128)(2,1)}, u32[]{:S(2)}, u32[]{:S(2)}) async-start(bf16[3,32,8,320]{3,2,0,1:T(8,128)(2,1)} %copy.45), calls=%async_computation.1 | async-start | bytes 1179648 | tf_op jit(solution)/shard_map/all_to_all | solution.py:134
  20.0 0.1 copy.42
  20.1 0.1 reduce.1
  20.2 0.5 fusion.60
  20.7 0.6 convert_reduce_fusion.1
  21.3 0.1 convert_reduce_fusion
  21.4 0.1 reshape.213
  21.6 0.1 reduce_sum.129
  21.7 0.1 broadcast_in_dim.124
  21.7 0.1 sub.35
  21.9 0.2 fusion.13
  22.1 0.1 reshape.214
  22.2 0.1 reduce_sum.131
  22.3 0.6 divide_multiply_fusion
  22.9 0.1 rsqrt.16
  23.1 0.4 fusion.22
  23.5 1.9 pad_slice_fusion.8
  25.4 0.7 select_reduce_fusion
  26.1 8.0 %concatenate.9 = bf16[3,32,8,2880]{3,2,1,0:T(8,128)(2,1)} concatenate(bf16[3,32,8,320]{3,2,1,0:T(8,128)(2,1)} %get-tuple-element.24, bf16[3,32,8,320]{3,2,1,0:T(8,128)(2,1)S(1)} %get-tuple-element.18, bf16[3,32,8,320]{3,2,1,0:T(8,128)(2,1)S(1)} %get-tuple-element.19, bf16[3,32,8,320]{3,2,1,0:T(8,128)(2,1)S(1)} %get-tuple-element.20, bf16[3,32,8,320]{3,2,1,0:T(8,128)(2,1)S(1)} %fusion.22, ...), dimensions={3} | concatenate | bytes 8847360 | tf_op jit(solution)/shard_map/concatenate | solution.py:35
  34.1 5.4 %fusion.10 = bf16[3,32,8,320]{3,2,1,0:T(8,128)(2,1)S(1)} fusion(bf16[3,32,8,2880]{3,2,1,0:T(8,128)(2,1)} %concatenate.9, bf16[2880,320]{0,1:T(8,128)(2,1)} %param.14, bf16[1,3,32,8,320]{4,3,2,1,0:T(8,128)(2,1)S(1)} %copy-done), kind=kOutput, calls=%fused_computation.32 | convolution fusion | flops 1416314880 | bytes 7249920 | tf_op jit(solution)/shard_map/dot_general | solution.py:41
  39.6 0.9 copy.43
  40.5 0.1 select_reduce_fusion.2
  40.6 9.3 %all-to-all-start = ((bf16[3,32,8,320]{3,2,0,1:T(8,128)(2,1)}), bf16[3,32,8,320]{3,2,0,1:T(8,128)(2,1)S(1)}, u32[]{:S(2)}, u32[]{:S(2)}) async-start(bf16[3,32,8,320]{3,2,0,1:T(8,128)(2,1)} %copy.43), calls=%async_computation | async-start | bytes 1179648 | tf_op jit(solution)/shard_map/all_to_all | solution.py:133
  49.9 1.7 gather_fusion.2
  51.7 0.1 bitcast_select_fusion.1
  51.8 0.4 fusion.45
  52.2 0.5 convolution_add_fusion.1
  52.7 1.3 convolution_add_fusion
  54.1 0.3 copy.46
  54.3 0.1 fusion.68
  54.5 11.9 %all-to-all-done = bf16[3,32,8,320]{3,2,0,1:T(8,128)(2,1)S(1)} async-done(((bf16[3,32,8,320]{3,2,0,1:T(8,128)(2,1)}), bf16[3,32,8,320]{3,2,0,1:T(8,128)(2,1)S(1)}, u32[]{:S(2)}, u32[]{:S(2)}) %all-to-all-start) | async-done | bytes 491552 | tf_op jit(solution)/shard_map/all_to_all | solution.py:133
  66.4 0.7 gather_fusion.1
  67.1 0.5 fusion.49
  67.5 0.3 fusion.31
  67.8 0.4 convolution_bitcast_fusion
  68.2 1.2 convolution_bitcast_fusion.1
  69.4 0.4 convolution_bitcast_fusion.2
  69.8 0.2 copy.48
  70.0 0.7 gather_fusion
  70.7 1.1 fusion.41
  71.8 6.5 %all-to-all-start.2 = ((bf16[96,1,8,320]{3,2,1,0:T(8,128)(2,1)}), bf16[96,1,8,320]{3,2,1,0:T(8,128)(2,1)S(1)}, u32[]{:S(2)}, u32[]{:S(2)}) async-start(bf16[96,1,8,320]{3,2,1,0:T(8,128)(2,1)} %fusion.41), calls=%async_computation.2 | async-start | bytes 1179648 | tf_op jit(solution)/shard_map/all_to_all | solution.py:147
  78.3 0.2 all-reduce.6.cloned.1.call-start
  78.5 1.3 pad_maximum_fusion
  79.9 3.3 copy.52
  83.2 1.6 reverse_bitcast_fusion
  84.8 4.2 %copy.53 = bf16[9,320,320]{2,1,0:T(8,128)(2,1)} copy(bf16[9,320,320]{1,2,0:T(8,128)(2,1)} %reverse_bitcast_fusion) | data formatting | bytes 3686400 | tf_op jit(solution)/shard_map/transpose | solution.py:50
  89.0 0.6 fusion.59
  89.7 1.2 iota_compare_fusion.3
  90.9 273.9 %all-reduce.6.cloned.1.call-done = f32[960,320]{0,1:T(8,128)} async-done(((f32[960,320]{0,1:T(8,128)}), f32[960,320]{0,1:T(8,128)}) %all-reduce.6.cloned.1.call-update) | async-done | bytes 1228816 | tf_op jit(solution)/shard_map/psum | solution.py:154
  364.8 2.5 broadcast_multiply_fusion
  367.3 0.1 fusion.27
  367.5 1.9 pad_slice_fusion
  369.4 8.0 %concatenate.10 = bf16[3,32,8,2880]{3,2,1,0:T(8,128)(2,1)} concatenate(bf16[3,32,8,320]{3,2,1,0:T(8,128)(2,1)} %get-tuple-element.16, bf16[3,32,8,320]{3,2,1,0:T(8,128)(2,1)S(1)} %get-tuple-element.10, bf16[3,32,8,320]{3,2,1,0:T(8,128)(2,1)S(1)} %get-tuple-element.11, bf16[3,32,8,320]{3,2,1,0:T(8,128)(2,1)S(1)} %get-tuple-element.12, bf16[3,32,8,320]{3,2,1,0:T(8,128)(2,1)S(1)} %fusion.27, ...), dimensions={3} | concatenate | bytes 8847360 | tf_op jit(solution)/shard_map/concatenate | solution.py:35
  377.4 5.5 %fusion.26 = (f32[3,320]{1,0:T(4,128)S(1)}, f32[3,32,8,320]{3,2,1,0:T(8,128)S(1)}) fusion(bf16[1,3,32,8,320]{4,3,2,1,0:T(8,128)(2,1)S(1)} %copy-done, f32[3,320]{1,0:T(4,128)S(1)} %sub.35, f32[320]{0:T(512)} %param.13, f32[320]{0:T(512)} %param.12, f32[3,320]{1,0:T(4,128)S(1)} %rsqrt.16, bf16[3,32,8,2880]{3,2,1,0:T(8,128)(2,1)} %concatenate.10, ...), kind=kOutput, calls=%fused_computation.52 | convolution fusion | flops 1419754496 | bytes 7755520 | tf_op jit(solution)/shard_map/dot_general | solution.py:41
  382.9 0.1 reduce_sum.137
  383.0 0.2 multiply_reduce_fusion
  383.2 0.1 reshape.221
  383.4 0.3 fusion.42
  383.7 0.1 reduce_sum.140
  383.8 0.1 reduce_sum.141
  383.9 0.1 broadcast_in_dim.133
  384.0 0.1 reshape.222
  384.1 1.2 fusion.39
  (45 shorter events, 0.4 us)
Async XLA Ops:
  7.2 12.8 %copy-start.7 = (s32[1,32]{1,0:T(1,128)S(1)}, s32[1,32]{1,0:T(1,128)}, u32[]{:S(2)}) copy-start(s32[1,32]{1,0:T(1,128)} %param.11) | copy-start | bytes 388
  7.2 14.2 %copy-start = (bf16[1,3,32,8,320]{4,3,2,1,0:T(8,128)(2,1)S(1)}, bf16[1,3,32,8,320]{4,3,2,1,0:T(8,128)(2,1)}, u32[]{:S(2)}) copy-start(bf16[1,3,32,8,320]{4,3,2,1,0:T(8,128)(2,1)} %param.9) | copy-start | bytes 1474564
  9.2 13.9 %copy-start.5 = (f32[320]{0:T(512)S(1)}, f32[320]{0:T(512)}, u32[]{:S(2)}) copy-start(f32[320]{0:T(512)} %param.13) | copy-start | bytes 3844
  9.2 13.9 %copy-start.6 = (f32[320]{0:T(512)S(1)}, f32[320]{0:T(512)}, u32[]{:S(2)}) copy-start(f32[320]{0:T(512)} %param.12) | copy-start | bytes 3844
  9.2 31.4 %all-to-all-start.1 = ((bf16[3,32,8,320]{3,2,0,1:T(8,128)(2,1)}), bf16[3,32,8,320]{3,2,0,1:T(8,128)(2,1)}, u32[]{:S(2)}, u32[]{:S(2)}) async-start(bf16[3,32,8,320]{3,2,0,1:T(8,128)(2,1)} %copy.45), calls=%async_computation.1 | async-start | bytes 1179648 | tf_op jit(solution)/shard_map/all_to_all | solution.py:134
  23.5 1.9 copy-start.10
  23.5 1.9 copy-start.12
  34.1 5.5 %copy-start.13 = (s32[64]{0:T(128)S(1)}, s32[64]{0:T(128)}, u32[]{:S(2)}) copy-start(s32[64]{0:T(128)} %convert_reduce_fusion.1) | copy-start | bytes 772
  34.1 5.5 %copy-start.14 = (s32[64]{0:T(128)S(1)}, s32[64]{0:T(128)}, u32[]{:S(2)}) copy-start(s32[64]{0:T(128)} %select_reduce_fusion) | copy-start | bytes 772
  39.5 0.9 copy-start.8
  39.5 0.9 copy-start.11
  40.6 11.2 %copy-start.2 = (bf16[960,320]{0,1:T(8,128)(2,1)S(1)}, bf16[960,320]{0,1:T(8,128)(2,1)}, u32[]{:S(2)}) copy-start(bf16[960,320]{0,1:T(8,128)(2,1)} %param.15) | copy-start | bytes 1843204
  40.6 25.8 %all-to-all-start = ((bf16[3,32,8,320]{3,2,0,1:T(8,128)(2,1)}), bf16[3,32,8,320]{3,2,0,1:T(8,128)(2,1)S(1)}, u32[]{:S(2)}, u32[]{:S(2)}) async-start(bf16[3,32,8,320]{3,2,0,1:T(8,128)(2,1)} %copy.43), calls=%async_computation | async-start | bytes 1179648 | tf_op jit(solution)/shard_map/all_to_all | solution.py:133
  71.8 6.7 %copy-start.3 = (f32[320,320]{0,1:T(8,128)S(1)}, f32[320,320]{0,1:T(8,128)}, u32[]{:S(2)}) copy-start(f32[320,320]{0,1:T(8,128)} %convolution_bitcast_fusion.1) | copy-start | bytes 1228804
  71.8 295.5 %all-to-all-start.2 = ((bf16[96,1,8,320]{3,2,1,0:T(8,128)(2,1)}), bf16[96,1,8,320]{3,2,1,0:T(8,128)(2,1)S(1)}, u32[]{:S(2)}, u32[]{:S(2)}) async-start(bf16[96,1,8,320]{3,2,1,0:T(8,128)(2,1)} %fusion.41), calls=%async_computation.2 | async-start | bytes 1179648 | tf_op jit(solution)/shard_map/all_to_all | solution.py:147
  78.3 286.5 %all-reduce.6.cloned.1.call-start = ((), (), s32[]{:S(2)}) async-start(), calls=%async_computation.3 | async-start | bytes 2621440 | tf_op jit(solution)/shard_map/psum | solution.py:154
  90.9 276.5 %copy-start.1 = (bf16[1,3,32,8,320]{4,3,2,1,0:T(8,128)(2,1)S(1)}, bf16[1,3,32,8,320]{4,3,2,1,0:T(8,128)(2,1)}, u32[]{:S(2)}) copy-start(bf16[1,3,32,8,320]{4,3,2,1,0:T(8,128)(2,1)} %param.10) | copy-start | bytes 1474564
  377.4 5.6 %copy-start.4 = (f32[3,32]{1,0:T(4,128)S(1)}, f32[3,32]{1,0:T(4,128)}, u32[]{:S(2)}) copy-start(f32[3,32]{1,0:T(4,128)} %get-tuple-element.25) | copy-start | bytes 1156
  382.9 1.2 copy-start.9
Sparse Core Ops, SparseCore 0:
  84.7 280.0 all-reduce.5
where the time goes:
time: 395 us; the launch traced here: 392 us
  waiting for transfers between devices  286 us (72%)
  local copies, waits for them, and re-layouts  36.7 us (9%)
  starting transfers between devices  26.7 us (7%)
  matrix products  15 us (4%)
  between operations  14.4 us (4%)
  other arithmetic  13.4 us (3%)
    psum x1, waiting for transfers between devices, shards(): summed = lax.psum(grad_part, ('dp', 'tm'))  274 us
    concatenate x2, local copies, waits for them, and re-layouts, patches(): return jnp.concatenate(pieces, axis=3)  16 us
    all_to_all x1, waiting for transfers between devices, shards(): lax.all_to_all(y_out, 'tm', split_axis=1, concat_axis=0, tiled=True)  11.9 us
    dot_general x2, matrix products, spatial_conv(): jnp.dot(stacked.reshape(-1, stacked.shape[3]), weight, preferred_element_...  10.9 us
    all_to_all x1, starting transfers between devices, shards(): lax.all_to_all(cotan, 'tm', split_axis=1, concat_axis=0, tiled=True)  10.7 us
    all_to_all x1, starting transfers between devices, shards(): lax.all_to_all(y_out, 'tm', split_axis=1, concat_axis=0, tiled=True)  9.29 us
  transfers between devices with their start and end apart: 4, of which 2 were waited for; matrix products, arithmetic and copies ran while one was open for 10% of the time, Pallas kernels for 0%

commit v1 on v0

v1 whole, which is shorter than its diff:
```python
import math

import jax
import jax.numpy as jnp
from jax import lax
from jax.experimental import pallas as pl
from jax.experimental.pallas import tpu as pltpu
from jax.sharding import Mesh
from jax.sharding import PartitionSpec as P

F32 = jnp.float32
BF16 = jnp.bfloat16
C = 320
GROUPS = 32
PER_GROUP = C // GROUPS
CAP = 3
HH = 32
WW = 8
PIX = HH * WW
ROWS = CAP * PIX
ENTRIES = PIX * PER_GROUP
VMEM = pltpu.VMEM
LANES = 128
HALF = 4 * C
PARAMS = pltpu.CompilerParams(vmem_limit_bytes=48 * 1024 * 1024)


def group_matrix():
    row = lax.broadcasted_iota(jnp.int32, (C, C), 0).astype(F32)
    col = lax.broadcasted_iota(jnp.int32, (C, C), 1).astype(F32)
    inv = 1.0 / PER_GROUP
    return (jnp.floor((row + 0.5) * inv) == jnp.floor((col + 0.5) * inv)).astype(F32)


def group_mean(sums, matrix):
    return (
        jnp.dot(sums, matrix, precision=lax.Precision.HIGHEST, preferred_element_type=F32) / ENTRIES
    )


def frame(s):
    return pl.ds(pl.multiple_of(s * PIX, PIX), PIX)


def sigmoid(values):
    return 0.5 * jnp.tanh(0.5 * values) + 0.5


def shifted(values, step):
    cube = values.reshape(HH, WW, C)
    rolled = jnp.roll(cube, -step, axis=1)
    col = lax.broadcasted_iota(jnp.int32, (HH, WW, C), 1)
    keep = (col < WW - 1) if step > 0 else (col > 0)
    return jnp.where(keep, rolled, 0.0).reshape(PIX, C)


def down(values):
    return jnp.concatenate([jnp.zeros((WW, C), F32), values[:-WW]], axis=0)


def up(values):
    return jnp.concatenate([values[WW:], jnp.zeros((WW, C), F32)], axis=0)


def forward_kernel(n_ref, x_ref, gain_ref, shift_ref, w_ref, y_ref, u_ref, stats_ref, cols, wst, prod):
    for i in range(3):
        wst[i * C : (i + 1) * C, :] = w_ref[:, i * 3 * C : (i + 1) * 3 * C]
    matrix = group_matrix()
    blank = jnp.zeros((8 - CAP, C), F32)

    def per_frame(fn):
        return jnp.concatenate([fn(s) for s in range(CAP)] + [blank], axis=0)

    def load(s):
        return x_ref[s * PIX : (s + 1) * PIX, :].astype(F32)

    mean = group_mean(per_frame(lambda s: jnp.sum(load(s), axis=0, keepdims=True)), matrix)

    def squares(s):
        centred = load(s) - mean[s : s + 1]
        return jnp.sum(centred * centred, axis=0, keepdims=True)

    inv = lax.rsqrt(group_mean(per_frame(squares), matrix) + 1e-05)
    stats_ref[0] = mean
    stats_ref[1] = inv

    def activate(s, carry):
        values = (x_ref[frame(s), :].astype(F32) - stats_ref[0, pl.ds(s, 1), :]) * stats_ref[
            1, pl.ds(s, 1), :
        ] * gain_ref[...] + shift_ref[...]
        act = values * sigmoid(values)
        cols[frame(s), 0:C] = shifted(act, -1).astype(BF16)
        cols[frame(s), C : 2 * C] = act.astype(BF16)
        cols[frame(s), 2 * C : 3 * C] = shifted(act, 1).astype(BF16)
        return carry

    lax.fori_loop(0, CAP, activate, 0)

    def convolve(s, carry):
        prod[...] = lax.dot_general(
            cols[frame(s), :], wst[...], (((1,), (1,)), ((), ())), preferred_element_type=F32
        )
        mixed = down(prod[:, 0:C]) + prod[:, C : 2 * C] + up(prod[:, 2 * C : 3 * C])
        y = (x_ref[frame(s), :].astype(F32) + mixed).astype(BF16)
        y_ref[frame(s), :] = y
        yf = y.astype(F32)
        live = (s < n_ref[0]).astype(F32)
        u_ref[frame(s), :] = (yf * sigmoid(yf) * live).astype(BF16)
        return carry

    lax.fori_loop(0, CAP, convolve, 0)


def extend(n, ext, g_ref, before_ref, after_ref):
    ext[0:PIX, :] = before_ref[...]
    ext[PIX : PIX + ROWS, :] = g_ref[...]
    ext[PIX + ROWS :, :] = after_ref[...]
    ext[frame(n + 1), :] = after_ref[...]


def grad_kernel(n_ref, core_ref, u_ref, g_ref, before_ref, after_ref, keep_ref, send_ref, ext, whole):
    extend(n_ref[0], ext, g_ref, before_ref, after_ref)
    flipped = ext[...].T
    whole[:, 2 * C + 2 * LANES :] = jnp.zeros((C, 8 * LANES - 2 * C - 2 * LANES), F32)
    for k in range(3):
        lo = (2 - k) * PIX
        whole[:, k * C : (k + 1) * C] = jnp.dot(
            flipped[:, lo : lo + ROWS], u_ref[...], preferred_element_type=F32
        )
    core = core_ref[0]
    for j in range(4):
        first = whole[:, j * LANES : (j + 1) * LANES]
        second = whole[:, (j + 4) * LANES : (j + 5) * LANES]
        keep_ref[j * C : (j + 1) * C, :] = jnp.where(core == 0, first, second)
        send_ref[j * C : (j + 1) * C, :] = jnp.where(core == 0, second, first).astype(BF16)


def backward_kernel(
    n_ref, x_ref, y_ref, g_ref, before_ref, after_ref, stats_ref, gain_ref, shift_ref, w_ref, wt_ref,
    out_ref, ext, cols, wst, prod, dys, grads,
):
    extend(n_ref[0], ext, g_ref, before_ref, after_ref)
    for i in range(3):
        for j in range(3):
            tap = 3 * i + j
            wst[j * C : (j + 1) * C, i * C : (i + 1) * C] = w_ref[:, tap * C : (tap + 1) * C]

    def temporal(s, carry):
        back = jnp.zeros((PIX, C), F32)
        for k in range(3):
            back = back + jnp.dot(
                ext[frame(s + 2 - k), :],
                wt_ref[:, k * C : (k + 1) * C],
                preferred_element_type=F32,
            )
        yf = y_ref[frame(s), :].astype(F32)
        sig = sigmoid(yf)
        back = (sig * (1.0 + yf * (1.0 - sig)) * back).astype(BF16)
        dy = (g_ref[frame(s), :].astype(F32) + back.astype(F32)).astype(BF16)
        dys[frame(s), :] = dy
        dyf = dy.astype(F32)
        cols[frame(s), 0:C] = shifted(dyf, 1).astype(BF16)
        cols[frame(s), C : 2 * C] = dy
        cols[frame(s), 2 * C : 3 * C] = shifted(dyf, -1).astype(BF16)
        return carry

    lax.fori_loop(0, CAP, temporal, 0)
    matrix = group_matrix()

    def finish(s, carry):
        prod[...] = jnp.dot(cols[frame(s), :], wst[...], preferred_element_type=F32)
        da = up(prod[:, 0:C]) + prod[:, C : 2 * C] + down(prod[:, 2 * C : 3 * C])
        mean = stats_ref[0, pl.ds(s, 1), :]
        inv = stats_ref[1, pl.ds(s, 1), :]
        normed = (x_ref[frame(s), :].astype(F32) - mean) * inv
        values = normed * gain_ref[...] + shift_ref[...]
        sig = sigmoid(values)
        dn = da * (sig * (1.0 + values * (1.0 - sig))) * gain_ref[...]
        sums = jnp.concatenate(
            [
                jnp.sum(dn, axis=0, keepdims=True),
                jnp.sum(dn * normed, axis=0, keepdims=True),
                jnp.zeros((6, C), F32),
            ],
            axis=0,
        )
        means = group_mean(sums, matrix)
        dx = inv * (dn - means[0:1] - normed * means[1:2])
        total = dys[frame(s), :].astype(F32) + dx
        out_ref[frame(s), :] = jnp.where(s < n_ref[0], total, 0.0).astype(BF16)
        return carry

    lax.fori_loop(0, CAP, finish, 0)


def final_kernel(scale, core_ref, mine_ref, other_ref, out_ref):
    core = core_ref[0]
    for j in range(4):
        mine = mine_ref[j * C : (j + 1) * C, :].astype(F32) * scale
        other = other_ref[j * C : (j + 1) * C, :].astype(F32) * scale
        out_ref[:, j * LANES : (j + 1) * LANES] = jnp.where(core == 0, mine, other)
        width = min(LANES, 3 * C - (j + 4) * LANES)
        upper = jnp.where(core == 0, other, mine)
        out_ref[:, (j + 4) * LANES : (j + 4) * LANES + width] = upper[:, :width]


SMEM_SPEC = pl.BlockSpec(memory_space=pltpu.SMEM)
VMEM_SPEC = pl.BlockSpec(memory_space=pltpu.VMEM)


def call(body, scalars, arrays, outs, scratch, cost):
    return pl.pallas_call(
        body,
        out_shape=outs,
        in_specs=[SMEM_SPEC] * len(scalars) + [VMEM_SPEC] * len(arrays),
        out_specs=[VMEM_SPEC] * len(outs) if isinstance(outs, list) else VMEM_SPEC,
        scratch_shapes=scratch,
        compiler_params=PARAMS,
        cost_estimate=pl.CostEstimate(flops=cost[0], bytes_accessed=cost[1], transcendentals=0),
    )(*scalars, *arrays)


def shards(frames_in, cotangent, counts, norm_gain, norm_shift, spatial_weight, temporal_weight):
    shape = frames_in.shape
    x = frames_in.reshape(ROWS, C)
    g = cotangent.reshape(ROWS, C)
    counts_row = counts[0]
    tm_size = lax.axis_size("tm")
    z_size = lax.axis_size("z")
    own = lax.dynamic_slice(counts_row, (lax.axis_index("tm"),), (1,))
    core = lax.axis_index("c").astype(jnp.int32).reshape(1)
    gain = norm_gain.reshape(1, C)
    shift = norm_shift.reshape(1, C)
    w_t = spatial_weight.T
    wt_t = temporal_weight.T

    last = lax.dynamic_slice(g, ((own[0] - 1) * PIX, 0), (PIX, C))
    before = lax.ppermute(last, "tm", [(t, t + 1) for t in range(tm_size - 1)])
    after = lax.ppermute(g[:PIX], "tm", [(t + 1, t) for t in range(tm_size - 1)])

    y, u, stats = call(
        forward_kernel,
        (own,),
        (x, gain, shift, w_t),
        [
            jax.ShapeDtypeStruct((ROWS, C), BF16),
            jax.ShapeDtypeStruct((ROWS, C), BF16),
            jax.ShapeDtypeStruct((2, 8, C), F32),
        ],
        [VMEM((ROWS, 3 * C), BF16), VMEM((3 * C, 3 * C), BF16), VMEM((PIX, 3 * C), F32)],
        (2 * ROWS * 9 * C * C, 4_000_000),
    )

    keep, send = call(
        grad_kernel,
        (own, core),
        (u, g, before, after),
        [jax.ShapeDtypeStruct((HALF, LANES), F32), jax.ShapeDtypeStruct((HALF, LANES), BF16)],
        [VMEM((5 * PIX, C), BF16), VMEM((C, 8 * LANES), F32)],
        (2 * ROWS * 3 * C * C, 2_500_000),
    )
    pair = [(0, 1), (1, 0)]
    got = lax.ppermute(send, "c", pair)
    part = (keep + got.astype(F32)).astype(BF16).reshape(tm_size, HALF // tm_size, LANES)
    part = lax.all_to_all(part, "tm", 0, 0, tiled=True)
    part = part.astype(F32).sum(axis=0).astype(BF16)
    part = lax.all_to_all(
        jnp.broadcast_to(part, (z_size,) + part.shape), "z", 0, 0, tiled=True
    )
    part = part.astype(F32).sum(axis=0).astype(BF16)
    part = lax.all_to_all(
        jnp.broadcast_to(part, (tm_size,) + part.shape), "tm", 0, 0, tiled=True
    )
    mine = part.reshape(HALF, LANES)
    other = lax.ppermute(mine, "c", pair)

    d_in = call(
        backward_kernel,
        (own,),
        (x, y, g, before, after, stats, gain, shift, w_t, wt_t),
        jax.ShapeDtypeStruct((ROWS, C), BF16),
        [
            VMEM((5 * PIX, C), BF16),
            VMEM((ROWS, 3 * C), BF16),
            VMEM((3 * C, 3 * C), BF16),
            VMEM((PIX, 3 * C), F32),
            VMEM((ROWS, C), BF16),
            VMEM((8, C), F32),
        ],
        (2 * ROWS * 12 * C * C, 5_000_000),
    )

    frames = lax.axis_size("z") * lax.axis_size("c") * 2 * tm_size
    scale = 1.0 / math.sqrt(frames * HH * WW)

    def finish(*refs):
        final_kernel(scale, *refs)

    grad = call(
        finish,
        (core,),
        (mine, other),
        jax.ShapeDtypeStruct((C, 3 * C), F32),
        [],
        (1_000_000, 2_000_000),
    )
    return (d_in.reshape(shape), grad.T)


def solution(mesh):
    devices = mesh.devices
    dp, tm = devices.shape
    split = Mesh(devices.reshape(dp // 2, 2, tm), ("z", "c", "tm"))
    return jax.shard_map(
        shards,
        mesh=split,
        in_specs=(
            P(("z", "c"), "tm", None, None, None),
            P(("z", "c"), "tm", None, None, None),
            P(("z", "c"), None),
            P(),
            P(),
            P(),
            P(),
        ),
        out_specs=(P(("z", "c"), "tm", None, None, None), P()),
        check_vma=False,
    )
```

time: 395 us -> 107 us (0.27)
  waiting for transfers between devices: 286 us -> 1.24 us
  blocking collectives: 0 us -> 51.6 us
  local copies, waits for them, and re-layouts: 36.7 us -> 9.45 us
  Pallas kernels: 0 us -> 16.6 us
  matrix products: 15 us -> 0 us
  between operations: 14.4 us -> 1.45 us
  other arithmetic: 13.4 us -> 4.48 us
  starting transfers between devices: 26.7 us -> 21.1 us
    psum x1 -> x0, waiting for transfers between devices: 274 us -> none  [shards(): summed = lax.psum(grad_part, ('dp', 'tm'))]
    all_to_all x0 -> x3, blocking collectives: none -> 51.6 us  [the longest x1 18.8 us: shards(): part = lax.all_to_all(part, 'tm', 0, 0, tiled=True)]
    all_to_all x3 -> x0, starting transfers between devices: 26.5 us -> none  [the longest x1 10.7 us: shards(): lax.all_to_all(cotan, 'tm', split_axis=1, concat_axis=0, tiled=True)]
    ppermute x0 -> x4, starting transfers between devices: none -> 21.1 us  [the longest x1 8.89 us: shards(): got = lax.ppermute(send, 'c', pair)]
    pallas_call x0 -> x4, Pallas kernels: none -> 16.6 us  [call(): pl.pallas_call(body, out_shape=outs, in_specs=[SMEM_SPEC] * len(scalars)...]
    concatenate x2 -> x0, local copies, waits for them, and re-layouts: 16 us -> none  [patches(): return jnp.concatenate(pieces, axis=3)]
    dot_general x8 -> x0, matrix products: 15 us -> none  [the longest x2 10.9 us: spatial_conv(): jnp.dot(stacked.reshape(-1, stacked.shape[3]), weight, preferred_element_...]
    all_to_all x3 -> x0, waiting for transfers between devices: 11.9 us -> none  [the longest x1 11.9 us: shards(): lax.all_to_all(y_out, 'tm', split_axis=1, concat_axis=0, tiled=True)]
  transfers between devices with their start and end apart: 4 -> 4, of which waited for: 2 -> 1; matrix products, arithmetic and copies ran while one was open for 10% -> 3% of each run, Pallas kernels for 0% -> 13%
where the time goes in v1:
time: 107 us; the launch traced here: 106 us
  blocking collectives  51.6 us (48%)
  starting transfers between devices  21.1 us (20%)
  Pallas kernels  16.6 us (16%)
  local copies, waits for them, and re-layouts  9.45 us (9%)
  other arithmetic  4.48 us (4%)
  between operations  1.45 us (1%)
  waiting for transfers between devices  1.24 us (1%)
    all_to_all x1, blocking collectives, shards(): part = lax.all_to_all(part, 'tm', 0, 0, tiled=True)  18.8 us
    all_to_all x1, blocking collectives, shards(): lax.all_to_all(jnp.broadcast_to(part, (z_size,) + part.shape), 'z', 0, 0,...  17.3 us
    pallas_call x4, Pallas kernels, call(): pl.pallas_call(body, out_shape=outs, in_specs=[SMEM_SPEC] * len(scalars)...  16.6 us
    all_to_all x1, blocking collectives, shards(): lax.all_to_all(jnp.broadcast_to(part, (tm_size,) + part.shape), 'tm', 0,...  15.5 us
    ppermute x1, starting transfers between devices, shards(): got = lax.ppermute(send, 'c', pair)  8.89 us
    ppermute x1, starting transfers between devices, shards(): other = lax.ppermute(mine, 'c', pair)  6.32 us
    unnamed x16, local copies, waits for them, and re-layouts  4.73 us
    ppermute x1, starting transfers between devices, shards(): before = lax.ppermute(last, 'tm', [(t, t + 1) for t in range(tm_size - 1)])  4.58 us
  transfers between devices with their start and end apart: 4, of which 1 were waited for; matrix products, arithmetic and copies ran while one was open for 3% of the time, Pallas kernels for 13%

profile of v1, /device:TPU:1, one launch (start us, length us, event | category | flops | bytes accessed | tf_op | source)
XLA Modules:
  0.0 106.0 jit_solution(8302858625857497582)
XLA Ops:
  0.6 0.9 slice_bitcast_fusion
  1.6 1.3 %collective-permute-start.1 = (bf16[256,320]{1,0:T(8,128)(2,1)S(1)}, bf16[256,320]{1,0:T(8,128)(2,1)S(1)}, u32[]{:S(2)}, u32[]{:S(2)}) collective-permute-start(bf16[256,320]{1,0:T(8,128)(2,1)S(1)} %slice_bitcast_fusion), channel_id=1, source_target_pairs={{1,0},{2,1},{3,2},{4,3},{5,4},{6,5},{7,6},{8,7},{9,8},{10,9},{11,1... | collective-permute-start | bytes 491528 | tf_op jit(solution)/shard_map/ppermute | solution.py:239
  2.9 1.3 %fusion = (s32[1,1]{1,0:T(1,128)}, s32[1,1]{1,0:T(1,128)}) fusion(s32[1,32]{1,0:T(1,128)} %param.9, s32[]{:T(128)S(6)} %select_n.6), kind=kLoop, calls=%fused_computation.4 | loop fusion | flops 1 | bytes 16 | tf_op jit(solution)/shard_map/sub | solution.py:237
  4.8 1.0 constant_dynamic-slice_fusion
  5.8 4.6 %collective-permute-start = (bf16[256,320]{1,0:T(8,128)(2,1)S(1)}, bf16[256,320]{1,0:T(8,128)(2,1)S(1)}, u32[]{:S(2)}, u32[]{:S(2)}) collective-permute-start(bf16[256,320]{1,0:T(8,128)(2,1)S(1)} %constant_dynamic-slice_fusion), channel_id=1, source_target_pairs={{0,1},{1,2},{2,3},{3,4},{4,5},{5,6},{6,7},{7,8},{8,9},{9,10},{10,1... | collective-permute-start | bytes 491528 | tf_op jit(solution)/shard_map/ppermute | solution.py:238
  10.4 0.7 reshape.36.gain_ref
  11.0 0.7 reshape.37.shift_ref
  11.7 0.0 copy-start.1
  11.7 1.5 %copy-done.1 = bf16[2880,320]{0,1:T(8,128)(2,1)S(1)} copy-done((bf16[2880,320]{0,1:T(8,128)(2,1)S(1)}, bf16[2880,320]{0,1:T(8,128)(2,1)}, u32[]{:S(2)}) %copy-start.1) | copy-done | bytes 1843224
  13.2 0.0 copy-start.4
  13.2 1.1 %copy-done.4 = bf16[1,3,32,8,320]{4,3,2,1,0:T(8,128)(2,1)S(1)} copy-done((bf16[1,3,32,8,320]{4,3,2,1,0:T(8,128)(2,1)S(1)}, bf16[1,3,32,8,320]{4,3,2,1,0:T(8,128)(2,1)}, u32[]{:S(2)}) %copy-start.4) | copy-done | bytes 491544
  14.3 0.0 copy-start
  14.3 5.3 %shard_map.86 = (bf16[768,320]{1,0:T(8,128)(2,1)S(1)}, bf16[768,320]{1,0:T(8,128)(2,1)S(1)}, f32[2,8,320]{2,1,0:T(8,128)S(1)}) custom-call(s32[1]{0:T(128)} %bitcast.n_ref, bf16[768,320]{1,0:T(8,128)(2,1)S(1)} %bitcast.21, f32[1,320]{1,0:T(1,128)S(1)} %reshape.36.gain_ref, f32[1,320]{1,0:T(1,128)S(1)} %reshape.37.shift_ref, bf16[320,2880]{1,0:T(8,128)(2,1)S(1)} %bitcast.18), custom_call_target="tpu_custom_call" | custom-call | flops 1415577600 | bytes 4000000 | tf_op jit(solution)/shard_map/pallas_call | solution.py:212
  19.6 0.0 copy-start.6
  19.6 0.0 collective-permute-done.1.after_ref
  19.6 0.0 collective-permute-done.before_ref
  19.6 0.0 copy-done
  19.6 1.7 %shard_map.88 = (f32[1280,128]{1,0:T(8,128)S(1)}, bf16[1280,128]{1,0:T(8,128)(2,1)S(1)}) custom-call(s32[1]{0:T(128)} %bitcast.n_ref, s32[1]{0:T(128)} %bitcast.8.core_ref.refs_0_, bf16[768,320]{1,0:T(8,128)(2,1)S(1)} %get-tuple-element.9.u_ref, bf16[768,320]{1,0:T(8,128)(2,1)S(1)} %bitcast.16, bf16[256,320]{1,0:T(8,128)(2,1)S(1)} %collective-permute-done.before_ref, ...), custom_call_target="tpu_custom_call" | custom-call | flops 471859200 | bytes 2500000 | tf_op jit(solution)/shard_map/pallas_call | solution.py:212
  21.4 0.0 copy-start.2
  21.4 0.0 copy-start.3
  21.4 8.9 %collective-permute-start.2 = (bf16[1280,128]{1,0:T(8,128)(2,1)S(1)}, bf16[1280,128]{1,0:T(8,128)(2,1)S(1)}, u32[]{:S(2)}, u32[]{:S(2)}) collective-permute-start(bf16[1280,128]{1,0:T(8,128)(2,1)S(1)} %get-tuple-element.11), channel_id=1, source_target_pairs={{0,32},{32,0},{1,33},{33,1},{2,34},{34,2},{3,35},{35,3},{4,36},{36... | collective-permute-start | bytes 983048 | tf_op jit(solution)/shard_map/ppermute | solution.py:263
  30.3 1.2 %collective-permute-done.2 = bf16[1280,128]{1,0:T(8,128)(2,1)S(1)} collective-permute-done((bf16[1280,128]{1,0:T(8,128)(2,1)S(1)}, bf16[1280,128]{1,0:T(8,128)(2,1)S(1)}, u32[]{:S(2)}, u32[]{:S(2)}) %collective-permute-start.2) | collective-permute-done | bytes 327712 | tf_op jit(solution)/shard_map/ppermute | solution.py:263
  31.5 0.1 add_convert_fusion
  31.6 0.0 copy-done.6
  31.6 18.8 %all_to_all.15 = bf16[32,40,128]{2,1,0:T(8,128)(2,1)} all-to-all(bf16[32,40,128]{2,1,0:T(8,128)(2,1)S(1)} %bitcast.23), channel_id=1, replica_groups=mesh['z'=8,'c'=2,'tm'=32] {'tm'}, dimensions={0} | all-to-all | bytes 655360 | tf_op jit(solution)/shard_map/all_to_all | solution.py:265
  50.4 1.6 %reduce_sum.24 = bf16[40,128]{1,0:T(8,128)(2,1)} reduce(bf16[32,40,128]{2,1,0:T(8,128)(2,1)} %all_to_all.15, bf16[]{:T(256)} %constant.26.clone.1), dimensions={0}, to_apply=%region_0.0 | reduce | flops 158720 | bytes 337922 | tf_op jit(solution)/shard_map/reduce_sum | solution.py:266
  52.0 0.7 broadcast_in_dim.6
  52.8 17.3 %all_to_all.16 = bf16[8,40,128]{2,1,0:T(8,128)(2,1)} all-to-all(bf16[8,40,128]{2,1,0:T(8,128)(2,1)S(1)} %broadcast_in_dim.6), channel_id=1, replica_groups=mesh['z'=8,'c'=2,'tm'=32] {'z'}, dimensions={0} | all-to-all | bytes 163840 | tf_op jit(solution)/shard_map/all_to_all | solution.py:267
  70.1 1.5 %reduce_sum.25 = bf16[40,128]{1,0:T(8,128)(2,1)} reduce(bf16[8,40,128]{2,1,0:T(8,128)(2,1)} %all_to_all.16, bf16[]{:T(256)} %constant.26.clone.1), dimensions={0}, to_apply=%region_1.0 | reduce | flops 35840 | bytes 92162 | tf_op jit(solution)/shard_map/reduce_sum | solution.py:270
  71.6 0.7 broadcast_in_dim.7
  72.4 15.5 %all_to_all.17 = bf16[32,40,128]{2,1,0:T(8,128)(2,1)S(1)} all-to-all(bf16[32,40,128]{2,1,0:T(8,128)(2,1)S(1)} %broadcast_in_dim.7), channel_id=1, replica_groups=mesh['z'=8,'c'=2,'tm'=32] {'tm'}, dimensions={0} | all-to-all | bytes 655360 | tf_op jit(solution)/shard_map/all_to_all | solution.py:271
  87.8 6.3 %collective-permute-start.3 = (bf16[1280,128]{1,0:T(8,128)(2,1)S(1)}, bf16[1280,128]{1,0:T(8,128)(2,1)S(1)}, u32[]{:S(2)}, u32[]{:S(2)}) collective-permute-start(bf16[1280,128]{1,0:T(8,128)(2,1)S(1)} %bitcast.13), channel_id=1, source_target_pairs={{0,32},{32,0},{1,33},{33,1},{2,34},{34,2},{3,35},{35,3},{4,36},{36... | collective-permute-start | bytes 983048 | tf_op jit(solution)/shard_map/ppermute | solution.py:275
  94.2 0.0 copy-done.2
  94.2 0.0 copy-done.3
  94.2 0.0 copy-start.5
  94.2 1.1 copy-done.5
  95.2 0.0 copy-start.7
  95.2 1.1 %copy-done.7 = bf16[768,320]{1,0:T(8,128)(2,1)S(1)} copy-done((bf16[768,320]{1,0:T(8,128)(2,1)S(1)}, bf16[768,320]{1,0:T(8,128)(2,1)}, u32[]{:S(2)}) %copy-start.7) | copy-done | bytes 491544
  96.3 8.4 %shard_map.87 = bf16[768,320]{1,0:T(8,128)(2,1)} custom-call(s32[1]{0:T(128)} %bitcast.n_ref, bf16[768,320]{1,0:T(8,128)(2,1)S(1)} %bitcast.22, bf16[768,320]{1,0:T(8,128)(2,1)S(1)} %copy-done.7, bf16[768,320]{1,0:T(8,128)(2,1)S(1)} %bitcast.17, bf16[256,320]{1,0:T(8,128)(2,1)S(1)} %collective-permute-done.before_ref, ...), custom_call_target="tpu_custom_call" | custom-call | flops 1887436800 | bytes 5000000 | tf_op jit(solution)/shard_map/pallas_call | solution.py:212
  104.7 0.0 collective-permute-done.3.refs_2_
  104.7 1.3 %shard_map.89 = f32[320,960]{1,0:T(8,128)} custom-call(s32[1]{0:T(128)} %bitcast.8.core_ref.refs_0_, bf16[1280,128]{1,0:T(8,128)(2,1)S(1)} %bitcast.14, bf16[1280,128]{1,0:T(8,128)(2,1)S(1)} %collective-permute-done.3.refs_2_), custom_call_target="tpu_custom_call" | custom-call | flops 1000000 | bytes 2000000 | tf_op jit(solution)/shard_map/pallas_call | solution.py:212
Async XLA Ops:
  1.6 18.0 %collective-permute-start.1 = (bf16[256,320]{1,0:T(8,128)(2,1)S(1)}, bf16[256,320]{1,0:T(8,128)(2,1)S(1)}, u32[]{:S(2)}, u32[]{:S(2)}) collective-permute-start(bf16[256,320]{1,0:T(8,128)(2,1)S(1)} %slice_bitcast_fusion), channel_id=1, source_target_pairs={{1,0},{2,1},{3,2},{4,3},{5,4},{6,5},{7,6},{8,7},{9,8},{10,9},{11,1... | collective-permute-start | bytes 491528 | tf_op jit(solution)/shard_map/ppermute | solution.py:239
  5.8 13.8 %collective-permute-start = (bf16[256,320]{1,0:T(8,128)(2,1)S(1)}, bf16[256,320]{1,0:T(8,128)(2,1)S(1)}, u32[]{:S(2)}, u32[]{:S(2)}) collective-permute-start(bf16[256,320]{1,0:T(8,128)(2,1)S(1)} %constant_dynamic-slice_fusion), channel_id=1, source_target_pairs={{0,1},{1,2},{2,3},{3,4},{4,5},{5,6},{6,7},{7,8},{8,9},{9,10},{10,1... | collective-permute-start | bytes 491528 | tf_op jit(solution)/shard_map/ppermute | solution.py:238
  11.7 1.5 %copy-start.1 = (bf16[2880,320]{0,1:T(8,128)(2,1)S(1)}, bf16[2880,320]{0,1:T(8,128)(2,1)}, u32[]{:S(2)}) copy-start(bf16[2880,320]{0,1:T(8,128)(2,1)} %param.12) | copy-start | bytes 5529604
  13.2 1.1 %copy-start.4 = (bf16[1,3,32,8,320]{4,3,2,1,0:T(8,128)(2,1)S(1)}, bf16[1,3,32,8,320]{4,3,2,1,0:T(8,128)(2,1)}, u32[]{:S(2)}) copy-start(bf16[1,3,32,8,320]{4,3,2,1,0:T(8,128)(2,1)} %param.7) | copy-start | bytes 1474564
  14.3 5.3 %copy-start = (bf16[1,3,32,8,320]{4,3,2,1,0:T(8,128)(2,1)S(1)}, bf16[1,3,32,8,320]{4,3,2,1,0:T(8,128)(2,1)}, u32[]{:S(2)}) copy-start(bf16[1,3,32,8,320]{4,3,2,1,0:T(8,128)(2,1)} %param.8) | copy-start | bytes 1474564
  19.6 12.0 %copy-start.6 = (bf16[768,320]{1,0:T(8,128)(2,1)}, bf16[768,320]{1,0:T(8,128)(2,1)S(1)}, u32[]{:S(2)}) copy-start(bf16[768,320]{1,0:T(8,128)(2,1)S(1)} %get-tuple-element.7.y_ref) | copy-start | bytes 1474564
  21.4 72.8 %copy-start.2 = (bf16[2880,320]{0,1:T(8,128)(2,1)S(1)}, bf16[2880,320]{0,1:T(8,128)(2,1)}, u32[]{:S(2)}) copy-start(bf16[2880,320]{0,1:T(8,128)(2,1)} %param.12) | copy-start | bytes 5529604
  21.4 72.8 %copy-start.3 = (bf16[960,320]{0,1:T(8,128)(2,1)S(1)}, bf16[960,320]{0,1:T(8,128)(2,1)}, u32[]{:S(2)}) copy-start(bf16[960,320]{0,1:T(8,128)(2,1)} %param.13) | copy-start | bytes 1843204
  21.4 10.1 %collective-permute-start.2 = (bf16[1280,128]{1,0:T(8,128)(2,1)S(1)}, bf16[1280,128]{1,0:T(8,128)(2,1)S(1)}, u32[]{:S(2)}, u32[]{:S(2)}) collective-permute-start(bf16[1280,128]{1,0:T(8,128)(2,1)S(1)} %get-tuple-element.11), channel_id=1, source_target_pairs={{0,32},{32,0},{1,33},{33,1},{2,34},{34,2},{3,35},{35,3},{4,36},{36... | collective-permute-start | bytes 983048 | tf_op jit(solution)/shard_map/ppermute | solution.py:263
  87.8 16.9 %collective-permute-start.3 = (bf16[1280,128]{1,0:T(8,128)(2,1)S(1)}, bf16[1280,128]{1,0:T(8,128)(2,1)S(1)}, u32[]{:S(2)}, u32[]{:S(2)}) collective-permute-start(bf16[1280,128]{1,0:T(8,128)(2,1)S(1)} %bitcast.13), channel_id=1, source_target_pairs={{0,32},{32,0},{1,33},{33,1},{2,34},{34,2},{3,35},{35,3},{4,36},{36... | collective-permute-start | bytes 983048 | tf_op jit(solution)/shard_map/ppermute | solution.py:275
  94.2 1.1 %copy-start.5 = (bf16[1,3,32,8,320]{4,3,2,1,0:T(8,128)(2,1)S(1)}, bf16[1,3,32,8,320]{4,3,2,1,0:T(8,128)(2,1)}, u32[]{:S(2)}) copy-start(bf16[1,3,32,8,320]{4,3,2,1,0:T(8,128)(2,1)} %param.7) | copy-start | bytes 1474564
  95.2 1.1 %copy-start.7 = (bf16[768,320]{1,0:T(8,128)(2,1)S(1)}, bf16[768,320]{1,0:T(8,128)(2,1)}, u32[]{:S(2)}) copy-start(bf16[768,320]{1,0:T(8,128)(2,1)} %copy-done.6) | copy-start | bytes 1474564

commit v2 on v1

v2 whole, which is shorter than its diff:
```python
import math

import jax
import jax.numpy as jnp
from jax import lax
from jax.experimental import pallas as pl
from jax.experimental.pallas import tpu as pltpu
from jax.sharding import Mesh
from jax.sharding import PartitionSpec as P

F32 = jnp.float32
BF16 = jnp.bfloat16
C = 320
GROUPS = 32
PER_GROUP = C // GROUPS
CAP = 3
HH = 32
WW = 8
PIX = HH * WW
ROWS = CAP * PIX
ENTRIES = PIX * PER_GROUP
VMEM = pltpu.VMEM
LANES = 128
HALF = 4 * C
PARAMS = pltpu.CompilerParams(vmem_limit_bytes=28 * 1024 * 1024)


def group_matrix():
    row = lax.broadcasted_iota(jnp.int32, (C, C), 0).astype(F32)
    col = lax.broadcasted_iota(jnp.int32, (C, C), 1).astype(F32)
    inv = 1.0 / PER_GROUP
    same = jnp.floor((row + 0.5) * inv) == jnp.floor((col + 0.5) * inv)
    return same.astype(F32).astype(BF16)


def group_mean(sums, matrix):
    high = sums.astype(BF16).astype(F32)
    rest = sums - high
    middle = rest.astype(BF16).astype(F32)
    terms = jnp.concatenate([high, middle, rest - middle, jnp.zeros((8, C), F32)], axis=0)
    added = jnp.dot(terms.astype(BF16), matrix, preferred_element_type=F32)
    return (added[0:8] + added[8:16] + added[16:24]) / ENTRIES


def frame(s):
    return pl.ds(pl.multiple_of(s * PIX, PIX), PIX)


def sigmoid(values):
    return 0.5 * jnp.tanh(0.5 * values) + 0.5


def shifted(values, step):
    cube = values.reshape(HH, WW, C)
    rolled = jnp.roll(cube, -step, axis=1)
    col = lax.broadcasted_iota(jnp.int32, (HH, WW, C), 1)
    keep = (col < WW - 1) if step > 0 else (col > 0)
    return jnp.where(keep, rolled, 0.0).reshape(PIX, C)


def down(values):
    return jnp.concatenate([jnp.zeros((WW, C), F32), values[:-WW]], axis=0)


def up(values):
    return jnp.concatenate([values[WW:], jnp.zeros((WW, C), F32)], axis=0)


def start_all(sems, *pairs):
    copies = [pltpu.make_async_copy(src, dst, sems.at[i]) for i, (src, dst) in enumerate(pairs)]
    for copy in copies:
        copy.start()
    return copies


def edge_kernel(t_ref, counts_hbm, g_hbm, first_ref, last_ref, g_ref, counts, sems):
    for copy in start_all(sems, (counts_hbm, counts), (g_hbm, g_ref)):
        copy.wait()
    n = counts[0, t_ref[0]]
    first_ref[...] = g_ref[0:PIX, :]
    last_ref[...] = g_ref[frame(n - 1), :]


def forward_kernel(
    t_ref, counts_hbm, x_hbm, gain_hbm, shift_hbm, w_hbm, y_ref, u_ref, stats_ref,
    counts, x_ref, gain_ref, shift_ref, w_ref, cols, wst, prod, sems,
):
    copies = start_all(
        sems,
        (x_hbm, x_ref),
        (gain_hbm, gain_ref),
        (shift_hbm, shift_ref),
        (counts_hbm, counts),
        (w_hbm, w_ref),
    )
    matrix = group_matrix()
    blank = jnp.zeros((8 - CAP, C), F32)
    copies[0].wait()

    def per_frame(fn):
        return jnp.concatenate([fn(s) for s in range(CAP)] + [blank], axis=0)

    def load(s):
        return x_ref[s * PIX : (s + 1) * PIX, :].astype(F32)

    mean = group_mean(per_frame(lambda s: jnp.sum(load(s), axis=0, keepdims=True)), matrix)

    def squares(s):
        centred = load(s) - mean[s : s + 1]
        return jnp.sum(centred * centred, axis=0, keepdims=True)

    inv = lax.rsqrt(group_mean(per_frame(squares), matrix) + 1e-05)
    stats_ref[0] = mean
    stats_ref[1] = inv
    for copy in copies[1:4]:
        copy.wait()
    n = counts[0, t_ref[0]]
    gain = gain_ref[...].reshape(1, C)
    shift = shift_ref[...].reshape(1, C)

    def activate(s, carry):
        values = (x_ref[frame(s), :].astype(F32) - stats_ref[0, pl.ds(s, 1), :]) * stats_ref[
            1, pl.ds(s, 1), :
        ] * gain + shift
        act = values * sigmoid(values)
        cols[frame(s), 0:C] = shifted(act, -1).astype(BF16)
        cols[frame(s), C : 2 * C] = act.astype(BF16)
        cols[frame(s), 2 * C : 3 * C] = shifted(act, 1).astype(BF16)
        return carry

    lax.fori_loop(0, CAP, activate, 0)
    copies[4].wait()
    for i in range(3):
        wst[i * C : (i + 1) * C, :] = w_ref[:, i * 3 * C : (i + 1) * 3 * C]
    prod[...] = lax.dot_general(
        cols[...], wst[...], (((1,), (1,)), ((), ())), preferred_element_type=F32
    )

    def add(s, carry):
        rows = frame(s)
        mixed = down(prod[rows, 0:C]) + prod[rows, C : 2 * C] + up(prod[rows, 2 * C : 3 * C])
        y = (x_ref[rows, :].astype(F32) + mixed).astype(BF16)
        y_ref[rows, :] = y
        yf = y.astype(F32)
        live = (s < n).astype(F32)
        u_ref[rows, :] = (yf * sigmoid(yf) * live).astype(BF16)
        return carry

    lax.fori_loop(0, CAP, add, 0)


def grad_kernel(
    t_ref, core_ref, u_ref, g_ref, before_ref, after_ref, counts_hbm, keep_ref, send_ref, ext,
    counts, whole, sems,
):
    (copy,) = start_all(sems, (counts_hbm, counts))
    ext[0:PIX, :] = before_ref[...]
    ext[PIX : PIX + ROWS, :] = g_ref[...]
    ext[PIX + ROWS :, :] = after_ref[...]
    copy.wait()
    n = counts[0, t_ref[0]]
    ext[frame(n + 1), :] = after_ref[...]
    flipped = ext[...].T
    whole[:, 2 * C + 2 * LANES :] = jnp.zeros((C, 8 * LANES - 2 * C - 2 * LANES), F32)
    for k in range(3):
        lo = (2 - k) * PIX
        whole[:, k * C : (k + 1) * C] = jnp.dot(
            flipped[:, lo : lo + ROWS], u_ref[...], preferred_element_type=F32
        )
    core = core_ref[0]
    for j in range(4):
        first = whole[:, j * LANES : (j + 1) * LANES]
        second = whole[:, (j + 4) * LANES : (j + 5) * LANES]
        keep_ref[j * C : (j + 1) * C, :] = jnp.where(core == 0, first, second)
        send_ref[j * C : (j + 1) * C, :] = jnp.where(core == 0, second, first).astype(BF16)


def temporal_kernel(y_ref, ext, wt_hbm, dy_ref, wt_ref, sems):
    (copy,) = start_all(sems, (wt_hbm, wt_ref))
    copy.wait()

    def body(s, carry):
        back = jnp.zeros((PIX, C), F32)
        for k in range(3):
            back = back + jnp.dot(
                ext[frame(s + 2 - k), :],
                wt_ref[:, k * C : (k + 1) * C],
                preferred_element_type=F32,
            )
        yf = y_ref[frame(s), :].astype(F32)
        sig = sigmoid(yf)
        back = (sig * (1.0 + yf * (1.0 - sig)) * back).astype(BF16)
        own = ext[frame(s + 1), :].astype(F32)
        dy_ref[frame(s), :] = (own + back.astype(F32)).astype(BF16)
        return carry

    lax.fori_loop(0, CAP, body, 0)


def spatial_kernel(
    t_ref, dy_ref, stats_ref, counts_hbm, x_hbm, gain_hbm, shift_hbm, w_hbm, out_ref,
    counts, x_ref, gain_ref, shift_ref, w_ref, cols, wst, prod, sems,
):
    copies = start_all(
        sems,
        (w_hbm, w_ref),
        (x_hbm, x_ref),
        (gain_hbm, gain_ref),
        (shift_hbm, shift_ref),
        (counts_hbm, counts),
    )

    def spread(s, carry):
        dy = dy_ref[frame(s), :]
        dyf = dy.astype(F32)
        cols[frame(s), 0:C] = shifted(dyf, 1).astype(BF16)
        cols[frame(s), C : 2 * C] = dy
        cols[frame(s), 2 * C : 3 * C] = shifted(dyf, -1).astype(BF16)
        return carry

    lax.fori_loop(0, CAP, spread, 0)
    copies[0].wait()
    for i in range(3):
        for j in range(3):
            tap = 3 * i + j
            wst[j * C : (j + 1) * C, i * C : (i + 1) * C] = w_ref[:, tap * C : (tap + 1) * C]
    prod[...] = jnp.dot(cols[...], wst[...], preferred_element_type=F32)
    matrix = group_matrix()
    for copy in copies[1:]:
        copy.wait()
    n = counts[0, t_ref[0]]
    gain = gain_ref[...].reshape(1, C)
    shift = shift_ref[...].reshape(1, C)

    def finish(s, carry):
        rows = frame(s)
        da = up(prod[rows, 0:C]) + prod[rows, C : 2 * C] + down(prod[rows, 2 * C : 3 * C])
        mean = stats_ref[0, pl.ds(s, 1), :]
        inv = stats_ref[1, pl.ds(s, 1), :]
        normed = (x_ref[rows, :].astype(F32) - mean) * inv
        values = normed * gain + shift
        sig = sigmoid(values)
        dn = da * (sig * (1.0 + values * (1.0 - sig))) * gain
        sums = jnp.concatenate(
            [
                jnp.sum(dn, axis=0, keepdims=True),
                jnp.sum(dn * normed, axis=0, keepdims=True),
                jnp.zeros((6, C), F32),
            ],
            axis=0,
        )
        means = group_mean(sums, matrix)
        dx = inv * (dn - means[0:1] - normed * means[1:2])
        total = dy_ref[rows, :].astype(F32) + dx
        out_ref[rows, :] = jnp.where(s < n, total, 0.0).astype(BF16)
        return carry

    lax.fori_loop(0, CAP, finish, 0)


def sum_kernel(copies, x_ref, out_ref):
    total = x_ref[0].astype(F32)
    for i in range(1, x_ref.shape[0]):
        total = total + x_ref[i].astype(F32)
    total = total.astype(BF16)
    for i in range(copies):
        out_ref[i] = total


def final_kernel(scale, core_ref, mine_ref, other_ref, out_ref):
    core = core_ref[0]
    for j in range(4):
        mine = mine_ref[j * C : (j + 1) * C, :].astype(F32) * scale
        other = other_ref[j * C : (j + 1) * C, :].astype(F32) * scale
        out_ref[:, j * LANES : (j + 1) * LANES] = jnp.where(core == 0, mine, other)
        width = min(LANES, 3 * C - (j + 4) * LANES)
        upper = jnp.where(core == 0, other, mine)
        out_ref[:, (j + 4) * LANES : (j + 4) * LANES + width] = upper[:, :width]


SMEM_SPEC = pl.BlockSpec(memory_space=pltpu.SMEM)
VMEM_SPEC = pl.BlockSpec(memory_space=pltpu.VMEM)
HBM_SPEC = pl.BlockSpec(memory_space=pltpu.HBM)


def call(body, scalars, arrays, away, outs, scratch, cost):
    away = [pltpu.with_memory_space_constraint(a, pltpu.HBM) for a in away]
    return pl.pallas_call(
        body,
        out_shape=outs,
        in_specs=[SMEM_SPEC] * len(scalars) + [VMEM_SPEC] * len(arrays) + [HBM_SPEC] * len(away),
        out_specs=[VMEM_SPEC] * len(outs) if isinstance(outs, list) else VMEM_SPEC,
        scratch_shapes=scratch,
        compiler_params=PARAMS,
        cost_estimate=pl.CostEstimate(flops=cost[0], bytes_accessed=cost[1], transcendentals=0),
    )(*scalars, *arrays, *away)


def shards(frames_in, cotangent, counts, norm_gain, norm_shift, spatial_weight, temporal_weight):
    shape = frames_in.shape
    x = frames_in.reshape(ROWS, C)
    g = cotangent.reshape(ROWS, C)
    tm_size = lax.axis_size("tm")
    z_size = lax.axis_size("z")
    place = lax.axis_index("tm").astype(jnp.int32).reshape(1)
    core = lax.axis_index("c").astype(jnp.int32).reshape(1)
    w_t = spatial_weight.T
    wt_t = temporal_weight.T
    array = jax.ShapeDtypeStruct
    dma = pltpu.SemaphoreType.DMA

    act = array((ROWS, C), BF16)
    one = array((PIX, C), BF16)
    counts_mem = pltpu.SMEM(counts.shape, jnp.int32)
    vector = VMEM((C,), F32)
    rows_mem = VMEM((ROWS, C), BF16)
    weights = VMEM((C, 9 * C), BF16)
    columns = VMEM((ROWS, 3 * C), BF16)
    stacked = VMEM((3 * C, 3 * C), BF16)
    product = VMEM((ROWS, 3 * C), F32)

    first, last, g_own = call(
        edge_kernel,
        (place,),
        (),
        (counts, g),
        [one, one, act],
        [counts_mem, dma((2,))],
        (0, 600_000),
    )
    before = lax.ppermute(last, "tm", [(t, t + 1) for t in range(tm_size - 1)])
    after = lax.ppermute(first, "tm", [(t + 1, t) for t in range(tm_size - 1)])

    y, u, stats = call(
        forward_kernel,
        (place,),
        (),
        (counts, x, norm_gain, norm_shift, w_t),
        [act, act, array((2, 8, C), F32)],
        [counts_mem, rows_mem, vector, vector, weights, columns, stacked, product, dma((5,))],
        (2 * ROWS * 9 * C * C, 4_000_000),
    )

    keep, send, ext = call(
        grad_kernel,
        (place, core),
        (u, g_own, before, after),
        (counts,),
        [
            array((HALF, LANES), F32),
            array((HALF, LANES), BF16),
            array((5 * PIX, C), BF16),
        ],
        [counts_mem, VMEM((C, 8 * LANES), F32), dma((1,))],
        (2 * ROWS * 3 * C * C, 2_500_000),
    )
    pair = [(0, 1), (1, 0)]

    def total(parts, copies):
        def body(*refs):
            sum_kernel(copies, *refs)

        return call(
            body,
            (),
            (parts,),
            (),
            array((copies,) + parts.shape[1:], BF16),
            [],
            (parts.size, 2 * parts.size),
        )

    got = lax.ppermute(send, "c", pair)
    part = (keep + got.astype(F32)).astype(BF16).reshape(tm_size, HALF // tm_size, LANES)
    dy = call(
        temporal_kernel,
        (),
        (y, ext),
        (wt_t,),
        act,
        [VMEM((C, 3 * C), BF16), dma((1,))],
        (2 * ROWS * 3 * C * C, 2_500_000),
    )
    part = lax.all_to_all(part, "tm", 0, 0, tiled=True)
    part, dy = lax.optimization_barrier((part, dy))
    part = total(part, z_size)
    part = total(lax.all_to_all(part, "z", 0, 0, tiled=True), tm_size)
    mine = lax.all_to_all(part, "tm", 0, 0, tiled=True).reshape(HALF, LANES)

    d_in = call(
        spatial_kernel,
        (place,),
        (dy, stats),
        (counts, x, norm_gain, norm_shift, w_t),
        act,
        [counts_mem, rows_mem, vector, vector, weights, columns, stacked, product, dma((5,))],
        (2 * ROWS * 9 * C * C, 4_000_000),
    )
    mine, d_in = lax.optimization_barrier((mine, d_in))
    other = lax.ppermute(mine, "c", pair)

    frames = z_size * lax.axis_size("c") * 2 * tm_size
    scale = 1.0 / math.sqrt(frames * HH * WW)

    def finish(*refs):
        final_kernel(scale, *refs)

    grad = call(
        finish,
        (core,),
        (mine, other),
        (),
        array((C, 3 * C), F32),
        [],
        (1_000_000, 2_000_000),
    )
    return (d_in.reshape(shape), grad.T)


def solution(mesh):
    devices = mesh.devices
    dp, tm = devices.shape
    split = Mesh(devices.reshape(dp // 2, 2, tm), ("z", "c", "tm"))
    return jax.shard_map(
        shards,
        mesh=split,
        in_specs=(
            P(("z", "c"), "tm", None, None, None),
            P(("z", "c"), "tm", None, None, None),
            P(("z", "c"), None),
            P(),
            P(),
            P(),
            P(),
        ),
        out_specs=(P(("z", "c"), "tm", None, None, None), P()),
        check_vma=False,
    )
```

time: 107 us -> 88.2 us (0.82)
  blocking collectives: 51.6 us -> 17.2 us
  waiting for transfers between devices: 1.24 us -> 16.9 us
  starting transfers between devices: 21.1 us -> 32.7 us
  local copies, waits for them, and re-layouts: 9.45 us -> 0 us
  other arithmetic: 4.48 us -> 0.81 us
  Pallas kernels: 16.6 us -> 19.3 us
    all_to_all x3 -> x1, blocking collectives: 51.6 us -> 17.2 us  [shards(): part = total(lax.all_to_all(part, 'z', 0, 0, tiled=True), tm_size)]
    all_to_all x0 -> x2, waiting for transfers between devices: none -> 14.4 us  [the longest x1 9.6 us: shards(): part = lax.all_to_all(part, 'tm', 0, 0, tiled=True)]
    all_to_all x0 -> x2, starting transfers between devices: none -> 14 us  [the longest x1 9.13 us: shards(): part = lax.all_to_all(part, 'tm', 0, 0, tiled=True)]
    unnamed x16 -> x0, local copies, waits for them, and re-layouts: 4.73 us -> none
    reduce_sum x2 -> x0, other arithmetic: 3.15 us -> none  [shards(): part = part.astype(F32).sum(axis=0).astype(BF16)]
    pallas_call x4 -> x8, Pallas kernels: 16.6 us -> 19.3 us  [call(): pl.pallas_call(body, out_shape=outs, in_specs=[SMEM_SPEC] * len(scalars)...]
    ppermute x1, starting transfers between devices: 8.89 us -> 7.13 us  [shards(): got = lax.ppermute(send, 'c', pair)]
    broadcast_in_dim x2 -> x0, local copies, waits for them, and re-layouts: 1.46 us -> none  [the longest x1 0.74 us: shards(): jnp.broadcast_to(part, (tm_size,) + part.shape)]
  transfers between devices with their start and end apart: 4 -> 6, of which waited for: 1 -> 4; matrix products, arithmetic and copies ran while one was open for 3% -> 0% of each run, Pallas kernels for 13% -> 16%
where the time goes in v2:
time: 88.2 us; the launch traced here: 87.6 us
  starting transfers between devices  32.7 us (37%)
  Pallas kernels  19.3 us (22%)
  blocking collectives  17.2 us (20%)
  waiting for transfers between devices  16.9 us (19%)
    pallas_call x8, Pallas kernels, call(): pl.pallas_call(body, out_shape=outs, in_specs=[SMEM_SPEC] * len(scalars)...  19.3 us
    all_to_all x1, blocking collectives, shards(): part = total(lax.all_to_all(part, 'z', 0, 0, tiled=True), tm_size)  17.2 us
    all_to_all x1, waiting for transfers between devices, shards(): part = lax.all_to_all(part, 'tm', 0, 0, tiled=True)  9.6 us
    all_to_all x1, starting transfers between devices, shards(): part = lax.all_to_all(part, 'tm', 0, 0, tiled=True)  9.13 us
    ppermute x1, starting transfers between devices, shards(): got = lax.ppermute(send, 'c', pair)  7.13 us
    ppermute x1, starting transfers between devices, shards(): other = lax.ppermute(mine, 'c', pair)  6.32 us
    all_to_all x1, starting transfers between devices, shards(): mine = lax.all_to_all(part, 'tm', 0, 0, tiled=True).reshape(HALF, LANES)  4.85 us
    all_to_all x1, waiting for transfers between devices, shards(): mine = lax.all_to_all(part, 'tm', 0, 0, tiled=True).reshape(HALF, LANES)  4.77 us
  transfers between devices with their start and end apart: 6, of which 4 were waited for; matrix products, arithmetic and copies ran while one was open for 0% of the time, Pallas kernels for 16%

profile of v2, /device:TPU:1, one launch (start us, length us, event | category | flops | bytes accessed | tf_op | source)
XLA Modules:
  0.0 87.6 jit_solution(8608554461478777210)
XLA Ops:
  0.6 1.1 %shard_map.87 = (bf16[256,320]{1,0:T(8,128)(2,1)S(1)}, bf16[256,320]{1,0:T(8,128)(2,1)S(1)}, bf16[768,320]{1,0:T(8,128)(2,1)S(1)}) custom-call(s32[1]{0:T(128)} %bitcast.t_ref, s32[1,32]{1,0:T(1,128)} %counts_hbm.7, bf16[768,320]{1,0:T(8,128)(2,1)} %bitcast.14), custom_call_target="tpu_custom_call" | custom-call | bytes 600000 | tf_op jit(solution)/shard_map/pallas_call | solution.py:288
  1.8 4.0 %collective-permute-start = (bf16[256,320]{1,0:T(8,128)(2,1)S(1)}, bf16[256,320]{1,0:T(8,128)(2,1)S(1)}, u32[]{:S(2)}, u32[]{:S(2)}) collective-permute-start(bf16[256,320]{1,0:T(8,128)(2,1)S(1)} %get-tuple-element.17), channel_id=1, source_target_pairs={{0,1},{1,2},{2,3},{3,4},{4,5},{5,6},{6,7},{7,8},{8,9},{9,10},{10,1... | collective-permute-start | bytes 491528 | tf_op jit(solution)/shard_map/ppermute | solution.py:331
  5.7 1.3 %collective-permute-start.1 = (bf16[256,320]{1,0:T(8,128)(2,1)S(1)}, bf16[256,320]{1,0:T(8,128)(2,1)S(1)}, u32[]{:S(2)}, u32[]{:S(2)}) collective-permute-start(bf16[256,320]{1,0:T(8,128)(2,1)S(1)} %get-tuple-element.18), channel_id=1, source_target_pairs={{1,0},{2,1},{3,2},{4,3},{5,4},{6,5},{7,6},{8,7},{9,8},{10,9},{11,1... | collective-permute-start | bytes 491528 | tf_op jit(solution)/shard_map/ppermute | solution.py:332
  7.0 5.2 %shard_map.86 = (bf16[768,320]{1,0:T(8,128)(2,1)S(1)}, bf16[768,320]{1,0:T(8,128)(2,1)S(1)}, f32[2,8,320]{2,1,0:T(8,128)S(1)}) custom-call(s32[1]{0:T(128)} %bitcast.t_ref, s32[1,32]{1,0:T(1,128)} %counts_hbm.7, bf16[768,320]{1,0:T(8,128)(2,1)} %bitcast.17, f32[320]{0:T(512)} %gain_hbm.3, f32[320]{0:T(512)} %shift_hbm.3, bf16[320,2880]{1,0:T(8,128)(2,1)} %bitcast.15), custom_call_target="tpu_custom_call" | custom-call | flops 1415577600 | bytes 4000000 | tf_op jit(solution)/shard_map/pallas_call | solution.py:288
  12.3 0.0 collective-permute-done.before_ref
  12.3 0.0 collective-permute-done.1.after_ref
  12.3 1.7 %shard_map.88 = (f32[1280,128]{1,0:T(8,128)S(1)}, bf16[1280,128]{1,0:T(8,128)(2,1)S(1)}, bf16[1280,320]{1,0:T(8,128)(2,1)S(1)}) custom-call(s32[1]{0:T(128)} %bitcast.t_ref, s32[1]{0:T(128)} %bitcast.1.core_ref.refs_0_, bf16[768,320]{1,0:T(8,128)(2,1)S(1)} %get-tuple-element.15.u_ref, bf16[768,320]{1,0:T(8,128)(2,1)S(1)} %get-tuple-element.16.g_ref, ...), custom_call_target="tpu_custom_call" | custom-call | flops 471859200 | bytes 2500000 | tf_op jit(solution)/shard_map/pallas_call | solution.py:288
  14.0 7.1 %collective-permute-start.2 = (bf16[1280,128]{1,0:T(8,128)(2,1)S(1)}, bf16[1280,128]{1,0:T(8,128)(2,1)S(1)}, u32[]{:S(2)}, u32[]{:S(2)}) collective-permute-start(bf16[1280,128]{1,0:T(8,128)(2,1)S(1)} %get-tuple-element.20), channel_id=1, source_target_pairs={{0,32},{32,0},{1,33},{33,1},{2,34},{34,2},{3,35},{35,3},{4,36},{36... | collective-permute-start | bytes 983048 | tf_op jit(solution)/shard_map/ppermute | solution.py:373
  21.1 1.2 %collective-permute-done.2 = bf16[1280,128]{1,0:T(8,128)(2,1)S(1)} collective-permute-done((bf16[1280,128]{1,0:T(8,128)(2,1)S(1)}, bf16[1280,128]{1,0:T(8,128)(2,1)S(1)}, u32[]{:S(2)}, u32[]{:S(2)}) %collective-permute-start.2) | collective-permute-done | bytes 327712 | tf_op jit(solution)/shard_map/ppermute | solution.py:373
  22.4 0.8 add_convert_fusion
  23.2 9.1 %all-to-all-start = ((bf16[32,40,128]{2,1,0:T(8,128)(2,1)}), bf16[32,40,128]{2,1,0:T(8,128)(2,1)S(1)}, u32[]{:S(2)}, u32[]{:S(2)}) async-start(bf16[32,40,128]{2,1,0:T(8,128)(2,1)} %bitcast.5), calls=%async_computation | async-start | bytes 655360 | tf_op jit(solution)/shard_map/all_to_all | solution.py:384
  32.3 3.1 %shard_map.89.dy_ref = bf16[768,320]{1,0:T(8,128)(2,1)S(1)} custom-call(bf16[768,320]{1,0:T(8,128)(2,1)S(1)} %get-tuple-element.21.y_ref, bf16[1280,320]{1,0:T(8,128)(2,1)S(1)} %get-tuple-element.22.ext, bf16[320,960]{1,0:T(8,128)(2,1)} %bitcast.13), custom_call_target="tpu_custom_call" | custom-call | flops 471859200 | bytes 2500000 | tf_op jit(solution)/shard_map/pallas_call | solution.py:288
  35.5 9.6 %all-to-all-done.refs_0_ = bf16[32,40,128]{2,1,0:T(8,128)(2,1)S(1)} async-done(((bf16[32,40,128]{2,1,0:T(8,128)(2,1)}), bf16[32,40,128]{2,1,0:T(8,128)(2,1)S(1)}, u32[]{:S(2)}, u32[]{:S(2)}) %all-to-all-start) | async-done | bytes 327712 | tf_op jit(solution)/shard_map/all_to_all | solution.py:384
  45.1 0.1 shard_map.90
  45.1 17.2 %all_to_all.15.refs_0_ = bf16[8,40,128]{2,1,0:T(8,128)(2,1)S(1)} all-to-all(bf16[8,40,128]{2,1,0:T(8,128)(2,1)S(1)} %shard_map.90), channel_id=1, replica_groups=mesh['z'=8,'c'=2,'tm'=32] {'z'}, dimensions={0} | all-to-all | bytes 163840 | tf_op jit(solution)/shard_map/all_to_all | solution.py:387
  62.4 0.8 shard_map.91
  63.1 4.9 %all-to-all-start.2 = ((bf16[32,40,128]{2,1,0:T(8,128)(2,1)}), bf16[32,40,128]{2,1,0:T(8,128)(2,1)S(1)}, u32[]{:S(2)}, u32[]{:S(2)}) async-start(bf16[32,40,128]{2,1,0:T(8,128)(2,1)} %shard_map.91), calls=%async_computation.2 | async-start | bytes 655360 | tf_op jit(solution)/shard_map/all_to_all | solution.py:388
  68.0 6.0 %shard_map.92 = bf16[768,320]{1,0:T(8,128)(2,1)} custom-call(s32[1]{0:T(128)} %bitcast.t_ref, bf16[768,320]{1,0:T(8,128)(2,1)S(1)} %shard_map.89.dy_ref, f32[2,8,320]{2,1,0:T(8,128)S(1)} %get-tuple-element.25.stats_ref, s32[1,32]{1,0:T(1,128)} %counts_hbm.7, bf16[768,320]{1,0:T(8,128)(2,1)} %bitcast.18, f32[320]{0:T(512)} %gain_hbm.3, f32[320]{0:T(512)} %shift_hbm.3, ...), custom_call_target="tpu_custom_call" | custom-call | flops 1415577600 | bytes 4000000 | tf_op jit(solution)/shard_map/pallas_call | solution.py:288
  74.0 4.8 %all-to-all-done.2 = bf16[32,40,128]{2,1,0:T(8,128)(2,1)S(1)} async-done(((bf16[32,40,128]{2,1,0:T(8,128)(2,1)}), bf16[32,40,128]{2,1,0:T(8,128)(2,1)S(1)}, u32[]{:S(2)}, u32[]{:S(2)}) %all-to-all-start.2) | async-done | bytes 327712 | tf_op jit(solution)/shard_map/all_to_all | solution.py:388
  78.8 6.3 %collective-permute-start.3 = (bf16[1280,128]{1,0:T(8,128)(2,1)S(1)}, bf16[1280,128]{1,0:T(8,128)(2,1)S(1)}, u32[]{:S(2)}, u32[]{:S(2)}) collective-permute-start(bf16[1280,128]{1,0:T(8,128)(2,1)S(1)} %bitcast.10), channel_id=1, source_target_pairs={{0,32},{32,0},{1,33},{33,1},{2,34},{34,2},{3,35},{35,3},{4,36},{36... | collective-permute-start | bytes 983048 | tf_op jit(solution)/shard_map/ppermute | solution.py:400
  85.2 1.2 %collective-permute-done.3.refs_2_ = bf16[1280,128]{1,0:T(8,128)(2,1)S(1)} collective-permute-done((bf16[1280,128]{1,0:T(8,128)(2,1)S(1)}, bf16[1280,128]{1,0:T(8,128)(2,1)S(1)}, u32[]{:S(2)}, u32[]{:S(2)}) %collective-permute-start.3) | collective-permute-done | bytes 327712 | tf_op jit(solution)/shard_map/ppermute | solution.py:400
  86.4 1.3 %shard_map.93 = f32[320,960]{1,0:T(8,128)} custom-call(s32[1]{0:T(128)} %bitcast.1.core_ref.refs_0_, bf16[1280,128]{1,0:T(8,128)(2,1)S(1)} %bitcast.11, bf16[1280,128]{1,0:T(8,128)(2,1)S(1)} %collective-permute-done.3.refs_2_), custom_call_target="tpu_custom_call" | custom-call | flops 1000000 | bytes 2000000 | tf_op jit(solution)/shard_map/pallas_call | solution.py:288
Async XLA Ops:
  1.8 10.5 %collective-permute-start = (bf16[256,320]{1,0:T(8,128)(2,1)S(1)}, bf16[256,320]{1,0:T(8,128)(2,1)S(1)}, u32[]{:S(2)}, u32[]{:S(2)}) collective-permute-start(bf16[256,320]{1,0:T(8,128)(2,1)S(1)} %get-tuple-element.17), channel_id=1, source_target_pairs={{0,1},{1,2},{2,3},{3,4},{4,5},{5,6},{6,7},{7,8},{8,9},{9,10},{10,1... | collective-permute-start | bytes 491528 | tf_op jit(solution)/shard_map/ppermute | solution.py:331
  5.7 6.6 %collective-permute-start.1 = (bf16[256,320]{1,0:T(8,128)(2,1)S(1)}, bf16[256,320]{1,0:T(8,128)(2,1)S(1)}, u32[]{:S(2)}, u32[]{:S(2)}) collective-permute-start(bf16[256,320]{1,0:T(8,128)(2,1)S(1)} %get-tuple-element.18), channel_id=1, source_target_pairs={{1,0},{2,1},{3,2},{4,3},{5,4},{6,5},{7,6},{8,7},{9,8},{10,9},{11,1... | collective-permute-start | bytes 491528 | tf_op jit(solution)/shard_map/ppermute | solution.py:332
  14.0 8.4 %collective-permute-start.2 = (bf16[1280,128]{1,0:T(8,128)(2,1)S(1)}, bf16[1280,128]{1,0:T(8,128)(2,1)S(1)}, u32[]{:S(2)}, u32[]{:S(2)}) collective-permute-start(bf16[1280,128]{1,0:T(8,128)(2,1)S(1)} %get-tuple-element.20), channel_id=1, source_target_pairs={{0,32},{32,0},{1,33},{33,1},{2,34},{34,2},{3,35},{35,3},{4,36},{36... | collective-permute-start | bytes 983048 | tf_op jit(solution)/shard_map/ppermute | solution.py:373
  23.2 21.9 %all-to-all-start = ((bf16[32,40,128]{2,1,0:T(8,128)(2,1)}), bf16[32,40,128]{2,1,0:T(8,128)(2,1)S(1)}, u32[]{:S(2)}, u32[]{:S(2)}) async-start(bf16[32,40,128]{2,1,0:T(8,128)(2,1)} %bitcast.5), calls=%async_computation | async-start | bytes 655360 | tf_op jit(solution)/shard_map/all_to_all | solution.py:384
  63.1 15.7 %all-to-all-start.2 = ((bf16[32,40,128]{2,1,0:T(8,128)(2,1)}), bf16[32,40,128]{2,1,0:T(8,128)(2,1)S(1)}, u32[]{:S(2)}, u32[]{:S(2)}) async-start(bf16[32,40,128]{2,1,0:T(8,128)(2,1)} %shard_map.91), calls=%async_computation.2 | async-start | bytes 655360 | tf_op jit(solution)/shard_map/all_to_all | solution.py:388
  78.8 7.6 %collective-permute-start.3 = (bf16[1280,128]{1,0:T(8,128)(2,1)S(1)}, bf16[1280,128]{1,0:T(8,128)(2,1)S(1)}, u32[]{:S(2)}, u32[]{:S(2)}) collective-permute-start(bf16[1280,128]{1,0:T(8,128)(2,1)S(1)} %bitcast.10), channel_id=1, source_target_pairs={{0,32},{32,0},{1,33},{33,1},{2,34},{34,2},{3,35},{35,3},{4,36},{36... | collective-permute-start | bytes 983048 | tf_op jit(solution)/shard_map/ppermute | solution.py:400

commit v3 on v2

v3 whole, which is shorter than its diff:
```python
import math

import jax
import jax.numpy as jnp
from jax import lax
from jax.experimental import pallas as pl
from jax.experimental.pallas import tpu as pltpu
from jax.sharding import Mesh
from jax.sharding import PartitionSpec as P

F32 = jnp.float32
BF16 = jnp.bfloat16
C = 320
GROUPS = 32
PER_GROUP = C // GROUPS
CAP = 3
HH = 32
WW = 8
PIX = HH * WW
ROWS = CAP * PIX
ENTRIES = PIX * PER_GROUP
VMEM = pltpu.VMEM
LANES = 128
X_SIZE = 4
HALF = 4 * C
PARAMS = pltpu.CompilerParams(vmem_limit_bytes=28 * 1024 * 1024)


def group_matrix():
    row = lax.broadcasted_iota(jnp.int32, (C, C), 0).astype(F32)
    col = lax.broadcasted_iota(jnp.int32, (C, C), 1).astype(F32)
    inv = 1.0 / PER_GROUP
    same = jnp.floor((row + 0.5) * inv) == jnp.floor((col + 0.5) * inv)
    return same.astype(F32).astype(BF16)


def group_mean(sums, matrix):
    high = sums.astype(BF16).astype(F32)
    rest = sums - high
    middle = rest.astype(BF16).astype(F32)
    terms = jnp.concatenate([high, middle, rest - middle, jnp.zeros((8, C), F32)], axis=0)
    added = jnp.dot(terms.astype(BF16), matrix, preferred_element_type=F32)
    return (added[0:8] + added[8:16] + added[16:24]) / ENTRIES


def frame(s):
    if isinstance(s, int):
        return pl.ds(s * PIX, PIX)
    return pl.ds(pl.multiple_of(s * PIX, PIX), PIX)


def sigmoid(values):
    return 0.5 * jnp.tanh(0.5 * values) + 0.5


def shifted(values, step):
    cube = values.reshape(HH, WW, C)
    rolled = jnp.roll(cube, -step, axis=1)
    col = lax.broadcasted_iota(jnp.int32, (HH, WW, C), 1)
    keep = (col < WW - 1) if step > 0 else (col > 0)
    return jnp.where(keep, rolled, 0.0).reshape(PIX, C)


def down(values):
    return jnp.concatenate([jnp.zeros((WW, C), F32), values[:-WW]], axis=0)


def up(values):
    return jnp.concatenate([values[WW:], jnp.zeros((WW, C), F32)], axis=0)


def start_all(sems, *pairs):
    copies = [pltpu.make_async_copy(src, dst, sems.at[i]) for i, (src, dst) in enumerate(pairs)]
    for copy in copies:
        copy.start()
    return copies


def edge_kernel(
    t_ref, core_ref, counts_hbm, g_hbm, x_hbm, one_ref, two_ref, g_ref, x_ref, counts, sems
):
    for copy in start_all(sems, (counts_hbm, counts), (g_hbm, g_ref), (x_hbm, x_ref)):
        copy.wait()
    last = (counts[0, t_ref[0]] - 1) * (1 - core_ref[0])
    one_ref[...] = g_ref[frame(last), :]
    last = (counts[0, t_ref[0]] - 1) * core_ref[0]
    two_ref[...] = g_ref[frame(last), :]


def forward_kernel(
    t_ref, x_ref, counts_hbm, gain_hbm, shift_hbm, wt_hbm, w_hbm, y_ref, u_ref, stats_ref, wt_ref,
    counts, gain_ref, shift_ref, w_ref, cols, wst, prod, sems,
):
    weights = [(w_hbm.at[pl.ds(q, 80), :], w_ref.at[pl.ds(q, 80), :]) for q in range(0, C, 80)]
    copies = start_all(
        sems,
        (gain_hbm, gain_ref),
        (shift_hbm, shift_ref),
        (counts_hbm, counts),
        (wt_hbm, wt_ref),
        *weights,
    )
    matrix = group_matrix()
    blank = jnp.zeros((8 - CAP, C), F32)

    def per_frame(fn):
        return jnp.concatenate([fn(s) for s in range(CAP)] + [blank], axis=0)

    def load(s):
        return x_ref[s * PIX : (s + 1) * PIX, :].astype(F32)

    mean = group_mean(per_frame(lambda s: jnp.sum(load(s), axis=0, keepdims=True)), matrix)

    def squares(s):
        centred = load(s) - mean[s : s + 1]
        return jnp.sum(centred * centred, axis=0, keepdims=True)

    inv = lax.rsqrt(group_mean(per_frame(squares), matrix) + 1e-05)
    stats_ref[0] = mean
    stats_ref[1] = inv
    for copy in copies[:3]:
        copy.wait()
    n = counts[0, t_ref[0]]
    gain = gain_ref[...].reshape(1, C)
    shift = shift_ref[...].reshape(1, C)

    def activate(s):
        values = (x_ref[frame(s), :].astype(F32) - stats_ref[0, pl.ds(s, 1), :]) * stats_ref[
            1, pl.ds(s, 1), :
        ] * gain + shift
        act = values * sigmoid(values)
        cols[frame(s), 0:C] = shifted(act, -1).astype(BF16)
        cols[frame(s), C : 2 * C] = act.astype(BF16)
        cols[frame(s), 2 * C : 3 * C] = shifted(act, 1).astype(BF16)

    for s in range(CAP):
        activate(s)
    for copy in copies[4:]:
        copy.wait()
    for i in range(3):
        wst[i * C : (i + 1) * C, :] = w_ref[:, i * 3 * C : (i + 1) * 3 * C]
    prod[...] = lax.dot_general(
        cols[...], wst[...], (((1,), (1,)), ((), ())), preferred_element_type=F32
    )

    def add(s):
        rows = frame(s)
        mixed = down(prod[rows, 0:C]) + prod[rows, C : 2 * C] + up(prod[rows, 2 * C : 3 * C])
        y = (x_ref[rows, :].astype(F32) + mixed).astype(BF16)
        y_ref[rows, :] = y
        yf = y.astype(F32)
        live = (jnp.int32(s) < n).astype(F32)
        u_ref[rows, :] = (yf * sigmoid(yf) * live).astype(BF16)

    for s in range(CAP):
        add(s)
    copies[3].wait()


def own_kernel(t_ref, u_ref, g_ref, counts_hbm, whole_ref, counts, sems):
    (copy,) = start_all(sems, (counts_hbm, counts))
    copy.wait()
    n = counts[0, t_ref[0]]
    live = [(jnp.int32(s) < n).astype(BF16) for s in range(CAP)]
    flipped = jnp.concatenate([g_ref[frame(s), :] * live[s] for s in range(CAP)], axis=0).T
    whole_ref[:, 3 * C - 3 * C % LANES :] = jnp.zeros((C, 8 * LANES - 3 * C + 3 * C % LANES), F32)

    def term(own, taken):
        return jnp.dot(own, taken, preferred_element_type=F32)

    whole_ref[:, 0:C] = term(flipped[:, PIX:], u_ref[0 : ROWS - PIX, :])
    whole_ref[:, C : 2 * C] = term(flipped, u_ref[...])
    whole_ref[:, 2 * C : 3 * C] = term(flipped[:, 0 : ROWS - PIX], u_ref[PIX:, :])


def sides(core, one_ref, two_ref):
    before = jnp.where(core == 0, one_ref[...], two_ref[...])
    after = jnp.where(core == 0, two_ref[...], one_ref[...])
    return before, after


def grad_kernel(
    t_ref, core_ref, whole_ref, u_ref, one_ref, two_ref, counts_hbm, keep_ref, send_ref, counts,
    whole, sems,
):
    (copy,) = start_all(sems, (counts_hbm, counts))
    core = core_ref[0]
    before, after = sides(core, one_ref, two_ref)
    copy.wait()
    n = counts[0, t_ref[0]]
    whole[...] = whole_ref[...]
    whole[:, 0:C] += jnp.dot(after.T, u_ref[frame(n - 1), :], preferred_element_type=F32)
    whole[:, 2 * C : 3 * C] += jnp.dot(before.T, u_ref[0:PIX, :], preferred_element_type=F32)
    for j in range(4):
        first = whole[:, j * LANES : (j + 1) * LANES]
        second = whole[:, (j + 4) * LANES : (j + 5) * LANES]
        keep_ref[j * C : (j + 1) * C, :] = jnp.where(core == 0, first, second)
        send_ref[j * C : (j + 1) * C, :] = jnp.where(core == 0, second, first).astype(BF16)


def temporal_kernel(
    t_ref, core_ref, y_ref, g_ref, one_ref, two_ref, wt_ref, counts_hbm, dy_ref, ext, counts, sems
):
    (copy,) = start_all(sems, (counts_hbm, counts))
    before, after = sides(core_ref[0], one_ref, two_ref)
    ext[0:PIX, :] = before
    ext[PIX : PIX + ROWS, :] = g_ref[...]
    ext[PIX + ROWS :, :] = after
    copy.wait()
    ext[frame(counts[0, t_ref[0]] + 1), :] = after
    for s in range(CAP):
        back = jnp.zeros((PIX, C), F32)
        for k in range(3):
            back = back + jnp.dot(
                ext[frame(s + 2 - k), :],
                wt_ref[:, k * C : (k + 1) * C],
                preferred_element_type=F32,
            )
        yf = y_ref[frame(s), :].astype(F32)
        sig = sigmoid(yf)
        back = (sig * (1.0 + yf * (1.0 - sig)) * back).astype(BF16)
        dy_ref[frame(s), :] = (g_ref[frame(s), :].astype(F32) + back.astype(F32)).astype(BF16)


def spatial_kernel(
    t_ref, dy_ref, stats_ref, x_ref, counts_hbm, gain_hbm, shift_hbm, w_hbm, out_ref,
    counts, gain_ref, shift_ref, w_ref, cols, wst, prod, sems,
):
    weights = [(w_hbm.at[pl.ds(q, 80), :], w_ref.at[pl.ds(q, 80), :]) for q in range(0, C, 80)]
    copies = start_all(
        sems,
        *weights,
        (gain_hbm, gain_ref),
        (shift_hbm, shift_ref),
        (counts_hbm, counts),
    )

    def spread(s):
        dy = dy_ref[frame(s), :]
        dyf = dy.astype(F32)
        cols[frame(s), 0:C] = shifted(dyf, 1).astype(BF16)
        cols[frame(s), C : 2 * C] = dy
        cols[frame(s), 2 * C : 3 * C] = shifted(dyf, -1).astype(BF16)

    for s in range(CAP):
        spread(s)
    for copy in copies:
        copy.wait()
    for i in range(3):
        for j in range(3):
            tap = 3 * i + j
            wst[j * C : (j + 1) * C, i * C : (i + 1) * C] = w_ref[:, tap * C : (tap + 1) * C]
    prod[...] = jnp.dot(cols[...], wst[...], preferred_element_type=F32)
    matrix = group_matrix()
    n = counts[0, t_ref[0]]
    gain = gain_ref[...].reshape(1, C)
    shift = shift_ref[...].reshape(1, C)

    def finish(s):
        rows = frame(s)
        da = up(prod[rows, 0:C]) + prod[rows, C : 2 * C] + down(prod[rows, 2 * C : 3 * C])
        mean = stats_ref[0, pl.ds(s, 1), :]
        inv = stats_ref[1, pl.ds(s, 1), :]
        normed = (x_ref[rows, :].astype(F32) - mean) * inv
        values = normed * gain + shift
        sig = sigmoid(values)
        dn = da * (sig * (1.0 + values * (1.0 - sig))) * gain
        sums = jnp.concatenate(
            [
                jnp.sum(dn, axis=0, keepdims=True),
                jnp.sum(dn * normed, axis=0, keepdims=True),
                jnp.zeros((6, C), F32),
            ],
            axis=0,
        )
        means = group_mean(sums, matrix)
        dx = inv * (dn - means[0:1] - normed * means[1:2])
        total = dy_ref[rows, :].astype(F32) + dx
        out_ref[rows, :] = jnp.where(jnp.int32(s) < n, total, 0.0).astype(BF16)

    for s in range(CAP):
        finish(s)


def sum_kernel(copies, x_ref, out_ref):
    total = x_ref[0].astype(F32)
    for i in range(1, x_ref.shape[0]):
        total = total + x_ref[i].astype(F32)
    total = total.astype(BF16)
    for i in range(copies):
        out_ref[i] = total


def final_kernel(scale, core_ref, mine_ref, other_ref, out_ref):
    core = core_ref[0]
    for j in range(4):
        mine = mine_ref[j * C : (j + 1) * C, :].astype(F32) * scale
        other = other_ref[j * C : (j + 1) * C, :].astype(F32) * scale
        out_ref[:, j * LANES : (j + 1) * LANES] = jnp.where(core == 0, mine, other)
        width = min(LANES, 3 * C - (j + 4) * LANES)
        upper = jnp.where(core == 0, other, mine)
        out_ref[:, (j + 4) * LANES : (j + 4) * LANES + width] = upper[:, :width]


SMEM_SPEC = pl.BlockSpec(memory_space=pltpu.SMEM)
VMEM_SPEC = pl.BlockSpec(memory_space=pltpu.VMEM)
HBM_SPEC = pl.BlockSpec(memory_space=pltpu.HBM)


def call(body, scalars, arrays, away, outs, scratch, cost):
    away = [pltpu.with_memory_space_constraint(a, pltpu.HBM) for a in away]
    return pl.pallas_call(
        body,
        out_shape=outs,
        in_specs=[SMEM_SPEC] * len(scalars) + [VMEM_SPEC] * len(arrays) + [HBM_SPEC] * len(away),
        out_specs=[VMEM_SPEC] * len(outs) if isinstance(outs, list) else VMEM_SPEC,
        scratch_shapes=scratch,
        compiler_params=PARAMS,
        cost_estimate=pl.CostEstimate(flops=cost[0], bytes_accessed=cost[1], transcendentals=0),
    )(*scalars, *arrays, *away)


array = jax.ShapeDtypeStruct
dma = pltpu.SemaphoreType.DMA
ACT = array((ROWS, C), BF16)
ONE = array((PIX, C), BF16)
VECTOR = VMEM((C,), F32)
WEIGHTS = VMEM((C, 9 * C), BF16)
COLUMNS = VMEM((ROWS, 3 * C), BF16)
STACKED = VMEM((3 * C, 3 * C), BF16)
PRODUCT = VMEM((ROWS, 3 * C), F32)


def counts_mem(counts):
    return pltpu.SMEM(counts.shape, jnp.int32)


def run_edge(place, core, counts, g, x):
    return call(
        edge_kernel,
        (place, core),
        (),
        (counts, g, x),
        [ONE, ONE, ACT, ACT],
        [counts_mem(counts), dma((3,))],
        (0, 1_200_000),
    )


def run_forward(place, counts, x, gain, shift, wt_t, w_t):
    return call(
        forward_kernel,
        (place,),
        (x,),
        (counts, gain, shift, wt_t, w_t),
        [ACT, ACT, array((2, 8, C), F32), array(wt_t.shape, BF16)],
        [counts_mem(counts), VECTOR, VECTOR, WEIGHTS, COLUMNS, STACKED, PRODUCT, dma((8,))],
        (2 * ROWS * 9 * C * C, 4_000_000),
    )


def run_own(place, u, g_own, counts):
    return call(
        own_kernel,
        (place,),
        (u, g_own),
        (counts,),
        array((C, 8 * LANES), F32),
        [counts_mem(counts), dma((1,))],
        (2 * ROWS * 3 * C * C, 2_500_000),
    )


def run_grad(place, core, whole, u, one, two, counts):
    return call(
        grad_kernel,
        (place, core),
        (whole, u, one, two),
        (counts,),
        [array((HALF, LANES), F32), array((HALF, LANES), BF16)],
        [counts_mem(counts), VMEM((C, 8 * LANES), F32), dma((1,))],
        (4 * PIX * C * C, 2_500_000),
    )


def run_temporal(place, core, y, g_own, one, two, wt_own, counts):
    return call(
        temporal_kernel,
        (place, core),
        (y, g_own, one, two, wt_own),
        (counts,),
        ACT,
        [VMEM((5 * PIX, C), BF16), counts_mem(counts), dma((1,))],
        (2 * ROWS * 3 * C * C, 2_500_000),
    )


def run_spatial(place, dy, stats, x, counts, gain, shift, w_t):
    return call(
        spatial_kernel,
        (place,),
        (dy, stats, x),
        (counts, gain, shift, w_t),
        ACT,
        [counts_mem(counts), VECTOR, VECTOR, WEIGHTS, COLUMNS, STACKED, PRODUCT, dma((7,))],
        (2 * ROWS * 9 * C * C, 4_000_000),
    )


def run_sum(parts, copies):
    def body(*refs):
        sum_kernel(copies, *refs)

    out = array((copies,) + parts.shape[1:], BF16)
    return call(body, (), (parts,), (), out, [], (parts.size, 2 * parts.size))


def run_final(scale, core, mine, other):
    def body(*refs):
        final_kernel(scale, *refs)

    return call(body, (core,), (mine, other), (), array((C, 3 * C), F32), [], (1_000_000, 2_000_000))


def shards(frames_in, cotangent, counts, norm_gain, norm_shift, spatial_weight, temporal_weight):
    shape = frames_in.shape
    x = frames_in.reshape(ROWS, C)
    g = cotangent.reshape(ROWS, C)
    place = lax.axis_index("tm").astype(jnp.int32).reshape(1)
    core = lax.axis_index("c").astype(jnp.int32).reshape(1)
    w_t = spatial_weight.T
    wt_t = temporal_weight.T
    tm_size = lax.axis_size("tm")
    pair = [(0, 1), (1, 0)]
    right = [[(c * tm_size + t, c * tm_size + t + 1) for t in range(tm_size - 1)] for c in range(2)]
    left = [[(b, a) for a, b in line] for line in right]

    one, two, g_own, x_own = run_edge(place, core, counts, g, x)
    one = lax.ppermute(one, ("c", "tm"), right[0] + left[1])
    two = lax.ppermute(two, ("c", "tm"), left[0] + right[1])
    y, u, stats, wt_own = run_forward(
        place, counts, x_own, norm_gain, norm_shift, wt_t, w_t
    )
    whole = run_own(place, u, g_own, counts)
    keep, send = run_grad(place, core, whole, u, one, two, counts)

    near, far = groups()
    size = len(near[0])
    got = lax.ppermute(send, "c", pair)
    part = (keep + got.astype(F32)).astype(BF16).reshape(size, HALF // size, LANES)
    part = run_sum(exchange(part, near), len(far[0]))
    part, one = lax.optimization_barrier((part, one))
    dy = run_temporal(place, core, y, g_own, one, two, wt_own, counts)
    d_in = run_spatial(place, dy, stats, x_own, counts, norm_gain, norm_shift, w_t)
    part, d_in = lax.optimization_barrier((exchange(part, far), d_in))
    part = run_sum(part, size)
    mine = exchange(part, near).reshape(HALF, LANES)
    other = lax.ppermute(mine, "c", pair)

    frames = lax.axis_size(("z", "c")) * 2 * tm_size
    grad = run_final(1.0 / math.sqrt(frames * HH * WW), core, mine, other)
    return (d_in.reshape(shape), grad.T)


def groups():
    zs, ys, xs = lax.axis_size("z"), lax.axis_size("tm") // X_SIZE, X_SIZE

    def at(z, c, y, x):
        return ((z * 2 + c) * ys + y) * xs + x

    near = [
        [at(z + i, c, y + j, x) for i in range(2) for j in range(2) for x in range(xs)]
        for z in range(0, zs, 2)
        for c in range(2)
        for y in range(0, ys, 2)
    ]
    far = [
        [at(z, c, y, x) for z in range(i, zs, 2) for y in range(j, ys, 2)]
        for i in range(2)
        for j in range(2)
        for c in range(2)
        for x in range(xs)
    ]
    return near, far


def exchange(parts, members):
    return lax.all_to_all(parts, ("z", "c", "tm"), 0, 0, axis_index_groups=members, tiled=True)


def solution(mesh):
    devices = mesh.devices
    dp, tm = devices.shape
    split = Mesh(devices.reshape(dp // 2, 2, tm), ("z", "c", "tm"))
    return jax.shard_map(
        shards,
        mesh=split,
        in_specs=(
            P(("z", "c"), "tm", None, None, None),
            P(("z", "c"), "tm", None, None, None),
            P(("z", "c"), None),
            P(),
            P(),
            P(),
            P(),
        ),
        out_specs=(P(("z", "c"), "tm", None, None, None), P()),
        check_vma=False,
    )
```

time: 88.2 us -> 83 us (0.941)
  waiting for transfers between devices: 16.9 us -> 9.36 us
  blocking collectives: 17.2 us -> 23.8 us
  Pallas kernels: 19.3 us -> 17.5 us
  starting transfers between devices: 32.7 us -> 31 us
    all_to_all x2 -> x1, waiting for transfers between devices: 14.4 us -> 6.88 us  [exchange(): lax.all_to_all(parts, ('z', 'c', 'tm'), 0, 0, axis_index_groups=members,...]
    all_to_all x1 -> x2, blocking collectives: 17.2 us -> 23.8 us  [exchange(): lax.all_to_all(parts, ('z', 'c', 'tm'), 0, 0, axis_index_groups=members,...]
    pallas_call x8 -> x9, Pallas kernels: 19.3 us -> 17.5 us  [call(): pl.pallas_call(body, out_shape=outs, in_specs=[SMEM_SPEC] * len(scalars)...]
    ppermute x1, starting transfers between devices: 6.32 us -> 5.21 us  [shards(): other = lax.ppermute(mine, 'c', pair)]
    all_to_all x2 -> x1, starting transfers between devices: 14 us -> 13.7 us  [exchange(): lax.all_to_all(parts, ('z', 'c', 'tm'), 0, 0, axis_index_groups=members,...]
  transfers between devices with their start and end apart: 6 -> 5, of which waited for: 4 -> 3; matrix products, arithmetic and copies ran while one was open for 0% -> 0% of each run, Pallas kernels for 16% -> 16%
where the time goes in v3:
time: 83 us; the launch traced here: 82.5 us
  starting transfers between devices  31 us (37%)
  blocking collectives  23.8 us (29%)
  Pallas kernels  17.5 us (21%)
  waiting for transfers between devices  9.36 us (11%)
    all_to_all x2, blocking collectives, exchange(): lax.all_to_all(parts, ('z', 'c', 'tm'), 0, 0, axis_index_groups=members,...  23.8 us
    pallas_call x9, Pallas kernels, call(): pl.pallas_call(body, out_shape=outs, in_specs=[SMEM_SPEC] * len(scalars)...  17.5 us
    all_to_all x1, starting transfers between devices, exchange(): lax.all_to_all(parts, ('z', 'c', 'tm'), 0, 0, axis_index_groups=members,...  13.7 us
    all_to_all x1, waiting for transfers between devices, exchange(): lax.all_to_all(parts, ('z', 'c', 'tm'), 0, 0, axis_index_groups=members,...  6.88 us
    ppermute x1, starting transfers between devices, shards(): got = lax.ppermute(send, 'c', pair)  6.25 us
    ppermute x1, starting transfers between devices, shards(): other = lax.ppermute(mine, 'c', pair)  5.21 us
    ppermute x1, starting transfers between devices, shards(): two = lax.ppermute(two, ('c', 'tm'), left[0] + right[1])  4.58 us
  transfers between devices with their start and end apart: 5, of which 3 were waited for; matrix products, arithmetic and copies ran while one was open for 0% of the time, Pallas kernels for 16%

profile of v3, /device:TPU:1, one launch (start us, length us, event | category | flops | bytes accessed | tf_op | source)
XLA Modules:
  0.0 82.5 jit_solution(11736510509172297014)
XLA Ops:
  0.6 1.3 %shard_map.86 = (bf16[256,320]{1,0:T(8,128)(2,1)S(1)}, bf16[256,320]{1,0:T(8,128)(2,1)S(1)}, bf16[768,320]{1,0:T(8,128)(2,1)S(1)}, bf16[768,320]{1,0:T(8,128)(2,1)S(1)}) custom-call(s32[1]{0:T(128)} %bitcast.t_ref, s32[1]{0:T(128)} %bitcast.1.core_ref.refs_0_, s32[1,32]{1,0:T(1,128)} %counts_hbm.11, bf16[768,320]{1,0:T(8,128)(2,1)} %bitcast.14, ...), custom_call_target="tpu_custom_call" | custom-call | bytes 1200000 | tf_op jit(solution)/shard_map/pallas_call | solution.py:312
  1.9 1.3 %collective-permute-start = (bf16[256,320]{1,0:T(8,128)(2,1)S(1)}, bf16[256,320]{1,0:T(8,128)(2,1)S(1)}, u32[]{:S(2)}, u32[]{:S(2)}) collective-permute-start(bf16[256,320]{1,0:T(8,128)(2,1)S(1)} %get-tuple-element.19), channel_id=1, source_target_pairs={{0,1},{1,2},{2,3},{3,4},{4,5},{5,6},{6,7},{7,8},{8,9},{9,10},{10,1... | collective-permute-start | bytes 491528 | tf_op jit(solution)/shard_map/ppermute | solution.py:439
  3.2 4.6 %collective-permute-start.1 = (bf16[256,320]{1,0:T(8,128)(2,1)S(1)}, bf16[256,320]{1,0:T(8,128)(2,1)S(1)}, u32[]{:S(2)}, u32[]{:S(2)}) collective-permute-start(bf16[256,320]{1,0:T(8,128)(2,1)S(1)} %get-tuple-element.20), channel_id=1, source_target_pairs={{1,0},{2,1},{3,2},{4,3},{5,4},{6,5},{7,6},{8,7},{9,8},{10,9},{11,1... | collective-permute-start | bytes 491528 | tf_op jit(solution)/shard_map/ppermute | solution.py:440
  7.8 4.0 %shard_map.87 = (bf16[768,320]{1,0:T(8,128)(2,1)S(1)}, bf16[768,320]{1,0:T(8,128)(2,1)S(1)}, f32[2,8,320]{2,1,0:T(8,128)S(1)}, bf16[320,960]{1,0:T(8,128)(2,1)S(1)}) custom-call(s32[1]{0:T(128)} %bitcast.t_ref, bf16[768,320]{1,0:T(8,128)(2,1)S(1)} %get-tuple-element.16.x_ref, s32[1,32]{1,0:T(1,128)} %counts_hbm.11, f32[320]{0:T(512)} %gain_hbm.3, ...), custom_call_target="tpu_custom_call" | custom-call | flops 1415577600 | bytes 4000000 | tf_op jit(solution)/shard_map/pallas_call | solution.py:312
  11.8 1.5 %shard_map.88.whole_ref = f32[320,1024]{1,0:T(8,128)S(1)} custom-call(s32[1]{0:T(128)} %bitcast.t_ref, bf16[768,320]{1,0:T(8,128)(2,1)S(1)} %get-tuple-element.17.u_ref, bf16[768,320]{1,0:T(8,128)(2,1)S(1)} %get-tuple-element.18.g_ref, s32[1,32]{1,0:T(1,128)} %counts_hbm.11), custom_call_target="tpu_custom_call" | custom-call | flops 471859200 | bytes 2500000 | tf_op jit(solution)/shard_map/pallas_call | solution.py:312
  13.3 0.0 collective-permute-done.one_ref
  13.3 0.0 collective-permute-done.1.two_ref
  13.4 1.1 %shard_map.89 = (f32[1280,128]{1,0:T(8,128)S(1)}, bf16[1280,128]{1,0:T(8,128)(2,1)S(1)}) custom-call(s32[1]{0:T(128)} %bitcast.t_ref, s32[1]{0:T(128)} %bitcast.1.core_ref.refs_0_, f32[320,1024]{1,0:T(8,128)S(1)} %shard_map.88.whole_ref, bf16[768,320]{1,0:T(8,128)(2,1)S(1)} %get-tuple-element.17.u_ref, bf16[256,320]{1,0:T(8,128)(2,1)S(1)} %collective-permute-done.one_ref, ...), custom_call_target="tpu_custom_call" | custom-call | flops 104857600 | bytes 2500000 | tf_op jit(solution)/shard_map/pallas_call | solution.py:312
  14.5 6.3 %collective-permute-start.2 = (bf16[1280,128]{1,0:T(8,128)(2,1)S(1)}, bf16[1280,128]{1,0:T(8,128)(2,1)S(1)}, u32[]{:S(2)}, u32[]{:S(2)}) collective-permute-start(bf16[1280,128]{1,0:T(8,128)(2,1)S(1)} %get-tuple-element.22), channel_id=1, source_target_pairs={{0,32},{32,0},{1,33},{33,1},{2,34},{34,2},{3,35},{35,3},{4,36},{36... | collective-permute-start | bytes 983048 | tf_op jit(solution)/shard_map/ppermute | solution.py:449
  20.7 1.2 %collective-permute-done.2 = bf16[1280,128]{1,0:T(8,128)(2,1)S(1)} collective-permute-done((bf16[1280,128]{1,0:T(8,128)(2,1)S(1)}, bf16[1280,128]{1,0:T(8,128)(2,1)S(1)}, u32[]{:S(2)}, u32[]{:S(2)}) %collective-permute-start.2) | collective-permute-done | bytes 327712 | tf_op jit(solution)/shard_map/ppermute | solution.py:449
  21.9 0.1 add_convert_fusion
  22.0 13.6 %all_to_all.15.refs_0_ = bf16[16,80,128]{2,1,0:T(8,128)(2,1)S(1)} all-to-all(bf16[16,80,128]{2,1,0:T(8,128)(2,1)S(1)} %bitcast.12), channel_id=1, replica_groups={{0,1,2,3,4,5,6,7,64,65,66,67,68,69,70,71},{8,9,10,11,12,13,14,15,72,73,..., dimensions={0} | all-to-all | bytes 655360 | tf_op jit(solution)/shard_map/all_to_all | solution.py:488
  35.6 0.8 shard_map.90
  36.4 13.7 %all-to-all-start.1 = ((bf16[16,80,128]{2,1,0:T(8,128)(2,1)}), bf16[16,80,128]{2,1,0:T(8,128)(2,1)S(1)}, u32[]{:S(2)}, u32[]{:S(2)}) async-start(bf16[16,80,128]{2,1,0:T(8,128)(2,1)} %shard_map.90), calls=%async_computation.1 | async-start | bytes 655360 | tf_op jit(solution)/shard_map/all_to_all | solution.py:488
  50.1 2.1 %shard_map.91.dy_ref = bf16[768,320]{1,0:T(8,128)(2,1)S(1)} custom-call(s32[1]{0:T(128)} %bitcast.t_ref, s32[1]{0:T(128)} %bitcast.1.core_ref.refs_0_, bf16[768,320]{1,0:T(8,128)(2,1)S(1)} %get-tuple-element.24.y_ref, bf16[768,320]{1,0:T(8,128)(2,1)S(1)} %get-tuple-element.18.g_ref, bf16[256,320]{1,0:T(8,128)(2,1)S(1)} %collective-permute-done.one_ref, ...), custom_call_target="tpu_custom_call" | custom-call | flops 471859200 | bytes 2500000 | tf_op jit(solution)/shard_map/pallas_call | solution.py:312
  52.2 5.5 %shard_map.92 = bf16[768,320]{1,0:T(8,128)(2,1)} custom-call(s32[1]{0:T(128)} %bitcast.t_ref, bf16[768,320]{1,0:T(8,128)(2,1)S(1)} %shard_map.91.dy_ref, f32[2,8,320]{2,1,0:T(8,128)S(1)} %get-tuple-element.27.stats_ref, bf16[768,320]{1,0:T(8,128)(2,1)S(1)} %get-tuple-element.16.x_ref, s32[1,32]{1,0:T(1,128)} %counts_hbm.11, f32[320]{0:T(512)} %gain_hbm.3, ...), custom_call_target="tpu_custom_call" | custom-call | flops 1415577600 | bytes 4000000 | tf_op jit(solution)/shard_map/pallas_call | solution.py:312
  57.7 6.9 %all-to-all-done.1.refs_0_ = bf16[16,80,128]{2,1,0:T(8,128)(2,1)S(1)} async-done(((bf16[16,80,128]{2,1,0:T(8,128)(2,1)}), bf16[16,80,128]{2,1,0:T(8,128)(2,1)S(1)}, u32[]{:S(2)}, u32[]{:S(2)}) %all-to-all-start.1) | async-done | bytes 327712 | tf_op jit(solution)/shard_map/all_to_all | solution.py:488
  64.6 0.1 shard_map.93
  64.7 10.2 %all_to_all.16 = bf16[16,80,128]{2,1,0:T(8,128)(2,1)S(1)} all-to-all(bf16[16,80,128]{2,1,0:T(8,128)(2,1)S(1)} %shard_map.93), channel_id=1, replica_groups={{0,1,2,3,4,5,6,7,64,65,66,67,68,69,70,71},{8,9,10,11,12,13,14,15,72,73,..., dimensions={0} | all-to-all | bytes 655360 | tf_op jit(solution)/shard_map/all_to_all | solution.py:488
  74.8 5.2 %collective-permute-start.3 = (bf16[1280,128]{1,0:T(8,128)(2,1)S(1)}, bf16[1280,128]{1,0:T(8,128)(2,1)S(1)}, u32[]{:S(2)}, u32[]{:S(2)}) collective-permute-start(bf16[1280,128]{1,0:T(8,128)(2,1)S(1)} %bitcast.10), channel_id=1, source_target_pairs={{0,32},{32,0},{1,33},{33,1},{2,34},{34,2},{3,35},{35,3},{4,36},{36... | collective-permute-start | bytes 983048 | tf_op jit(solution)/shard_map/ppermute | solution.py:458
  80.1 1.2 %collective-permute-done.3.refs_2_ = bf16[1280,128]{1,0:T(8,128)(2,1)S(1)} collective-permute-done((bf16[1280,128]{1,0:T(8,128)(2,1)S(1)}, bf16[1280,128]{1,0:T(8,128)(2,1)S(1)}, u32[]{:S(2)}, u32[]{:S(2)}) %collective-permute-start.3) | collective-permute-done | bytes 327712 | tf_op jit(solution)/shard_map/ppermute | solution.py:458
  81.3 1.3 %shard_map.94 = f32[320,960]{1,0:T(8,128)} custom-call(s32[1]{0:T(128)} %bitcast.1.core_ref.refs_0_, bf16[1280,128]{1,0:T(8,128)(2,1)S(1)} %bitcast.11, bf16[1280,128]{1,0:T(8,128)(2,1)S(1)} %collective-permute-done.3.refs_2_), custom_call_target="tpu_custom_call" | custom-call | flops 1000000 | bytes 2000000 | tf_op jit(solution)/shard_map/pallas_call | solution.py:312
Async XLA Ops:
  1.9 11.4 %collective-permute-start = (bf16[256,320]{1,0:T(8,128)(2,1)S(1)}, bf16[256,320]{1,0:T(8,128)(2,1)S(1)}, u32[]{:S(2)}, u32[]{:S(2)}) collective-permute-start(bf16[256,320]{1,0:T(8,128)(2,1)S(1)} %get-tuple-element.19), channel_id=1, source_target_pairs={{0,1},{1,2},{2,3},{3,4},{4,5},{5,6},{6,7},{7,8},{8,9},{9,10},{10,1... | collective-permute-start | bytes 491528 | tf_op jit(solution)/shard_map/ppermute | solution.py:439
  3.2 10.1 %collective-permute-start.1 = (bf16[256,320]{1,0:T(8,128)(2,1)S(1)}, bf16[256,320]{1,0:T(8,128)(2,1)S(1)}, u32[]{:S(2)}, u32[]{:S(2)}) collective-permute-start(bf16[256,320]{1,0:T(8,128)(2,1)S(1)} %get-tuple-element.20), channel_id=1, source_target_pairs={{1,0},{2,1},{3,2},{4,3},{5,4},{6,5},{7,6},{8,7},{9,8},{10,9},{11,1... | collective-permute-start | bytes 491528 | tf_op jit(solution)/shard_map/ppermute | solution.py:440
  14.5 7.5 %collective-permute-start.2 = (bf16[1280,128]{1,0:T(8,128)(2,1)S(1)}, bf16[1280,128]{1,0:T(8,128)(2,1)S(1)}, u32[]{:S(2)}, u32[]{:S(2)}) collective-permute-start(bf16[1280,128]{1,0:T(8,128)(2,1)S(1)} %get-tuple-element.22), channel_id=1, source_target_pairs={{0,32},{32,0},{1,33},{33,1},{2,34},{34,2},{3,35},{35,3},{4,36},{36... | collective-permute-start | bytes 983048 | tf_op jit(solution)/shard_map/ppermute | solution.py:449
  36.4 28.2 %all-to-all-start.1 = ((bf16[16,80,128]{2,1,0:T(8,128)(2,1)}), bf16[16,80,128]{2,1,0:T(8,128)(2,1)S(1)}, u32[]{:S(2)}, u32[]{:S(2)}) async-start(bf16[16,80,128]{2,1,0:T(8,128)(2,1)} %shard_map.90), calls=%async_computation.1 | async-start | bytes 655360 | tf_op jit(solution)/shard_map/all_to_all | solution.py:488
  74.8 6.5 %collective-permute-start.3 = (bf16[1280,128]{1,0:T(8,128)(2,1)S(1)}, bf16[1280,128]{1,0:T(8,128)(2,1)S(1)}, u32[]{:S(2)}, u32[]{:S(2)}) collective-permute-start(bf16[1280,128]{1,0:T(8,128)(2,1)S(1)} %bitcast.10), channel_id=1, source_target_pairs={{0,32},{32,0},{1,33},{33,1},{2,34},{34,2},{3,35},{35,3},{4,36},{36... | collective-permute-start | bytes 983048 | tf_op jit(solution)/shard_map/ppermute | solution.py:458

commit v4 on v3

--- a/solution.py
+++ b/solution.py
@@ -76,15 +76,29 @@
     return copies
 
 
+def packed(values):
+    half = PIX // 2
+    rest = values[:, 2 * LANES :]
+    rest = jnp.concatenate([rest[:half], rest[half:]], axis=1)
+    return jnp.concatenate([values[:, :LANES], values[:, LANES : 2 * LANES], rest], axis=0)
+
+
+def unpacked(values):
+    rest = values[2 * PIX :, :]
+    tail = C - 2 * LANES
+    rest = jnp.concatenate([rest[:, :tail], rest[:, tail:]], axis=0)
+    return jnp.concatenate([values[:PIX], values[PIX : 2 * PIX], rest], axis=1)
+
+
 def edge_kernel(
     t_ref, core_ref, counts_hbm, g_hbm, x_hbm, one_ref, two_ref, g_ref, x_ref, counts, sems
 ):
     for copy in start_all(sems, (counts_hbm, counts), (g_hbm, g_ref), (x_hbm, x_ref)):
         copy.wait()
     last = (counts[0, t_ref[0]] - 1) * (1 - core_ref[0])
-    one_ref[...] = g_ref[frame(last), :]
+    one_ref[...] = packed(g_ref[frame(last), :])
     last = (counts[0, t_ref[0]] - 1) * core_ref[0]
-    two_ref[...] = g_ref[frame(last), :]
+    two_ref[...] = packed(g_ref[frame(last), :])
 
 
 def forward_kernel(
@@ -176,7 +190,7 @@
 def sides(core, one_ref, two_ref):
     before = jnp.where(core == 0, one_ref[...], two_ref[...])
     after = jnp.where(core == 0, two_ref[...], one_ref[...])
-    return before, after
+    return unpacked(before), unpacked(after)
 
 
 def grad_kernel(
@@ -282,6 +296,11 @@
         finish(s)
 
 
+def add_kernel(core_ref, keep_ref, both_ref, out_ref):
+    got = jnp.where(core_ref[0] == 0, both_ref[1], both_ref[0])
+    out_ref[...] = (keep_ref[...] + got.astype(F32)).astype(BF16)
+
+
 def sum_kernel(copies, x_ref, out_ref):
     total = x_ref[0].astype(F32)
     for i in range(1, x_ref.shape[0]):
@@ -291,15 +310,12 @@
         out_ref[i] = total
 
 
-def final_kernel(scale, core_ref, mine_ref, other_ref, out_ref):
-    core = core_ref[0]
-    for j in range(4):
-        mine = mine_ref[j * C : (j + 1) * C, :].astype(F32) * scale
-        other = other_ref[j * C : (j + 1) * C, :].astype(F32) * scale
-        out_ref[:, j * LANES : (j + 1) * LANES] = jnp.where(core == 0, mine, other)
-        width = min(LANES, 3 * C - (j + 4) * LANES)
-        upper = jnp.where(core == 0, other, mine)
-        out_ref[:, (j + 4) * LANES : (j + 4) * LANES + width] = upper[:, :width]
+def final_kernel(scale, both_ref, out_ref):
+    for j in range(8):
+        width = min(LANES, 3 * C - j * LANES)
+        rows = (j % 4) * C
+        part = both_ref[j // 4, rows : rows + C, :].astype(F32) * scale
+        out_ref[:, j * LANES : j * LANES + width] = part[:, :width]
 
 
 SMEM_SPEC = pl.BlockSpec(memory_space=pltpu.SMEM)
@@ -323,7 +339,7 @@
 array = jax.ShapeDtypeStruct
 dma = pltpu.SemaphoreType.DMA
 ACT = array((ROWS, C), BF16)
-ONE = array((PIX, C), BF16)
+ONE = array((PIX * C // LANES, LANES), BF16)
 VECTOR = VMEM((C,), F32)
 WEIGHTS = VMEM((C, 9 * C), BF16)
 COLUMNS = VMEM((ROWS, 3 * C), BF16)
@@ -415,11 +431,16 @@
     return call(body, (), (parts,), (), out, [], (parts.size, 2 * parts.size))
 
 
-def run_final(scale, core, mine, other):
+def run_add(core, keep, both):
+    out = array(keep.shape, BF16)
+    return call(add_kernel, (core,), (keep, both), (), out, [], (keep.size, 8 * keep.size))
+
+
+def run_final(scale, both):
     def body(*refs):
         final_kernel(scale, *refs)
 
-    return call(body, (core,), (mine, other), (), array((C, 3 * C), F32), [], (1_000_000, 2_000_000))
+    return call(body, (), (both,), (), array((C, 3 * C), F32), [], (1_000_000, 2_000_000))
 
 
 def shards(frames_in, cotangent, counts, norm_gain, norm_shift, spatial_weight, temporal_weight):
@@ -431,7 +452,6 @@
     w_t = spatial_weight.T
     wt_t = temporal_weight.T
     tm_size = lax.axis_size("tm")
-    pair = [(0, 1), (1, 0)]
     right = [[(c * tm_size + t, c * tm_size + t + 1) for t in range(tm_size - 1)] for c in range(2)]
     left = [[(b, a) for a, b in line] for line in right]
 
@@ -446,8 +466,7 @@
 
     near, far = groups()
     size = len(near[0])
-    got = lax.ppermute(send, "c", pair)
-    part = (keep + got.astype(F32)).astype(BF16).reshape(size, HALF // size, LANES)
+    part = run_add(core, keep, lax.all_gather(send, "c")).reshape(size, HALF // size, LANES)
     part = run_sum(exchange(part, near), len(far[0]))
     part, one = lax.optimization_barrier((part, one))
     dy = run_temporal(place, core, y, g_own, one, two, wt_own, counts)
@@ -455,10 +474,10 @@
     part, d_in = lax.optimization_barrier((exchange(part, far), d_in))
     part = run_sum(part, size)
     mine = exchange(part, near).reshape(HALF, LANES)
-    other = lax.ppermute(mine, "c", pair)
+    both = lax.all_gather(mine, "c")
 
     frames = lax.axis_size(("z", "c")) * 2 * tm_size
-    grad = run_final(1.0 / math.sqrt(frames * HH * WW), core, mine, other)
+    grad = run_final(1.0 / math.sqrt(frames * HH * WW), both)
     return (d_in.reshape(shape), grad.T)
 
 

time: 83 us -> 80.3 us (0.967)
  starting transfers between devices: 31 us -> 19.6 us
  blocking collectives: 23.8 us -> 35.1 us
  waiting for transfers between devices: 9.36 us -> 6.71 us
    ppermute x2 -> x0, starting transfers between devices: 11.5 us -> none  [the longest x1 6.25 us: shards(): got = lax.ppermute(send, 'c', pair)]
    all_gather x0 -> x2, blocking collectives: none -> 11.3 us  [the longest x1 5.89 us: shards(): lax.all_gather(send, 'c')]
    ppermute x2 -> x0, waiting for transfers between devices: 2.47 us -> none  [the longest x1 1.23 us: shards(): got = lax.ppermute(send, 'c', pair)]
    pallas_call x9 -> x10, Pallas kernels: 17.5 us -> 17.8 us  [call(): pl.pallas_call(body, out_shape=outs, in_specs=[SMEM_SPEC] * len(scalars)...]
  transfers between devices with their start and end apart: 5 -> 3, of which waited for: 3 -> 1; matrix products, arithmetic and copies ran while one was open for 0% -> 0% of each run, Pallas kernels for 16% -> 16%
where the time goes in v4:
time: 80.3 us; the launch traced here: 79.9 us
  blocking collectives  35.1 us (44%)
  starting transfers between devices  19.6 us (24%)
  Pallas kernels  17.8 us (22%)
  waiting for transfers between devices  6.71 us (8%)
    all_to_all x2, blocking collectives, exchange(): lax.all_to_all(parts, ('z', 'c', 'tm'), 0, 0, axis_index_groups=members,...  23.8 us
    pallas_call x10, Pallas kernels, call(): pl.pallas_call(body, out_shape=outs, in_specs=[SMEM_SPEC] * len(scalars)...  17.8 us
    all_to_all x1, starting transfers between devices, exchange(): lax.all_to_all(parts, ('z', 'c', 'tm'), 0, 0, axis_index_groups=members,...  13.7 us
    all_to_all x1, waiting for transfers between devices, exchange(): lax.all_to_all(parts, ('z', 'c', 'tm'), 0, 0, axis_index_groups=members,...  6.7 us
    all_gather x1, blocking collectives, shards(): lax.all_gather(send, 'c')  5.89 us
    all_gather x1, blocking collectives, shards(): both = lax.all_gather(mine, 'c')  5.42 us
    ppermute x1, starting transfers between devices, shards(): two = lax.ppermute(two, ('c', 'tm'), left[0] + right[1])  4.58 us
  transfers between devices with their start and end apart: 3, of which 1 were waited for; matrix products, arithmetic and copies ran while one was open for 0% of the time, Pallas kernels for 16%

profile of v4, /device:TPU:1, one launch (start us, length us, event | category | flops | bytes accessed | tf_op | source)
XLA Modules:
  0.0 79.9 jit_solution(15738389072232523581)
XLA Ops:
  0.6 1.4 %shard_map.86 = (bf16[640,128]{1,0:T(8,128)(2,1)S(1)}, bf16[640,128]{1,0:T(8,128)(2,1)S(1)}, bf16[768,320]{1,0:T(8,128)(2,1)S(1)}, bf16[768,320]{1,0:T(8,128)(2,1)S(1)}) custom-call(s32[1]{0:T(128)} %bitcast.1.t_ref, s32[1]{0:T(128)} %bitcast.core_ref, s32[1,32]{1,0:T(1,128)} %counts_hbm.11, bf16[768,320]{1,0:T(8,128)(2,1)} %bitcast.15, ...), custom_call_target="tpu_custom_call" | custom-call | bytes 1200000 | tf_op jit(solution)/shard_map/pallas_call | solution.py:328
  2.0 1.3 %collective-permute-start = (bf16[640,128]{1,0:T(8,128)(2,1)S(1)}, bf16[640,128]{1,0:T(8,128)(2,1)S(1)}, u32[]{:S(2)}, u32[]{:S(2)}) collective-permute-start(bf16[640,128]{1,0:T(8,128)(2,1)S(1)} %get-tuple-element.19), channel_id=1, source_target_pairs={{0,1},{1,2},{2,3},{3,4},{4,5},{5,6},{6,7},{7,8},{8,9},{9,10},{10,1... | collective-permute-start | bytes 491528 | tf_op jit(solution)/shard_map/ppermute | solution.py:459
  3.3 4.6 %collective-permute-start.1 = (bf16[640,128]{1,0:T(8,128)(2,1)S(1)}, bf16[640,128]{1,0:T(8,128)(2,1)S(1)}, u32[]{:S(2)}, u32[]{:S(2)}) collective-permute-start(bf16[640,128]{1,0:T(8,128)(2,1)S(1)} %get-tuple-element.20), channel_id=1, source_target_pairs={{1,0},{2,1},{3,2},{4,3},{5,4},{6,5},{7,6},{8,7},{9,8},{10,9},{11,1... | collective-permute-start | bytes 491528 | tf_op jit(solution)/shard_map/ppermute | solution.py:460
  7.9 4.0 %shard_map.87 = (bf16[768,320]{1,0:T(8,128)(2,1)S(1)}, bf16[768,320]{1,0:T(8,128)(2,1)S(1)}, f32[2,8,320]{2,1,0:T(8,128)S(1)}, bf16[320,960]{1,0:T(8,128)(2,1)S(1)}) custom-call(s32[1]{0:T(128)} %bitcast.1.t_ref, bf16[768,320]{1,0:T(8,128)(2,1)S(1)} %get-tuple-element.16.x_ref, s32[1,32]{1,0:T(1,128)} %counts_hbm.11, f32[320]{0:T(512)} %gain_hbm.3, ...), custom_call_target="tpu_custom_call" | custom-call | flops 1415577600 | bytes 4000000 | tf_op jit(solution)/shard_map/pallas_call | solution.py:328
  11.9 1.5 %shard_map.88.whole_ref = f32[320,1024]{1,0:T(8,128)S(1)} custom-call(s32[1]{0:T(128)} %bitcast.1.t_ref, bf16[768,320]{1,0:T(8,128)(2,1)S(1)} %get-tuple-element.17.u_ref, bf16[768,320]{1,0:T(8,128)(2,1)S(1)} %get-tuple-element.18.g_ref, s32[1,32]{1,0:T(1,128)} %counts_hbm.11), custom_call_target="tpu_custom_call" | custom-call | flops 471859200 | bytes 2500000 | tf_op jit(solution)/shard_map/pallas_call | solution.py:328
  13.4 0.0 collective-permute-done.one_ref
  13.4 0.0 collective-permute-done.1.two_ref
  13.4 1.2 %shard_map.89 = (f32[1280,128]{1,0:T(8,128)S(1)}, bf16[1280,128]{1,0:T(8,128)(2,1)S(1)}) custom-call(s32[1]{0:T(128)} %bitcast.1.t_ref, s32[1]{0:T(128)} %bitcast.core_ref, f32[320,1024]{1,0:T(8,128)S(1)} %shard_map.88.whole_ref, bf16[768,320]{1,0:T(8,128)(2,1)S(1)} %get-tuple-element.17.u_ref, bf16[640,128]{1,0:T(8,128)(2,1)S(1)} %collective-permute-done.one_ref, ...), custom_call_target="tpu_custom_call" | custom-call | flops 104857600 | bytes 2500000 | tf_op jit(solution)/shard_map/pallas_call | solution.py:328
  14.6 5.9 %all-gather = bf16[2560,128]{1,0:T(8,128)(2,1)S(1)} all-gather(bf16[1280,128]{1,0:T(8,128)(2,1)S(1)} %get-tuple-element.22), channel_id=2, replica_groups=mesh['z'=8,'c'=2,'tm'=32] {'c'}, dimensions={0}, use_global_device_ids=true | all-gather | bytes 983040 | tf_op jit(solution)/shard_map/all_gather | solution.py:469
  20.5 0.1 shard_map.90
  20.6 13.6 %all_to_all.15.refs_0_ = bf16[16,80,128]{2,1,0:T(8,128)(2,1)S(1)} all-to-all(bf16[16,80,128]{2,1,0:T(8,128)(2,1)S(1)} %bitcast.12), channel_id=1, replica_groups={{0,1,2,3,4,5,6,7,64,65,66,67,68,69,70,71},{8,9,10,11,12,13,14,15,72,73,..., dimensions={0} | all-to-all | bytes 655360 | tf_op jit(solution)/shard_map/all_to_all | solution.py:507
  34.2 0.8 shard_map.91
  35.0 13.7 %all-to-all-start.1 = ((bf16[16,80,128]{2,1,0:T(8,128)(2,1)}), bf16[16,80,128]{2,1,0:T(8,128)(2,1)S(1)}, u32[]{:S(2)}, u32[]{:S(2)}) async-start(bf16[16,80,128]{2,1,0:T(8,128)(2,1)} %shard_map.91), calls=%async_computation.1 | async-start | bytes 655360 | tf_op jit(solution)/shard_map/all_to_all | solution.py:507
  48.7 2.2 %shard_map.92.dy_ref = bf16[768,320]{1,0:T(8,128)(2,1)S(1)} custom-call(s32[1]{0:T(128)} %bitcast.1.t_ref, s32[1]{0:T(128)} %bitcast.core_ref, bf16[768,320]{1,0:T(8,128)(2,1)S(1)} %get-tuple-element.24.y_ref, bf16[768,320]{1,0:T(8,128)(2,1)S(1)} %get-tuple-element.18.g_ref, bf16[640,128]{1,0:T(8,128)(2,1)S(1)} %collective-permute-done.one_ref, ...), custom_call_target="tpu_custom_call" | custom-call | flops 471859200 | bytes 2500000 | tf_op jit(solution)/shard_map/pallas_call | solution.py:328
  50.8 5.5 %shard_map.93 = bf16[768,320]{1,0:T(8,128)(2,1)} custom-call(s32[1]{0:T(128)} %bitcast.1.t_ref, bf16[768,320]{1,0:T(8,128)(2,1)S(1)} %shard_map.92.dy_ref, f32[2,8,320]{2,1,0:T(8,128)S(1)} %get-tuple-element.27.stats_ref, bf16[768,320]{1,0:T(8,128)(2,1)S(1)} %get-tuple-element.16.x_ref, s32[1,32]{1,0:T(1,128)} %counts_hbm.11, f32[320]{0:T(512)} %gain_hbm.3, ...), custom_call_target="tpu_custom_call" | custom-call | flops 1415577600 | bytes 4000000 | tf_op jit(solution)/shard_map/pallas_call | solution.py:328
  56.3 6.7 %all-to-all-done.1.refs_0_ = bf16[16,80,128]{2,1,0:T(8,128)(2,1)S(1)} async-done(((bf16[16,80,128]{2,1,0:T(8,128)(2,1)}), bf16[16,80,128]{2,1,0:T(8,128)(2,1)S(1)}, u32[]{:S(2)}, u32[]{:S(2)}) %all-to-all-start.1) | async-done | bytes 327712 | tf_op jit(solution)/shard_map/all_to_all | solution.py:507
  63.0 0.1 shard_map.94
  63.1 10.2 %all_to_all.16 = bf16[16,80,128]{2,1,0:T(8,128)(2,1)S(1)} all-to-all(bf16[16,80,128]{2,1,0:T(8,128)(2,1)S(1)} %shard_map.94), channel_id=1, replica_groups={{0,1,2,3,4,5,6,7,64,65,66,67,68,69,70,71},{8,9,10,11,12,13,14,15,72,73,..., dimensions={0} | all-to-all | bytes 655360 | tf_op jit(solution)/shard_map/all_to_all | solution.py:507
  73.3 5.4 %all_gather.11.refs_0_ = bf16[2,1280,128]{2,1,0:T(8,128)(2,1)S(1)} all-gather(bf16[1,1280,128]{2,1,0:T(8,128)(2,1)S(1)} %bitcast.14), channel_id=1, replica_groups=mesh['z'=8,'c'=2,'tm'=32] {'c'}, dimensions={0}, use_global_device_ids=true | all-gather | bytes 983040 | tf_op jit(solution)/shard_map/all_gather | solution.py:477
  78.7 1.2 %shard_map.95 = f32[320,960]{1,0:T(8,128)} custom-call(bf16[2,1280,128]{2,1,0:T(8,128)(2,1)S(1)} %all_gather.11.refs_0_), custom_call_target="tpu_custom_call" | custom-call | flops 1000000 | bytes 2000000 | tf_op jit(solution)/shard_map/pallas_call | solution.py:328
Async XLA Ops:
  2.0 11.4 %collective-permute-start = (bf16[640,128]{1,0:T(8,128)(2,1)S(1)}, bf16[640,128]{1,0:T(8,128)(2,1)S(1)}, u32[]{:S(2)}, u32[]{:S(2)}) collective-permute-start(bf16[640,128]{1,0:T(8,128)(2,1)S(1)} %get-tuple-element.19), channel_id=1, source_target_pairs={{0,1},{1,2},{2,3},{3,4},{4,5},{5,6},{6,7},{7,8},{8,9},{9,10},{10,1... | collective-permute-start | bytes 491528 | tf_op jit(solution)/shard_map/ppermute | solution.py:459
  3.3 10.1 %collective-permute-start.1 = (bf16[640,128]{1,0:T(8,128)(2,1)S(1)}, bf16[640,128]{1,0:T(8,128)(2,1)S(1)}, u32[]{:S(2)}, u32[]{:S(2)}) collective-permute-start(bf16[640,128]{1,0:T(8,128)(2,1)S(1)} %get-tuple-element.20), channel_id=1, source_target_pairs={{1,0},{2,1},{3,2},{4,3},{5,4},{6,5},{7,6},{8,7},{9,8},{10,9},{11,1... | collective-permute-start | bytes 491528 | tf_op jit(solution)/shard_map/ppermute | solution.py:460
  35.0 28.0 %all-to-all-start.1 = ((bf16[16,80,128]{2,1,0:T(8,128)(2,1)}), bf16[16,80,128]{2,1,0:T(8,128)(2,1)S(1)}, u32[]{:S(2)}, u32[]{:S(2)}) async-start(bf16[16,80,128]{2,1,0:T(8,128)(2,1)} %shard_map.91), calls=%async_computation.1 | async-start | bytes 655360 | tf_op jit(solution)/shard_map/all_to_all | solution.py:507

commit v5 on v4

--- a/solution.py
+++ b/solution.py
@@ -90,35 +90,45 @@
     return jnp.concatenate([values[:PIX], values[PIX : 2 * PIX], rest], axis=1)
 
 
+def left_first(t_ref, core_ref):
+    return lax.rem(t_ref[0] + core_ref[0], 2)
+
+
 def edge_kernel(
-    t_ref, core_ref, counts_hbm, g_hbm, x_hbm, one_ref, two_ref, g_ref, x_ref, counts, sems
+    t_ref, core_ref, counts_hbm, g_hbm, one_ref, two_ref, g_ref, counts, sems
 ):
-    for copy in start_all(sems, (counts_hbm, counts), (g_hbm, g_ref), (x_hbm, x_ref)):
+    frames = [(g_hbm.at[frame(s), :], g_ref.at[frame(s), :]) for s in range(CAP)]
+    for copy in start_all(sems, (counts_hbm, counts), *frames):
         copy.wait()
-    last = (counts[0, t_ref[0]] - 1) * (1 - core_ref[0])
-    one_ref[...] = packed(g_ref[frame(last), :])
-    last = (counts[0, t_ref[0]] - 1) * core_ref[0]
-    two_ref[...] = packed(g_ref[frame(last), :])
+    last = counts[0, t_ref[0]] - 1
+    turn = left_first(t_ref, core_ref)
+    one_ref[...] = packed(g_ref[frame(last * (1 - turn)), :])
+    two_ref[...] = packed(g_ref[frame(last * turn), :])
 
 
 def forward_kernel(
-    t_ref, x_ref, counts_hbm, gain_hbm, shift_hbm, wt_hbm, w_hbm, y_ref, u_ref, stats_ref, wt_ref,
-    counts, gain_ref, shift_ref, w_ref, cols, wst, prod, sems,
+    t_ref, counts_hbm, x_hbm, gain_hbm, shift_hbm, wt_hbm, w_hbm, y_ref, u_ref, inner_ref, last_ref,
+    stats_ref, wt_ref, x_ref, counts, gain_ref, shift_ref, w_ref, cols, wst, prod, sems,
 ):
     weights = [(w_hbm.at[pl.ds(q, 80), :], w_ref.at[pl.ds(q, 80), :]) for q in range(0, C, 80)]
+    frames = [(x_hbm.at[frame(s), :], x_ref.at[frame(s), :]) for s in range(CAP)]
     copies = start_all(
         sems,
+        *frames,
         (gain_hbm, gain_ref),
         (shift_hbm, shift_ref),
         (counts_hbm, counts),
+        *weights,
         (wt_hbm, wt_ref),
-        *weights,
     )
     matrix = group_matrix()
     blank = jnp.zeros((8 - CAP, C), F32)
 
     def per_frame(fn):
         return jnp.concatenate([fn(s) for s in range(CAP)] + [blank], axis=0)
+
+    for copy in copies[:CAP]:
+        copy.wait()
 
     def load(s):
         return x_ref[s * PIX : (s + 1) * PIX, :].astype(F32)
@@ -132,7 +142,7 @@
     inv = lax.rsqrt(group_mean(per_frame(squares), matrix) + 1e-05)
     stats_ref[0] = mean
     stats_ref[1] = inv
-    for copy in copies[:3]:
+    for copy in copies[CAP : CAP + 3]:
         copy.wait()
     n = counts[0, t_ref[0]]
     gain = gain_ref[...].reshape(1, C)
@@ -149,13 +159,15 @@
 
     for s in range(CAP):
         activate(s)
-    for copy in copies[4:]:
+    for copy in copies[CAP + 3 : -1]:
         copy.wait()
     for i in range(3):
         wst[i * C : (i + 1) * C, :] = w_ref[:, i * 3 * C : (i + 1) * 3 * C]
     prod[...] = lax.dot_general(
         cols[...], wst[...], (((1,), (1,)), ((), ())), preferred_element_type=F32
     )
+
+    zero = jnp.zeros((PIX, C), BF16)
 
     def add(s):
         rows = frame(s)
@@ -163,47 +175,42 @@
         y = (x_ref[rows, :].astype(F32) + mixed).astype(BF16)
         y_ref[rows, :] = y
         yf = y.astype(F32)
-        live = (jnp.int32(s) < n).astype(F32)
-        u_ref[rows, :] = (yf * sigmoid(yf) * live).astype(BF16)
+        units = (yf * sigmoid(yf)).astype(BF16)
+        u_ref[rows, :] = jnp.where(jnp.int32(s) < n, units, zero)
+        if s < CAP - 1:
+            inner_ref[rows, :] = jnp.where(jnp.int32(s + 1) < n, units, zero)
 
     for s in range(CAP):
         add(s)
-    copies[3].wait()
-
-
-def own_kernel(t_ref, u_ref, g_ref, counts_hbm, whole_ref, counts, sems):
-    (copy,) = start_all(sems, (counts_hbm, counts))
-    copy.wait()
-    n = counts[0, t_ref[0]]
-    live = [(jnp.int32(s) < n).astype(BF16) for s in range(CAP)]
-    flipped = jnp.concatenate([g_ref[frame(s), :] * live[s] for s in range(CAP)], axis=0).T
+    last_ref[...] = u_ref[frame(n - 1), :]
+    copies[-1].wait()
+
+
+def own_kernel(u_ref, inner_ref, g_ref, whole_ref):
+    flipped = g_ref[...].T
     whole_ref[:, 3 * C - 3 * C % LANES :] = jnp.zeros((C, 8 * LANES - 3 * C + 3 * C % LANES), F32)
 
     def term(own, taken):
         return jnp.dot(own, taken, preferred_element_type=F32)
 
-    whole_ref[:, 0:C] = term(flipped[:, PIX:], u_ref[0 : ROWS - PIX, :])
+    whole_ref[:, 0:C] = term(flipped[:, PIX:], inner_ref[...])
     whole_ref[:, C : 2 * C] = term(flipped, u_ref[...])
     whole_ref[:, 2 * C : 3 * C] = term(flipped[:, 0 : ROWS - PIX], u_ref[PIX:, :])
 
 
-def sides(core, one_ref, two_ref):
-    before = jnp.where(core == 0, one_ref[...], two_ref[...])
-    after = jnp.where(core == 0, two_ref[...], one_ref[...])
+def sides(turn, one_ref, two_ref):
+    before = jnp.where(turn == 1, one_ref[...], two_ref[...])
+    after = jnp.where(turn == 1, two_ref[...], one_ref[...])
     return unpacked(before), unpacked(after)
 
 
 def grad_kernel(
-    t_ref, core_ref, whole_ref, u_ref, one_ref, two_ref, counts_hbm, keep_ref, send_ref, counts,
-    whole, sems,
+    t_ref, core_ref, whole_ref, u_ref, last_ref, one_ref, two_ref, keep_ref, send_ref, whole
 ):
-    (copy,) = start_all(sems, (counts_hbm, counts))
     core = core_ref[0]
-    before, after = sides(core, one_ref, two_ref)
-    copy.wait()
-    n = counts[0, t_ref[0]]
+    before, after = sides(left_first(t_ref, core_ref), one_ref, two_ref)
     whole[...] = whole_ref[...]
-    whole[:, 0:C] += jnp.dot(after.T, u_ref[frame(n - 1), :], preferred_element_type=F32)
+    whole[:, 0:C] += jnp.dot(after.T, last_ref[...], preferred_element_type=F32)
     whole[:, 2 * C : 3 * C] += jnp.dot(before.T, u_ref[0:PIX, :], preferred_element_type=F32)
     for j in range(4):
         first = whole[:, j * LANES : (j + 1) * LANES]
@@ -216,7 +223,7 @@
     t_ref, core_ref, y_ref, g_ref, one_ref, two_ref, wt_ref, counts_hbm, dy_ref, ext, counts, sems
 ):
     (copy,) = start_all(sems, (counts_hbm, counts))
-    before, after = sides(core_ref[0], one_ref, two_ref)
+    before, after = sides(left_first(t_ref, core_ref), one_ref, two_ref)
     ext[0:PIX, :] = before
     ext[PIX : PIX + ROWS, :] = g_ref[...]
     ext[PIX + ROWS :, :] = after
@@ -310,12 +317,19 @@
         out_ref[i] = total
 
 
-def final_kernel(scale, both_ref, out_ref):
-    for j in range(8):
-        width = min(LANES, 3 * C - j * LANES)
-        rows = (j % 4) * C
-        part = both_ref[j // 4, rows : rows + C, :].astype(F32) * scale
-        out_ref[:, j * LANES : j * LANES + width] = part[:, :width]
+def final_kernel(scale, both_ref, out_hbm, whole, sems):
+    copies = []
+    for i, row in enumerate(range(0, C, C // 4)):
+        rows = pl.ds(row, C // 4)
+        for j in range(8):
+            width = min(LANES, 3 * C - j * LANES)
+            start = (j % 4) * C + row
+            part = both_ref[j // 4, start : start + C // 4, :].astype(F32) * scale
+            whole[rows, j * LANES : j * LANES + width] = part[:, :width]
+        copies.append(pltpu.make_async_copy(whole.at[rows, :], out_hbm.at[rows, :], sems.at[i]))
+        copies[-1].start()
+    for copy in copies:
+        copy.wait()
 
 
 SMEM_SPEC = pl.BlockSpec(memory_space=pltpu.SMEM)
@@ -323,13 +337,14 @@
 HBM_SPEC = pl.BlockSpec(memory_space=pltpu.HBM)
 
 
-def call(body, scalars, arrays, away, outs, scratch, cost):
+def call(body, scalars, arrays, away, outs, scratch, cost, out_away=False):
     away = [pltpu.with_memory_space_constraint(a, pltpu.HBM) for a in away]
+    out_spec = HBM_SPEC if out_away else VMEM_SPEC
     return pl.pallas_call(
         body,
         out_shape=outs,
         in_specs=[SMEM_SPEC] * len(scalars) + [VMEM_SPEC] * len(arrays) + [HBM_SPEC] * len(away),
-        out_specs=[VMEM_SPEC] * len(outs) if isinstance(outs, list) else VMEM_SPEC,
+        out_specs=[VMEM_SPEC] * len(outs) if isinstance(outs, list) else out_spec,
         scratch_shapes=scratch,
         compiler_params=PARAMS,
         cost_estimate=pl.CostEstimate(flops=cost[0], bytes_accessed=cost[1], transcendentals=0),
@@ -351,15 +366,15 @@
     return pltpu.SMEM(counts.shape, jnp.int32)
 
 
-def run_edge(place, core, counts, g, x):
+def run_edge(place, core, counts, g):
     return call(
         edge_kernel,
         (place, core),
         (),
-        (counts, g, x),
-        [ONE, ONE, ACT, ACT],
-        [counts_mem(counts), dma((3,))],
-        (0, 1_200_000),
+        (counts, g),
+        [ONE, ONE, ACT],
+        [counts_mem(counts), dma((4,))],
+        (0, 600_000),
     )
 
 
@@ -367,34 +382,30 @@
     return call(
         forward_kernel,
         (place,),
-        (x,),
-        (counts, gain, shift, wt_t, w_t),
-        [ACT, ACT, array((2, 8, C), F32), array(wt_t.shape, BF16)],
-        [counts_mem(counts), VECTOR, VECTOR, WEIGHTS, COLUMNS, STACKED, PRODUCT, dma((8,))],
+        (),
+        (counts, x, gain, shift, wt_t, w_t),
+        [
+            ACT, ACT, array((ROWS - PIX, C), BF16), array((PIX, C), BF16), array((2, 8, C), F32),
+            array(wt_t.shape, BF16), ACT,
+        ],
+        [counts_mem(counts), VECTOR, VECTOR, WEIGHTS, COLUMNS, STACKED, PRODUCT, dma((11,))],
         (2 * ROWS * 9 * C * C, 4_000_000),
     )
 
 
-def run_own(place, u, g_own, counts):
-    return call(
-        own_kernel,
-        (place,),
-        (u, g_own),
-        (counts,),
-        array((C, 8 * LANES), F32),
-        [counts_mem(counts), dma((1,))],
-        (2 * ROWS * 3 * C * C, 2_500_000),
-    )
-
-
-def run_grad(place, core, whole, u, one, two, counts):
+def run_own(u, inner, g_own):
+    out = array((C, 8 * LANES), F32)
+    return call(own_kernel, (), (u, inner, g_own), (), out, [], (2 * ROWS * 3 * C * C, 2_500_000))
+
+
+def run_grad(place, core, whole, u, last, one, two):
     return call(
         grad_kernel,
         (place, core),
-        (whole, u, one, two),
-        (counts,),
+        (whole, u, last, one, two),
+        (),
         [array((HALF, LANES), F32), array((HALF, LANES), BF16)],
-        [counts_mem(counts), VMEM((C, 8 * LANES), F32), dma((1,))],
+        [VMEM((C, 8 * LANES), F32)],
         (4 * PIX * C * C, 2_500_000),
     )
 
@@ -440,7 +451,10 @@
     def body(*refs):
         final_kernel(scale, *refs)
 
-    return call(body, (), (both,), (), array((C, 3 * C), F32), [], (1_000_000, 2_000_000))
+    whole = VMEM((C, 3 * C), F32)
+    out = array((C, 3 * C), F32)
+    cost = (1_000_000, 2_000_000)
+    return call(body, (), (both,), (), out, [whole, dma((4,))], cost, out_away=True)
 
 
 def shards(frames_in, cotangent, counts, norm_gain, norm_shift, spatial_weight, temporal_weight):
@@ -452,17 +466,20 @@
     w_t = spatial_weight.T
     wt_t = temporal_weight.T
     tm_size = lax.axis_size("tm")
-    right = [[(c * tm_size + t, c * tm_size + t + 1) for t in range(tm_size - 1)] for c in range(2)]
-    left = [[(b, a) for a, b in line] for line in right]
-
-    one, two, g_own, x_own = run_edge(place, core, counts, g, x)
-    one = lax.ppermute(one, ("c", "tm"), right[0] + left[1])
-    two = lax.ppermute(two, ("c", "tm"), left[0] + right[1])
-    y, u, stats, wt_own = run_forward(
-        place, counts, x_own, norm_gain, norm_shift, wt_t, w_t
-    )
-    whole = run_own(place, u, g_own, counts)
-    keep, send = run_grad(place, core, whole, u, one, two, counts)
+    pairs = [[], []]
+    for c in range(2):
+        for t in range(tm_size - 1):
+            here = c * tm_size + t
+            pairs[(t + c) % 2] += [(here, here + 1), (here + 1, here)]
+
+    one, two, g_own = run_edge(place, core, counts, g)
+    one = lax.ppermute(one, ("c", "tm"), pairs[0])
+    two = lax.ppermute(two, ("c", "tm"), pairs[1])
+    y, u, inner, last, stats, wt_own, x_own = run_forward(
+        place, counts, x, norm_gain, norm_shift, wt_t, w_t
+    )
+    whole = run_own(u, inner, g_own)
+    keep, send = run_grad(place, core, whole, u, last, one, two)
 
     near, far = groups()
     size = len(near[0])

time: 80.3 us -> 78.6 us (0.979)
  blocking collectives: 35.1 us -> 34.2 us
    all_gather x1, blocking collectives: 5.89 us -> 4.3 us  [shards(): lax.all_gather(send, 'c')]
    all_to_all x1, starting transfers between devices: 13.7 us -> 12.2 us  [exchange(): lax.all_to_all(parts, ('z', 'c', 'tm'), 0, 0, axis_index_groups=members,...]
    ppermute x2, starting transfers between devices: 5.87 us -> 7.07 us  [the longest x1 6.4 us: shards(): two = lax.ppermute(two, ('c', 'tm'), pairs[1])]
    all_to_all x2, blocking collectives: 23.8 us -> 24.7 us  [exchange(): lax.all_to_all(parts, ('z', 'c', 'tm'), 0, 0, axis_index_groups=members,...]
  transfers between devices with their start and end apart: 3 -> 3, of which waited for: 1 -> 1; matrix products, arithmetic and copies ran while one was open for 0% -> 0% of each run, Pallas kernels for 16% -> 17%
where the time goes in v5:
time: 78.6 us; the launch traced here: 78.2 us
  blocking collectives  34.2 us (44%)
  starting transfers between devices  19.3 us (25%)
  Pallas kernels  17.1 us (22%)
  waiting for transfers between devices  6.85 us (9%)
    all_to_all x2, blocking collectives, exchange(): lax.all_to_all(parts, ('z', 'c', 'tm'), 0, 0, axis_index_groups=members,...  24.7 us
    pallas_call x10, Pallas kernels, call(): pl.pallas_call(body, out_shape=outs, in_specs=[SMEM_SPEC] * len(scalars)...  17.1 us
    all_to_all x1, starting transfers between devices, exchange(): lax.all_to_all(parts, ('z', 'c', 'tm'), 0, 0, axis_index_groups=members,...  12.2 us
    all_to_all x1, waiting for transfers between devices, exchange(): lax.all_to_all(parts, ('z', 'c', 'tm'), 0, 0, axis_index_groups=members,...  6.85 us
    ppermute x1, starting transfers between devices, shards(): two = lax.ppermute(two, ('c', 'tm'), pairs[1])  6.4 us
    all_gather x1, blocking collectives, shards(): both = lax.all_gather(mine, 'c')  5.21 us
    all_gather x1, blocking collectives, shards(): lax.all_gather(send, 'c')  4.3 us
  transfers between devices with their start and end apart: 3, of which 1 were waited for; matrix products, arithmetic and copies ran while one was open for 0% of the time, Pallas kernels for 17%

profile of v5, /device:TPU:1, one launch (start us, length us, event | category | flops | bytes accessed | tf_op | source)
XLA Modules:
  0.0 78.2 jit_solution(8948576820132958899)
XLA Ops:
  0.6 1.3 %shard_map.87 = (bf16[640,128]{1,0:T(8,128)(2,1)S(1)}, bf16[640,128]{1,0:T(8,128)(2,1)S(1)}, bf16[768,320]{1,0:T(8,128)(2,1)S(1)}) custom-call(s32[1]{0:T(128)} %bitcast.1.t_ref, s32[1]{0:T(128)} %bitcast.core_ref, s32[1,32]{1,0:T(1,128)} %counts_hbm.7, bf16[768,320]{1,0:T(8,128)(2,1)} %bitcast.15), custom_call_target="tpu_custom_call" | custom-call | bytes 600000 | tf_op jit(solution)/shard_map/pallas_call | solution.py:343
  1.9 0.7 collective-permute-start
  2.6 6.4 %collective-permute-start.1 = (bf16[640,128]{1,0:T(8,128)(2,1)S(1)}, bf16[640,128]{1,0:T(8,128)(2,1)S(1)}, u32[]{:S(2)}, u32[]{:S(2)}) collective-permute-start(bf16[640,128]{1,0:T(8,128)(2,1)S(1)} %get-tuple-element.23), channel_id=1, source_target_pairs={{1,2},{2,1},{3,4},{4,3},{5,6},{6,5},{7,8},{8,7},{9,10},{10,9},{11,... | collective-permute-start | bytes 491528 | tf_op jit(solution)/shard_map/ppermute | solution.py:477
  9.0 4.9 %shard_map.86 = (bf16[768,320]{1,0:T(8,128)(2,1)S(1)}, bf16[768,320]{1,0:T(8,128)(2,1)S(1)}, bf16[512,320]{1,0:T(8,128)(2,1)S(1)}, bf16[256,320]{1,0:T(8,128)(2,...) custom-call(s32[1]{0:T(128)} %bitcast.1.t_ref, s32[1,32]{1,0:T(1,128)} %counts_hbm.7, ...), custom_call_target="tpu_custom_call" | custom-call | flops 1415577600 | bytes 4000000 | tf_op jit(solution)/shard_map/pallas_call | solution.py:343
  13.9 0.8 %shard_map.88.whole_ref = f32[320,1024]{1,0:T(8,128)S(1)} custom-call(bf16[768,320]{1,0:T(8,128)(2,1)S(1)} %get-tuple-element.18.u_ref, bf16[512,320]{1,0:T(8,128)(2,1)S(1)} %get-tuple-element.19.inner_ref, bf16[768,320]{1,0:T(8,128)(2,1)S(1)} %get-tuple-element.20.g_ref), custom_call_target="tpu_custom_call" | custom-call | flops 471859200 | bytes 2500000 | tf_op jit(solution)/shard_map/pallas_call | solution.py:343
  14.7 0.0 collective-permute-done.one_ref
  14.7 0.0 collective-permute-done.1.two_ref
  14.7 0.5 shard_map.89
  15.2 4.3 %all-gather = bf16[2560,128]{1,0:T(8,128)(2,1)S(1)} all-gather(bf16[1280,128]{1,0:T(8,128)(2,1)S(1)} %get-tuple-element.25), channel_id=2, replica_groups=mesh['z'=8,'c'=2,'tm'=32] {'c'}, dimensions={0}, use_global_device_ids=true | all-gather | bytes 983040 | tf_op jit(solution)/shard_map/all_gather | solution.py:486
  19.5 0.1 shard_map.90
  19.6 14.5 %all_to_all.15.refs_0_ = bf16[16,80,128]{2,1,0:T(8,128)(2,1)S(1)} all-to-all(bf16[16,80,128]{2,1,0:T(8,128)(2,1)S(1)} %bitcast.12), channel_id=1, replica_groups={{0,1,2,3,4,5,6,7,64,65,66,67,68,69,70,71},{8,9,10,11,12,13,14,15,72,73,..., dimensions={0} | all-to-all | bytes 655360 | tf_op jit(solution)/shard_map/all_to_all | solution.py:524
  34.1 0.8 shard_map.91
  34.9 12.2 %all-to-all-start.1 = ((bf16[16,80,128]{2,1,0:T(8,128)(2,1)}), bf16[16,80,128]{2,1,0:T(8,128)(2,1)S(1)}, u32[]{:S(2)}, u32[]{:S(2)}) async-start(bf16[16,80,128]{2,1,0:T(8,128)(2,1)} %shard_map.91), calls=%async_computation.1 | async-start | bytes 655360 | tf_op jit(solution)/shard_map/all_to_all | solution.py:524
  47.1 2.2 %shard_map.92.dy_ref = bf16[768,320]{1,0:T(8,128)(2,1)S(1)} custom-call(s32[1]{0:T(128)} %bitcast.1.t_ref, s32[1]{0:T(128)} %bitcast.core_ref, bf16[768,320]{1,0:T(8,128)(2,1)S(1)} %get-tuple-element.27.y_ref, bf16[768,320]{1,0:T(8,128)(2,1)S(1)} %get-tuple-element.20.g_ref, bf16[640,128]{1,0:T(8,128)(2,1)S(1)} %collective-permute-done.one_ref, ...), custom_call_target="tpu_custom_call" | custom-call | flops 471859200 | bytes 2500000 | tf_op jit(solution)/shard_map/pallas_call | solution.py:343
  49.3 5.5 %shard_map.93 = bf16[768,320]{1,0:T(8,128)(2,1)} custom-call(s32[1]{0:T(128)} %bitcast.1.t_ref, bf16[768,320]{1,0:T(8,128)(2,1)S(1)} %shard_map.92.dy_ref, f32[2,8,320]{2,1,0:T(8,128)S(1)} %get-tuple-element.30.stats_ref, bf16[768,320]{1,0:T(8,128)(2,1)S(1)} %get-tuple-element.31.x_ref, s32[1,32]{1,0:T(1,128)} %counts_hbm.7, f32[320]{0:T(512)} %gain_hbm.3, ...), custom_call_target="tpu_custom_call" | custom-call | flops 1415577600 | bytes 4000000 | tf_op jit(solution)/shard_map/pallas_call | solution.py:343
  54.8 6.8 %all-to-all-done.1.refs_0_ = bf16[16,80,128]{2,1,0:T(8,128)(2,1)S(1)} async-done(((bf16[16,80,128]{2,1,0:T(8,128)(2,1)}), bf16[16,80,128]{2,1,0:T(8,128)(2,1)S(1)}, u32[]{:S(2)}, u32[]{:S(2)}) %all-to-all-start.1) | async-done | bytes 327712 | tf_op jit(solution)/shard_map/all_to_all | solution.py:524
  61.6 0.1 shard_map.94
  61.7 10.2 %all_to_all.16 = bf16[16,80,128]{2,1,0:T(8,128)(2,1)S(1)} all-to-all(bf16[16,80,128]{2,1,0:T(8,128)(2,1)S(1)} %shard_map.94), channel_id=1, replica_groups={{0,1,2,3,4,5,6,7,64,65,66,67,68,69,70,71},{8,9,10,11,12,13,14,15,72,73,..., dimensions={0} | all-to-all | bytes 655360 | tf_op jit(solution)/shard_map/all_to_all | solution.py:524
  71.9 5.2 %all_gather.11.refs_0_ = bf16[2,1280,128]{2,1,0:T(8,128)(2,1)S(1)} all-gather(bf16[1,1280,128]{2,1,0:T(8,128)(2,1)S(1)} %bitcast.14), channel_id=1, replica_groups=mesh['z'=8,'c'=2,'tm'=32] {'c'}, dimensions={0}, use_global_device_ids=true | all-gather | bytes 983040 | tf_op jit(solution)/shard_map/all_gather | solution.py:494
  77.1 1.1 %shard_map.95 = f32[320,960]{1,0:T(8,128)} custom-call(bf16[2,1280,128]{2,1,0:T(8,128)(2,1)S(1)} %all_gather.11.refs_0_), custom_call_target="tpu_custom_call" | custom-call | flops 1000000 | bytes 2000000 | tf_op jit(solution)/shard_map/pallas_call | solution.py:343
Async XLA Ops:
  1.9 12.8 %collective-permute-start = (bf16[640,128]{1,0:T(8,128)(2,1)S(1)}, bf16[640,128]{1,0:T(8,128)(2,1)S(1)}, u32[]{:S(2)}, u32[]{:S(2)}) collective-permute-start(bf16[640,128]{1,0:T(8,128)(2,1)S(1)} %get-tuple-element.22), channel_id=1, source_target_pairs={{0,1},{1,0},{2,3},{3,2},{4,5},{5,4},{6,7},{7,6},{8,9},{9,8},{10,11... | collective-permute-start | bytes 491528 | tf_op jit(solution)/shard_map/ppermute | solution.py:476
  2.6 12.1 %collective-permute-start.1 = (bf16[640,128]{1,0:T(8,128)(2,1)S(1)}, bf16[640,128]{1,0:T(8,128)(2,1)S(1)}, u32[]{:S(2)}, u32[]{:S(2)}) collective-permute-start(bf16[640,128]{1,0:T(8,128)(2,1)S(1)} %get-tuple-element.23), channel_id=1, source_target_pairs={{1,2},{2,1},{3,4},{4,3},{5,6},{6,5},{7,8},{8,7},{9,10},{10,9},{11,... | collective-permute-start | bytes 491528 | tf_op jit(solution)/shard_map/ppermute | solution.py:477
  34.9 26.7 %all-to-all-start.1 = ((bf16[16,80,128]{2,1,0:T(8,128)(2,1)}), bf16[16,80,128]{2,1,0:T(8,128)(2,1)S(1)}, u32[]{:S(2)}, u32[]{:S(2)}) async-start(bf16[16,80,128]{2,1,0:T(8,128)(2,1)} %shard_map.91), calls=%async_computation.1 | async-start | bytes 655360 | tf_op jit(solution)/shard_map/all_to_all | solution.py:524

commit v6 on v5

--- a/solution.py
+++ b/solution.py
@@ -107,8 +107,8 @@
 
 
 def forward_kernel(
-    t_ref, counts_hbm, x_hbm, gain_hbm, shift_hbm, wt_hbm, w_hbm, y_ref, u_ref, inner_ref, last_ref,
-    stats_ref, wt_ref, x_ref, counts, gain_ref, shift_ref, w_ref, cols, wst, prod, sems,
+    t_ref, g_ref, counts_hbm, x_hbm, gain_hbm, shift_hbm, wt_hbm, w_hbm, y_ref, u_ref, whole_ref,
+    last_ref, stats_ref, wt_ref, x_ref, inner, flipped, counts, gain_ref, shift_ref, w_ref, cols, wst, prod, sems,
 ):
     weights = [(w_hbm.at[pl.ds(q, 80), :], w_ref.at[pl.ds(q, 80), :]) for q in range(0, C, 80)]
     frames = [(x_hbm.at[frame(s), :], x_ref.at[frame(s), :]) for s in range(CAP)]
@@ -127,6 +127,9 @@
     def per_frame(fn):
         return jnp.concatenate([fn(s) for s in range(CAP)] + [blank], axis=0)
 
+    flipped[...] = g_ref[...].T
+    edge = 3 * C - 3 * C % LANES
+    whole_ref[:, edge:] = jnp.zeros((C, 8 * LANES - edge), F32)
     for copy in copies[:CAP]:
         copy.wait()
 
@@ -178,24 +181,19 @@
         units = (yf * sigmoid(yf)).astype(BF16)
         u_ref[rows, :] = jnp.where(jnp.int32(s) < n, units, zero)
         if s < CAP - 1:
-            inner_ref[rows, :] = jnp.where(jnp.int32(s + 1) < n, units, zero)
+            inner[rows, :] = jnp.where(jnp.int32(s + 1) < n, units, zero)
 
     for s in range(CAP):
         add(s)
     last_ref[...] = u_ref[frame(n - 1), :]
-    copies[-1].wait()
-
-
-def own_kernel(u_ref, inner_ref, g_ref, whole_ref):
-    flipped = g_ref[...].T
-    whole_ref[:, 3 * C - 3 * C % LANES :] = jnp.zeros((C, 8 * LANES - 3 * C + 3 * C % LANES), F32)
 
     def term(own, taken):
         return jnp.dot(own, taken, preferred_element_type=F32)
 
-    whole_ref[:, 0:C] = term(flipped[:, PIX:], inner_ref[...])
-    whole_ref[:, C : 2 * C] = term(flipped, u_ref[...])
+    whole_ref[:, 0:C] = term(flipped[:, PIX:], inner[...])
+    whole_ref[:, C : 2 * C] = term(flipped[...], u_ref[...])
     whole_ref[:, 2 * C : 3 * C] = term(flipped[:, 0 : ROWS - PIX], u_ref[PIX:, :])
+    copies[-1].wait()
 
 
 def sides(turn, one_ref, two_ref):
@@ -219,16 +217,25 @@
         send_ref[j * C : (j + 1) * C, :] = jnp.where(core == 0, second, first).astype(BF16)
 
 
-def temporal_kernel(
-    t_ref, core_ref, y_ref, g_ref, one_ref, two_ref, wt_ref, counts_hbm, dy_ref, ext, counts, sems
+def backward_kernel(
+    t_ref, core_ref, y_ref, g_ref, one_ref, two_ref, wt_ref, stats_ref, x_ref, counts_hbm, gain_hbm,
+    shift_hbm, w_hbm, out_ref, ext, dys, counts, gain_ref, shift_ref, w_ref, cols, wst, prod, sems,
 ):
-    (copy,) = start_all(sems, (counts_hbm, counts))
+    weights = [(w_hbm.at[pl.ds(q, 80), :], w_ref.at[pl.ds(q, 80), :]) for q in range(0, C, 80)]
+    copies = start_all(
+        sems,
+        (counts_hbm, counts),
+        *weights,
+        (gain_hbm, gain_ref),
+        (shift_hbm, shift_ref),
+    )
     before, after = sides(left_first(t_ref, core_ref), one_ref, two_ref)
     ext[0:PIX, :] = before
     ext[PIX : PIX + ROWS, :] = g_ref[...]
     ext[PIX + ROWS :, :] = after
-    copy.wait()
-    ext[frame(counts[0, t_ref[0]] + 1), :] = after
+    copies[0].wait()
+    n = counts[0, t_ref[0]]
+    ext[frame(n + 1), :] = after
     for s in range(CAP):
         back = jnp.zeros((PIX, C), F32)
         for k in range(3):
@@ -240,32 +247,13 @@
         yf = y_ref[frame(s), :].astype(F32)
         sig = sigmoid(yf)
         back = (sig * (1.0 + yf * (1.0 - sig)) * back).astype(BF16)
-        dy_ref[frame(s), :] = (g_ref[frame(s), :].astype(F32) + back.astype(F32)).astype(BF16)
-
-
-def spatial_kernel(
-    t_ref, dy_ref, stats_ref, x_ref, counts_hbm, gain_hbm, shift_hbm, w_hbm, out_ref,
-    counts, gain_ref, shift_ref, w_ref, cols, wst, prod, sems,
-):
-    weights = [(w_hbm.at[pl.ds(q, 80), :], w_ref.at[pl.ds(q, 80), :]) for q in range(0, C, 80)]
-    copies = start_all(
-        sems,
-        *weights,
-        (gain_hbm, gain_ref),
-        (shift_hbm, shift_ref),
-        (counts_hbm, counts),
-    )
-
-    def spread(s):
-        dy = dy_ref[frame(s), :]
+        dy = (g_ref[frame(s), :].astype(F32) + back.astype(F32)).astype(BF16)
+        dys[frame(s), :] = dy
         dyf = dy.astype(F32)
         cols[frame(s), 0:C] = shifted(dyf, 1).astype(BF16)
         cols[frame(s), C : 2 * C] = dy
         cols[frame(s), 2 * C : 3 * C] = shifted(dyf, -1).astype(BF16)
-
-    for s in range(CAP):
-        spread(s)
-    for copy in copies:
+    for copy in copies[1:]:
         copy.wait()
     for i in range(3):
         for j in range(3):
@@ -273,7 +261,6 @@
             wst[j * C : (j + 1) * C, i * C : (i + 1) * C] = w_ref[:, tap * C : (tap + 1) * C]
     prod[...] = jnp.dot(cols[...], wst[...], preferred_element_type=F32)
     matrix = group_matrix()
-    n = counts[0, t_ref[0]]
     gain = gain_ref[...].reshape(1, C)
     shift = shift_ref[...].reshape(1, C)
 
@@ -296,7 +283,7 @@
         )
         means = group_mean(sums, matrix)
         dx = inv * (dn - means[0:1] - normed * means[1:2])
-        total = dy_ref[rows, :].astype(F32) + dx
+        total = dys[rows, :].astype(F32) + dx
         out_ref[rows, :] = jnp.where(jnp.int32(s) < n, total, 0.0).astype(BF16)
 
     for s in range(CAP):
@@ -378,24 +365,22 @@
     )
 
 
-def run_forward(place, counts, x, gain, shift, wt_t, w_t):
+def run_forward(place, g_own, counts, x, gain, shift, wt_t, w_t):
     return call(
         forward_kernel,
         (place,),
-        (),
+        (g_own,),
         (counts, x, gain, shift, wt_t, w_t),
         [
-            ACT, ACT, array((ROWS - PIX, C), BF16), array((PIX, C), BF16), array((2, 8, C), F32),
+            ACT, ACT, array((C, 8 * LANES), F32), array((PIX, C), BF16), array((2, 8, C), F32),
             array(wt_t.shape, BF16), ACT,
         ],
-        [counts_mem(counts), VECTOR, VECTOR, WEIGHTS, COLUMNS, STACKED, PRODUCT, dma((11,))],
-        (2 * ROWS * 9 * C * C, 4_000_000),
-    )
-
-
-def run_own(u, inner, g_own):
-    out = array((C, 8 * LANES), F32)
-    return call(own_kernel, (), (u, inner, g_own), (), out, [], (2 * ROWS * 3 * C * C, 2_500_000))
+        [
+            VMEM((ROWS - PIX, C), BF16), VMEM((C, ROWS), BF16), counts_mem(counts), VECTOR, VECTOR,
+            WEIGHTS, COLUMNS, STACKED, PRODUCT, dma((11,)),
+        ],
+        (2 * ROWS * 12 * C * C, 4_000_000),
+    )
 
 
 def run_grad(place, core, whole, u, last, one, two):
@@ -410,27 +395,18 @@
     )
 
 
-def run_temporal(place, core, y, g_own, one, two, wt_own, counts):
+def run_backward(place, core, y, g_own, one, two, wt_own, stats, x_own, counts, gain, shift, w_t):
     return call(
-        temporal_kernel,
+        backward_kernel,
         (place, core),
-        (y, g_own, one, two, wt_own),
-        (counts,),
-        ACT,
-        [VMEM((5 * PIX, C), BF16), counts_mem(counts), dma((1,))],
-        (2 * ROWS * 3 * C * C, 2_500_000),
-    )
-
-
-def run_spatial(place, dy, stats, x, counts, gain, shift, w_t):
-    return call(
-        spatial_kernel,
-        (place,),
-        (dy, stats, x),
+        (y, g_own, one, two, wt_own, stats, x_own),
         (counts, gain, shift, w_t),
         ACT,
-        [counts_mem(counts), VECTOR, VECTOR, WEIGHTS, COLUMNS, STACKED, PRODUCT, dma((7,))],
-        (2 * ROWS * 9 * C * C, 4_000_000),
+        [
+            VMEM((5 * PIX, C), BF16), VMEM((ROWS, C), BF16), counts_mem(counts), VECTOR, VECTOR,
+            WEIGHTS, COLUMNS, STACKED, PRODUCT, dma((7,)),
+        ],
+        (2 * ROWS * 12 * C * C, 4_000_000),
     )
 
 
@@ -475,10 +451,9 @@
     one, two, g_own = run_edge(place, core, counts, g)
     one = lax.ppermute(one, ("c", "tm"), pairs[0])
     two = lax.ppermute(two, ("c", "tm"), pairs[1])
-    y, u, inner, last, stats, wt_own, x_own = run_forward(
-        place, counts, x, norm_gain, norm_shift, wt_t, w_t
-    )
-    whole = run_own(u, inner, g_own)
+    y, u, whole, last, stats, wt_own, x_own = run_forward(
+        place, g_own, counts, x, norm_gain, norm_shift, wt_t, w_t
+    )
     keep, send = run_grad(place, core, whole, u, last, one, two)
 
     near, far = groups()
@@ -486,8 +461,9 @@
     part = run_add(core, keep, lax.all_gather(send, "c")).reshape(size, HALF // size, LANES)
     part = run_sum(exchange(part, near), len(far[0]))
     part, one = lax.optimization_barrier((part, one))
-    dy = run_temporal(place, core, y, g_own, one, two, wt_own, counts)
-    d_in = run_spatial(place, dy, stats, x_own, counts, norm_gain, norm_shift, w_t)
+    d_in = run_backward(
+        place, core, y, g_own, one, two, wt_own, stats, x_own, counts, norm_gain, norm_shift, w_t
+    )
     part, d_in = lax.optimization_barrier((exchange(part, far), d_in))
     part = run_sum(part, size)
     mine = exchange(part, near).reshape(HALF, LANES)
@@ -504,14 +480,23 @@
     def at(z, c, y, x):
         return ((z * 2 + c) * ys + y) * xs + x
 
+    def kind(i):
+        return bin(i).count("1") % 2
+
+    def pair(i):
+        return sorted((i, i + 1), key=kind)
+
+    def alike(i, size):
+        return [p for p in range(size) if kind(p) == i]
+
     near = [
-        [at(z + i, c, y + j, x) for i in range(2) for j in range(2) for x in range(xs)]
+        [at(zz, c, yy, x) for zz in pair(z) for yy in pair(y) for x in range(xs)]
         for z in range(0, zs, 2)
         for c in range(2)
         for y in range(0, ys, 2)
     ]
     far = [
-        [at(z, c, y, x) for z in range(i, zs, 2) for y in range(j, ys, 2)]
+        [at(z, c, y, x) for z in alike(i, zs) for y in alike(j, ys)]
         for i in range(2)
         for j in range(2)
         for c in range(2)

time: 78.6 us -> 78 us (level)
  Pallas kernels: 17.1 us -> 15.7 us
    all_to_all x2, blocking collectives: 24.7 us -> 26.2 us  [exchange(): lax.all_to_all(parts, ('z', 'c', 'tm'), 0, 0, axis_index_groups=members,...]
    pallas_call x10 -> x8, Pallas kernels: 17.1 us -> 15.7 us  [call(): pl.pallas_call(body, out_shape=outs, in_specs=[SMEM_SPEC] * len(scalars)...]
  transfers between devices with their start and end apart: 3 -> 3, of which waited for: 1 -> 1; matrix products, arithmetic and copies ran while one was open for 0% -> 0% of each run, Pallas kernels for 17% -> 15%
where the time goes in v6:
time: 78 us; the launch traced here: 77.6 us
  blocking collectives  34.9 us (45%)
  starting transfers between devices  19.4 us (25%)
  Pallas kernels  15.7 us (20%)
  waiting for transfers between devices  6.82 us (9%)
    all_to_all x2, blocking collectives, exchange(): lax.all_to_all(parts, ('z', 'c', 'tm'), 0, 0, axis_index_groups=members,...  26.2 us
    pallas_call x8, Pallas kernels, call(): pl.pallas_call(body, out_shape=outs, in_specs=[SMEM_SPEC] * len(scalars)...  15.7 us
    all_to_all x1, starting transfers between devices, exchange(): lax.all_to_all(parts, ('z', 'c', 'tm'), 0, 0, axis_index_groups=members,...  12.3 us
    all_to_all x1, waiting for transfers between devices, exchange(): lax.all_to_all(parts, ('z', 'c', 'tm'), 0, 0, axis_index_groups=members,...  6.82 us
    ppermute x1, starting transfers between devices, shards(): two = lax.ppermute(two, ('c', 'tm'), pairs[1])  6.4 us
    all_gather x1, blocking collectives, shards(): both = lax.all_gather(mine, 'c')  4.42 us
    all_gather x1, blocking collectives, shards(): lax.all_gather(send, 'c')  4.29 us
  transfers between devices with their start and end apart: 3, of which 1 were waited for; matrix products, arithmetic and copies ran while one was open for 0% of the time, Pallas kernels for 15%

profile of v6, /device:TPU:1, one launch (start us, length us, event | category | flops | bytes accessed | tf_op | source)
XLA Modules:
  0.0 77.6 jit_solution(5824985010955048239)
XLA Ops:
  0.6 1.3 %shard_map.86 = (bf16[640,128]{1,0:T(8,128)(2,1)S(1)}, bf16[640,128]{1,0:T(8,128)(2,1)S(1)}, bf16[768,320]{1,0:T(8,128)(2,1)S(1)}) custom-call(s32[1]{0:T(128)} %bitcast.1.t_ref, s32[1]{0:T(128)} %bitcast.core_ref, s32[1,32]{1,0:T(1,128)} %counts_hbm.5, bf16[768,320]{1,0:T(8,128)(2,1)} %bitcast.15), custom_call_target="tpu_custom_call" | custom-call | bytes 600000 | tf_op jit(solution)/shard_map/pallas_call | solution.py:330
  1.9 0.7 collective-permute-start
  2.6 6.4 %collective-permute-start.1 = (bf16[640,128]{1,0:T(8,128)(2,1)S(1)}, bf16[640,128]{1,0:T(8,128)(2,1)S(1)}, u32[]{:S(2)}, u32[]{:S(2)}) collective-permute-start(bf16[640,128]{1,0:T(8,128)(2,1)S(1)} %get-tuple-element.23), channel_id=1, source_target_pairs={{1,2},{2,1},{3,4},{4,3},{5,6},{6,5},{7,8},{8,7},{9,10},{10,9},{11,... | collective-permute-start | bytes 491528 | tf_op jit(solution)/shard_map/ppermute | solution.py:453
  9.0 5.5 %shard_map.87 = (bf16[768,320]{1,0:T(8,128)(2,1)S(1)}, bf16[768,320]{1,0:T(8,128)(2,1)S(1)}, f32[320,1024]{1,0:T(8,128)S(1)}, bf16[256,320]{1,0:T(8,128)(2,1)S(1...) custom-call(s32[1]{0:T(128)} %bitcast.1.t_ref, ...), custom_call_target="tpu_custom_call" | custom-call | flops 1887436800 | bytes 4000000 | tf_op jit(solution)/shard_map/pallas_call | solution.py:330
  14.5 0.0 collective-permute-done.one_ref
  14.5 0.0 collective-permute-done.1.two_ref
  14.5 0.5 shard_map.88
  15.0 4.3 %all-gather = bf16[2560,128]{1,0:T(8,128)(2,1)S(1)} all-gather(bf16[1280,128]{1,0:T(8,128)(2,1)S(1)} %get-tuple-element.25), channel_id=2, replica_groups=mesh['z'=8,'c'=2,'tm'=32] {'c'}, dimensions={0}, use_global_device_ids=true | all-gather | bytes 983040 | tf_op jit(solution)/shard_map/all_gather | solution.py:461
  19.3 0.1 shard_map.89
  19.4 14.5 %all_to_all.15.refs_0_ = bf16[16,80,128]{2,1,0:T(8,128)(2,1)S(1)} all-to-all(bf16[16,80,128]{2,1,0:T(8,128)(2,1)S(1)} %bitcast.12), channel_id=1, replica_groups={{0,1,2,3,4,5,6,7,64,65,66,67,68,69,70,71},{12,13,14,15,8,9,10,11,76,77,..., dimensions={0} | all-to-all | bytes 655360 | tf_op jit(solution)/shard_map/all_to_all | solution.py:509
  33.9 0.8 shard_map.90
  34.7 12.3 %all-to-all-start.1 = ((bf16[16,80,128]{2,1,0:T(8,128)(2,1)}), bf16[16,80,128]{2,1,0:T(8,128)(2,1)S(1)}, u32[]{:S(2)}, u32[]{:S(2)}) async-start(bf16[16,80,128]{2,1,0:T(8,128)(2,1)} %shard_map.90), calls=%async_computation.1 | async-start | bytes 655360 | tf_op jit(solution)/shard_map/all_to_all | solution.py:509
  47.1 6.4 %shard_map.91 = bf16[768,320]{1,0:T(8,128)(2,1)} custom-call(s32[1]{0:T(128)} %bitcast.1.t_ref, s32[1]{0:T(128)} %bitcast.core_ref, bf16[768,320]{1,0:T(8,128)(2,1)S(1)} %get-tuple-element.27.y_ref, bf16[768,320]{1,0:T(8,128)(2,1)S(1)} %get-tuple-element.18.g_ref, bf16[640,128]{1,0:T(8,128)(2,1)S(1)} %collective-permute-done.one_ref, ...), custom_call_target="tpu_custom_call" | custom-call | flops 1887436800 | bytes 4000000 | tf_op jit(solution)/shard_map/pallas_call | solution.py:330
  53.5 6.8 %all-to-all-done.1.refs_0_ = bf16[16,80,128]{2,1,0:T(8,128)(2,1)S(1)} async-done(((bf16[16,80,128]{2,1,0:T(8,128)(2,1)}), bf16[16,80,128]{2,1,0:T(8,128)(2,1)S(1)}, u32[]{:S(2)}, u32[]{:S(2)}) %all-to-all-start.1) | async-done | bytes 327712 | tf_op jit(solution)/shard_map/all_to_all | solution.py:509
  60.3 0.1 shard_map.92
  60.4 11.7 %all_to_all.16 = bf16[16,80,128]{2,1,0:T(8,128)(2,1)S(1)} all-to-all(bf16[16,80,128]{2,1,0:T(8,128)(2,1)S(1)} %shard_map.92), channel_id=1, replica_groups={{0,1,2,3,4,5,6,7,64,65,66,67,68,69,70,71},{12,13,14,15,8,9,10,11,76,77,..., dimensions={0} | all-to-all | bytes 655360 | tf_op jit(solution)/shard_map/all_to_all | solution.py:509
  72.1 4.4 %all_gather.11.refs_0_ = bf16[2,1280,128]{2,1,0:T(8,128)(2,1)S(1)} all-gather(bf16[1,1280,128]{2,1,0:T(8,128)(2,1)S(1)} %bitcast.14), channel_id=1, replica_groups=mesh['z'=8,'c'=2,'tm'=32] {'c'}, dimensions={0}, use_global_device_ids=true | all-gather | bytes 983040 | tf_op jit(solution)/shard_map/all_gather | solution.py:470
  76.5 1.1 %shard_map.93 = f32[320,960]{1,0:T(8,128)} custom-call(bf16[2,1280,128]{2,1,0:T(8,128)(2,1)S(1)} %all_gather.11.refs_0_), custom_call_target="tpu_custom_call" | custom-call | flops 1000000 | bytes 2000000 | tf_op jit(solution)/shard_map/pallas_call | solution.py:330
Async XLA Ops:
  1.9 12.6 %collective-permute-start = (bf16[640,128]{1,0:T(8,128)(2,1)S(1)}, bf16[640,128]{1,0:T(8,128)(2,1)S(1)}, u32[]{:S(2)}, u32[]{:S(2)}) collective-permute-start(bf16[640,128]{1,0:T(8,128)(2,1)S(1)} %get-tuple-element.22), channel_id=1, source_target_pairs={{0,1},{1,0},{2,3},{3,2},{4,5},{5,4},{6,7},{7,6},{8,9},{9,8},{10,11... | collective-permute-start | bytes 491528 | tf_op jit(solution)/shard_map/ppermute | solution.py:452
  2.6 11.9 %collective-permute-start.1 = (bf16[640,128]{1,0:T(8,128)(2,1)S(1)}, bf16[640,128]{1,0:T(8,128)(2,1)S(1)}, u32[]{:S(2)}, u32[]{:S(2)}) collective-permute-start(bf16[640,128]{1,0:T(8,128)(2,1)S(1)} %get-tuple-element.23), channel_id=1, source_target_pairs={{1,2},{2,1},{3,4},{4,3},{5,6},{6,5},{7,8},{8,7},{9,10},{10,9},{11,... | collective-permute-start | bytes 491528 | tf_op jit(solution)/shard_map/ppermute | solution.py:453
  34.7 25.6 %all-to-all-start.1 = ((bf16[16,80,128]{2,1,0:T(8,128)(2,1)}), bf16[16,80,128]{2,1,0:T(8,128)(2,1)S(1)}, u32[]{:S(2)}, u32[]{:S(2)}) async-start(bf16[16,80,128]{2,1,0:T(8,128)(2,1)} %shard_map.90), calls=%async_computation.1 | async-start | bytes 655360 | tf_op jit(solution)/shard_map/all_to_all | solution.py:509

commit v7 on v6

--- a/solution.py
+++ b/solution.py
@@ -490,7 +490,7 @@
         return [p for p in range(size) if kind(p) == i]
 
     near = [
-        [at(zz, c, yy, x) for zz in pair(z) for yy in pair(y) for x in range(xs)]
+        [at(zz, c, yy, x ^ (x >> 1)) for x in range(xs) for zz in pair(z) for yy in pair(y)]
         for z in range(0, zs, 2)
         for c in range(2)
         for y in range(0, ys, 2)

time: 78 us -> 76.1 us (0.976)
  blocking collectives: 34.9 us -> 33.9 us
  waiting for transfers between devices: 6.82 us -> 5.99 us
    all_to_all x2, blocking collectives: 26.2 us -> 24.5 us  [exchange(): lax.all_to_all(parts, ('z', 'c', 'tm'), 0, 0, axis_index_groups=members,...]
    all_to_all x1, waiting for transfers between devices: 6.82 us -> 5.99 us  [exchange(): lax.all_to_all(parts, ('z', 'c', 'tm'), 0, 0, axis_index_groups=members,...]
  transfers between devices with their start and end apart: 3 -> 3, of which waited for: 1 -> 1; matrix products, arithmetic and copies ran while one was open for 0% -> 0% of each run, Pallas kernels for 15% -> 16%
where the time goes in v7:
time: 76.1 us; the launch traced here: 75.7 us
  blocking collectives  33.9 us (45%)
  starting transfers between devices  19.4 us (25%)
  Pallas kernels  15.7 us (21%)
  waiting for transfers between devices  5.99 us (8%)
    all_to_all x2, blocking collectives, exchange(): lax.all_to_all(parts, ('z', 'c', 'tm'), 0, 0, axis_index_groups=members,...  24.5 us
    pallas_call x8, Pallas kernels, call(): pl.pallas_call(body, out_shape=outs, in_specs=[SMEM_SPEC] * len(scalars)...  15.7 us
    all_to_all x1, starting transfers between devices, exchange(): lax.all_to_all(parts, ('z', 'c', 'tm'), 0, 0, axis_index_groups=members,...  12.3 us
    ppermute x1, starting transfers between devices, shards(): two = lax.ppermute(two, ('c', 'tm'), pairs[1])  6.4 us
    all_to_all x1, waiting for transfers between devices, exchange(): lax.all_to_all(parts, ('z', 'c', 'tm'), 0, 0, axis_index_groups=members,...  5.99 us
    all_gather x1, blocking collectives, shards(): both = lax.all_gather(mine, 'c')  5.07 us
    all_gather x1, blocking collectives, shards(): lax.all_gather(send, 'c')  4.29 us
  transfers between devices with their start and end apart: 3, of which 1 were waited for; matrix products, arithmetic and copies ran while one was open for 0% of the time, Pallas kernels for 16%

profile of v7, /device:TPU:1, one launch (start us, length us, event | category | flops | bytes accessed | tf_op | source)
XLA Modules:
  0.0 75.7 jit_solution(6488378645610353992)
XLA Ops:
  0.6 1.3 %shard_map.86 = (bf16[640,128]{1,0:T(8,128)(2,1)S(1)}, bf16[640,128]{1,0:T(8,128)(2,1)S(1)}, bf16[768,320]{1,0:T(8,128)(2,1)S(1)}) custom-call(s32[1]{0:T(128)} %bitcast.1.t_ref, s32[1]{0:T(128)} %bitcast.core_ref, s32[1,32]{1,0:T(1,128)} %counts_hbm.5, bf16[768,320]{1,0:T(8,128)(2,1)} %bitcast.15), custom_call_target="tpu_custom_call" | custom-call | bytes 600000 | tf_op jit(solution)/shard_map/pallas_call | solution.py:330
  1.9 0.7 collective-permute-start
  2.6 6.4 %collective-permute-start.1 = (bf16[640,128]{1,0:T(8,128)(2,1)S(1)}, bf16[640,128]{1,0:T(8,128)(2,1)S(1)}, u32[]{:S(2)}, u32[]{:S(2)}) collective-permute-start(bf16[640,128]{1,0:T(8,128)(2,1)S(1)} %get-tuple-element.23), channel_id=1, source_target_pairs={{1,2},{2,1},{3,4},{4,3},{5,6},{6,5},{7,8},{8,7},{9,10},{10,9},{11,... | collective-permute-start | bytes 491528 | tf_op jit(solution)/shard_map/ppermute | solution.py:453
  9.0 5.5 %shard_map.87 = (bf16[768,320]{1,0:T(8,128)(2,1)S(1)}, bf16[768,320]{1,0:T(8,128)(2,1)S(1)}, f32[320,1024]{1,0:T(8,128)S(1)}, bf16[256,320]{1,0:T(8,128)(2,1)S(1...) custom-call(s32[1]{0:T(128)} %bitcast.1.t_ref, ...), custom_call_target="tpu_custom_call" | custom-call | flops 1887436800 | bytes 4000000 | tf_op jit(solution)/shard_map/pallas_call | solution.py:330
  14.5 0.0 collective-permute-done.one_ref
  14.5 0.0 collective-permute-done.1.two_ref
  14.5 0.5 shard_map.88
  15.0 4.3 %all-gather = bf16[2560,128]{1,0:T(8,128)(2,1)S(1)} all-gather(bf16[1280,128]{1,0:T(8,128)(2,1)S(1)} %get-tuple-element.25), channel_id=2, replica_groups=mesh['z'=8,'c'=2,'tm'=32] {'c'}, dimensions={0}, use_global_device_ids=true | all-gather | bytes 983040 | tf_op jit(solution)/shard_map/all_gather | solution.py:461
  19.3 0.1 shard_map.89
  19.4 12.8 %all_to_all.15.refs_0_ = bf16[16,80,128]{2,1,0:T(8,128)(2,1)S(1)} all-to-all(bf16[16,80,128]{2,1,0:T(8,128)(2,1)S(1)} %bitcast.12), channel_id=1, replica_groups={{0,4,64,68,1,5,65,69,3,7,67,71,2,6,66,70},{12,8,76,72,13,9,77,73,15,11,..., dimensions={0} | all-to-all | bytes 655360 | tf_op jit(solution)/shard_map/all_to_all | solution.py:509
  32.2 0.8 %shard_map.90 = bf16[16,80,128]{2,1,0:T(8,128)(2,1)} custom-call(bf16[16,80,128]{2,1,0:T(8,128)(2,1)S(1)} %all_to_all.15.refs_0_), custom_call_target="tpu_custom_call" | custom-call | flops 163840 | bytes 327680 | tf_op jit(solution)/shard_map/pallas_call | solution.py:330
  33.0 12.3 %all-to-all-start.1 = ((bf16[16,80,128]{2,1,0:T(8,128)(2,1)}), bf16[16,80,128]{2,1,0:T(8,128)(2,1)S(1)}, u32[]{:S(2)}, u32[]{:S(2)}) async-start(bf16[16,80,128]{2,1,0:T(8,128)(2,1)} %shard_map.90), calls=%async_computation.1 | async-start | bytes 655360 | tf_op jit(solution)/shard_map/all_to_all | solution.py:509
  45.3 6.4 %shard_map.91 = bf16[768,320]{1,0:T(8,128)(2,1)} custom-call(s32[1]{0:T(128)} %bitcast.1.t_ref, s32[1]{0:T(128)} %bitcast.core_ref, bf16[768,320]{1,0:T(8,128)(2,1)S(1)} %get-tuple-element.27.y_ref, bf16[768,320]{1,0:T(8,128)(2,1)S(1)} %get-tuple-element.18.g_ref, bf16[640,128]{1,0:T(8,128)(2,1)S(1)} %collective-permute-done.one_ref, ...), custom_call_target="tpu_custom_call" | custom-call | flops 1887436800 | bytes 4000000 | tf_op jit(solution)/shard_map/pallas_call | solution.py:330
  51.8 6.0 %all-to-all-done.1.refs_0_ = bf16[16,80,128]{2,1,0:T(8,128)(2,1)S(1)} async-done(((bf16[16,80,128]{2,1,0:T(8,128)(2,1)}), bf16[16,80,128]{2,1,0:T(8,128)(2,1)S(1)}, u32[]{:S(2)}, u32[]{:S(2)}) %all-to-all-start.1) | async-done | bytes 327712 | tf_op jit(solution)/shard_map/all_to_all | solution.py:509
  57.8 0.1 shard_map.92
  57.8 11.7 %all_to_all.16 = bf16[16,80,128]{2,1,0:T(8,128)(2,1)S(1)} all-to-all(bf16[16,80,128]{2,1,0:T(8,128)(2,1)S(1)} %shard_map.92), channel_id=1, replica_groups={{0,4,64,68,1,5,65,69,3,7,67,71,2,6,66,70},{12,8,76,72,13,9,77,73,15,11,..., dimensions={0} | all-to-all | bytes 655360 | tf_op jit(solution)/shard_map/all_to_all | solution.py:509
  69.5 5.1 %all_gather.11.refs_0_ = bf16[2,1280,128]{2,1,0:T(8,128)(2,1)S(1)} all-gather(bf16[1,1280,128]{2,1,0:T(8,128)(2,1)S(1)} %bitcast.14), channel_id=1, replica_groups=mesh['z'=8,'c'=2,'tm'=32] {'c'}, dimensions={0}, use_global_device_ids=true | all-gather | bytes 983040 | tf_op jit(solution)/shard_map/all_gather | solution.py:470
  74.6 1.1 %shard_map.93 = f32[320,960]{1,0:T(8,128)} custom-call(bf16[2,1280,128]{2,1,0:T(8,128)(2,1)S(1)} %all_gather.11.refs_0_), custom_call_target="tpu_custom_call" | custom-call | flops 1000000 | bytes 2000000 | tf_op jit(solution)/shard_map/pallas_call | solution.py:330
Async XLA Ops:
  1.9 12.6 %collective-permute-start = (bf16[640,128]{1,0:T(8,128)(2,1)S(1)}, bf16[640,128]{1,0:T(8,128)(2,1)S(1)}, u32[]{:S(2)}, u32[]{:S(2)}) collective-permute-start(bf16[640,128]{1,0:T(8,128)(2,1)S(1)} %get-tuple-element.22), channel_id=1, source_target_pairs={{0,1},{1,0},{2,3},{3,2},{4,5},{5,4},{6,7},{7,6},{8,9},{9,8},{10,11... | collective-permute-start | bytes 491528 | tf_op jit(solution)/shard_map/ppermute | solution.py:452
  2.6 11.9 %collective-permute-start.1 = (bf16[640,128]{1,0:T(8,128)(2,1)S(1)}, bf16[640,128]{1,0:T(8,128)(2,1)S(1)}, u32[]{:S(2)}, u32[]{:S(2)}) collective-permute-start(bf16[640,128]{1,0:T(8,128)(2,1)S(1)} %get-tuple-element.23), channel_id=1, source_target_pairs={{1,2},{2,1},{3,4},{4,3},{5,6},{6,5},{7,8},{8,7},{9,10},{10,9},{11,... | collective-permute-start | bytes 491528 | tf_op jit(solution)/shard_map/ppermute | solution.py:453
  33.0 24.8 %all-to-all-start.1 = ((bf16[16,80,128]{2,1,0:T(8,128)(2,1)}), bf16[16,80,128]{2,1,0:T(8,128)(2,1)S(1)}, u32[]{:S(2)}, u32[]{:S(2)}) async-start(bf16[16,80,128]{2,1,0:T(8,128)(2,1)} %shard_map.90), calls=%async_computation.1 | async-start | bytes 655360 | tf_op jit(solution)/shard_map/all_to_all | solution.py:509

commit v8 on v7

--- a/solution.py
+++ b/solution.py
@@ -490,7 +490,7 @@
         return [p for p in range(size) if kind(p) == i]
 
     near = [
-        [at(zz, c, yy, x ^ (x >> 1)) for x in range(xs) for zz in pair(z) for yy in pair(y)]
+        [at(pair(z)[k // 2], c, pair(y)[(k ^ (k >> 1)) % 2], x ^ (x >> 1)) for x in range(xs) for k in range(4)]
         for z in range(0, zs, 2)
         for c in range(2)
         for y in range(0, ys, 2)

time: 76.1 us -> 77.8 us (1.022)
  waiting for transfers between devices: 5.99 us -> 7.51 us
    all_to_all x1, waiting for transfers between devices: 5.99 us -> 7.5 us  [exchange(): lax.all_to_all(parts, ('z', 'c', 'tm'), 0, 0, axis_index_groups=members,...]
  transfers between devices with their start and end apart: 3 -> 3, of which waited for: 1 -> 1; matrix products, arithmetic and copies ran while one was open for 0% -> 0% of each run, Pallas kernels for 16% -> 15%
where the time goes in v8:
time: 77.8 us; the launch traced here: 77.5 us
  blocking collectives  34.1 us (44%)
  starting transfers between devices  19.4 us (25%)
  Pallas kernels  15.7 us (20%)
  waiting for transfers between devices  7.51 us (10%)
    all_to_all x2, blocking collectives, exchange(): lax.all_to_all(parts, ('z', 'c', 'tm'), 0, 0, axis_index_groups=members,...  24.7 us
    pallas_call x8, Pallas kernels, call(): pl.pallas_call(body, out_shape=outs, in_specs=[SMEM_SPEC] * len(scalars)...  15.7 us
    all_to_all x1, starting transfers between devices, exchange(): lax.all_to_all(parts, ('z', 'c', 'tm'), 0, 0, axis_index_groups=members,...  12.3 us
    all_to_all x1, waiting for transfers between devices, exchange(): lax.all_to_all(parts, ('z', 'c', 'tm'), 0, 0, axis_index_groups=members,...  7.5 us
    ppermute x1, starting transfers between devices, shards(): two = lax.ppermute(two, ('c', 'tm'), pairs[1])  6.4 us
    all_gather x1, blocking collectives, shards(): both = lax.all_gather(mine, 'c')  5.08 us
    all_gather x1, blocking collectives, shards(): lax.all_gather(send, 'c')  4.29 us
  transfers between devices with their start and end apart: 3, of which 1 were waited for; matrix products, arithmetic and copies ran while one was open for 0% of the time, Pallas kernels for 15%

profile of v8, /device:TPU:1, one launch (start us, length us, event | category | flops | bytes accessed | tf_op | source)
XLA Modules:
  0.0 77.5 jit_solution(16818893569330757607)
XLA Ops:
  0.6 1.3 %shard_map.86 = (bf16[640,128]{1,0:T(8,128)(2,1)S(1)}, bf16[640,128]{1,0:T(8,128)(2,1)S(1)}, bf16[768,320]{1,0:T(8,128)(2,1)S(1)}) custom-call(s32[1]{0:T(128)} %bitcast.1.t_ref, s32[1]{0:T(128)} %bitcast.core_ref, s32[1,32]{1,0:T(1,128)} %counts_hbm.5, bf16[768,320]{1,0:T(8,128)(2,1)} %bitcast.15), custom_call_target="tpu_custom_call" | custom-call | bytes 600000 | tf_op jit(solution)/shard_map/pallas_call | solution.py:330
  1.9 0.7 collective-permute-start
  2.6 6.4 %collective-permute-start.1 = (bf16[640,128]{1,0:T(8,128)(2,1)S(1)}, bf16[640,128]{1,0:T(8,128)(2,1)S(1)}, u32[]{:S(2)}, u32[]{:S(2)}) collective-permute-start(bf16[640,128]{1,0:T(8,128)(2,1)S(1)} %get-tuple-element.23), channel_id=1, source_target_pairs={{1,2},{2,1},{3,4},{4,3},{5,6},{6,5},{7,8},{8,7},{9,10},{10,9},{11,... | collective-permute-start | bytes 491528 | tf_op jit(solution)/shard_map/ppermute | solution.py:453
  9.0 5.5 %shard_map.87 = (bf16[768,320]{1,0:T(8,128)(2,1)S(1)}, bf16[768,320]{1,0:T(8,128)(2,1)S(1)}, f32[320,1024]{1,0:T(8,128)S(1)}, bf16[256,320]{1,0:T(8,128)(2,1)S(1...) custom-call(s32[1]{0:T(128)} %bitcast.1.t_ref, ...), custom_call_target="tpu_custom_call" | custom-call | flops 1887436800 | bytes 4000000 | tf_op jit(solution)/shard_map/pallas_call | solution.py:330
  14.5 0.0 collective-permute-done.one_ref
  14.5 0.0 collective-permute-done.1.two_ref
  14.5 0.5 shard_map.88
  15.0 4.3 %all-gather = bf16[2560,128]{1,0:T(8,128)(2,1)S(1)} all-gather(bf16[1280,128]{1,0:T(8,128)(2,1)S(1)} %get-tuple-element.25), channel_id=2, replica_groups=mesh['z'=8,'c'=2,'tm'=32] {'c'}, dimensions={0}, use_global_device_ids=true | all-gather | bytes 983040 | tf_op jit(solution)/shard_map/all_gather | solution.py:461
  19.3 0.1 shard_map.89
  19.4 14.5 %all_to_all.15.refs_0_ = bf16[16,80,128]{2,1,0:T(8,128)(2,1)S(1)} all-to-all(bf16[16,80,128]{2,1,0:T(8,128)(2,1)S(1)} %bitcast.12), channel_id=1, replica_groups={{0,4,68,64,1,5,69,65,3,7,71,67,2,6,70,66},{12,8,72,76,13,9,73,77,15,11,..., dimensions={0} | all-to-all | bytes 655360 | tf_op jit(solution)/shard_map/all_to_all | solution.py:509
  33.9 0.8 %shard_map.90 = bf16[16,80,128]{2,1,0:T(8,128)(2,1)} custom-call(bf16[16,80,128]{2,1,0:T(8,128)(2,1)S(1)} %all_to_all.15.refs_0_), custom_call_target="tpu_custom_call" | custom-call | flops 163840 | bytes 327680 | tf_op jit(solution)/shard_map/pallas_call | solution.py:330
  34.6 12.3 %all-to-all-start.1 = ((bf16[16,80,128]{2,1,0:T(8,128)(2,1)}), bf16[16,80,128]{2,1,0:T(8,128)(2,1)S(1)}, u32[]{:S(2)}, u32[]{:S(2)}) async-start(bf16[16,80,128]{2,1,0:T(8,128)(2,1)} %shard_map.90), calls=%async_computation.1 | async-start | bytes 655360 | tf_op jit(solution)/shard_map/all_to_all | solution.py:509
  47.0 6.4 %shard_map.91 = bf16[768,320]{1,0:T(8,128)(2,1)} custom-call(s32[1]{0:T(128)} %bitcast.1.t_ref, s32[1]{0:T(128)} %bitcast.core_ref, bf16[768,320]{1,0:T(8,128)(2,1)S(1)} %get-tuple-element.27.y_ref, bf16[768,320]{1,0:T(8,128)(2,1)S(1)} %get-tuple-element.18.g_ref, bf16[640,128]{1,0:T(8,128)(2,1)S(1)} %collective-permute-done.one_ref, ...), custom_call_target="tpu_custom_call" | custom-call | flops 1887436800 | bytes 4000000 | tf_op jit(solution)/shard_map/pallas_call | solution.py:330
  53.4 7.5 %all-to-all-done.1.refs_0_ = bf16[16,80,128]{2,1,0:T(8,128)(2,1)S(1)} async-done(((bf16[16,80,128]{2,1,0:T(8,128)(2,1)}), bf16[16,80,128]{2,1,0:T(8,128)(2,1)S(1)}, u32[]{:S(2)}, u32[]{:S(2)}) %all-to-all-start.1) | async-done | bytes 327712 | tf_op jit(solution)/shard_map/all_to_all | solution.py:509
  60.9 0.1 shard_map.92
  61.0 10.3 %all_to_all.16 = bf16[16,80,128]{2,1,0:T(8,128)(2,1)S(1)} all-to-all(bf16[16,80,128]{2,1,0:T(8,128)(2,1)S(1)} %shard_map.92), channel_id=1, replica_groups={{0,4,68,64,1,5,69,65,3,7,71,67,2,6,70,66},{12,8,72,76,13,9,73,77,15,11,..., dimensions={0} | all-to-all | bytes 655360 | tf_op jit(solution)/shard_map/all_to_all | solution.py:509
  71.3 5.1 %all_gather.11.refs_0_ = bf16[2,1280,128]{2,1,0:T(8,128)(2,1)S(1)} all-gather(bf16[1,1280,128]{2,1,0:T(8,128)(2,1)S(1)} %bitcast.14), channel_id=1, replica_groups=mesh['z'=8,'c'=2,'tm'=32] {'c'}, dimensions={0}, use_global_device_ids=true | all-gather | bytes 983040 | tf_op jit(solution)/shard_map/all_gather | solution.py:470
  76.3 1.1 %shard_map.93 = f32[320,960]{1,0:T(8,128)} custom-call(bf16[2,1280,128]{2,1,0:T(8,128)(2,1)S(1)} %all_gather.11.refs_0_), custom_call_target="tpu_custom_call" | custom-call | flops 1000000 | bytes 2000000 | tf_op jit(solution)/shard_map/pallas_call | solution.py:330
Async XLA Ops:
  1.9 12.6 %collective-permute-start = (bf16[640,128]{1,0:T(8,128)(2,1)S(1)}, bf16[640,128]{1,0:T(8,128)(2,1)S(1)}, u32[]{:S(2)}, u32[]{:S(2)}) collective-permute-start(bf16[640,128]{1,0:T(8,128)(2,1)S(1)} %get-tuple-element.22), channel_id=1, source_target_pairs={{0,1},{1,0},{2,3},{3,2},{4,5},{5,4},{6,7},{7,6},{8,9},{9,8},{10,11... | collective-permute-start | bytes 491528 | tf_op jit(solution)/shard_map/ppermute | solution.py:452
  2.6 11.9 %collective-permute-start.1 = (bf16[640,128]{1,0:T(8,128)(2,1)S(1)}, bf16[640,128]{1,0:T(8,128)(2,1)S(1)}, u32[]{:S(2)}, u32[]{:S(2)}) collective-permute-start(bf16[640,128]{1,0:T(8,128)(2,1)S(1)} %get-tuple-element.23), channel_id=1, source_target_pairs={{1,2},{2,1},{3,4},{4,3},{5,6},{6,5},{7,8},{8,7},{9,10},{10,9},{11,... | collective-permute-start | bytes 491528 | tf_op jit(solution)/shard_map/ppermute | solution.py:453
  34.6 26.3 %all-to-all-start.1 = ((bf16[16,80,128]{2,1,0:T(8,128)(2,1)}), bf16[16,80,128]{2,1,0:T(8,128)(2,1)S(1)}, u32[]{:S(2)}, u32[]{:S(2)}) async-start(bf16[16,80,128]{2,1,0:T(8,128)(2,1)} %shard_map.90), calls=%async_computation.1 | async-start | bytes 655360 | tf_op jit(solution)/shard_map/all_to_all | solution.py:509
